TPU v7x, 32 devices: a whole 2x2x4 slice. The times are simulated.
32 devices in a mesh: groups: 2 (over x), dp: 2 (over core), expert: 8 (over z, y).
Axes of the slice: x: 2, y: 2, z: 4, core: 2. Of those that a mesh axis runs over, the one named last changes fastest.
Arguments:
- tokens: bfloat16 [4096, 3584], P(('groups', 'dp', 'expert')), parts along dimension 0, may hold values from -6 to 6
- scores: float32 [4096, 8], P(('groups', 'dp', 'expert')), parts along dimension 0, may hold values from -8 to 8
- expert_ids: int32 [4096, 2], P(('groups', 'dp', 'expert')), parts along dimension 0, may hold values from 0 to 7, all different within a row; in each aligned block of 128 rows (0 to 127, 128 to 255, ...) at most 80 rows name the same one
- w_gate: bfloat16 [8, 3584, 1024], P('expert', None, 'dp'), may hold values from -0.09375 to 0.09375
- w_up: bfloat16 [8, 3584, 1024], P('expert', None, 'dp'), may hold values from -0.09375 to 0.09375
- w_down: bfloat16 [8, 1024, 3584], P('expert', 'dp'), may hold values from -0.1875 to 0.1875
Outputs:
- mixed: bfloat16 [4096, 3584], P(('groups', 'dp', 'expert')), parts along dimension 0
There are 2 independent parts, one for each index of `groups`. A program takes and returns all parts, laid end to end along the dimension named above; an argument that names none is the same for every part. Nothing has to cross between parts.
Inputs may be any that keep to these rules, and one draw needn't show every extreme that they name: `expert_ids`: the 2048 rows fall into aligned blocks of 128 rows, the rows of one device. Each row names 2 different experts. In no block is an expert named by more than 80 rows, and in every draw some block names some expert exactly 80 times.
All inputs are finite; a program needn't handle non-finite values.
Results may differ from a plain program's by a relative error of at most 0.0059.
Values may be sent and summed in bfloat16 or wider, within the bound.
No kernel may reach another device: no remote copies, remote signals or barrier semaphores. Data moves between devices by JAX's collectives and lax.ppermute only.
A program may use at most 128 MiB of HBM per device.

v0:
```python
import jax
import jax.numpy as jnp
from jax import lax
from jax.sharding import PartitionSpec as P


def per_device(tokens, scores, expert_ids, w_gate, w_up, w_down):
    experts = lax.axis_size("expert")
    tok_rows, width = tokens.shape
    topk = expert_ids.shape[1]
    capacity = min(tok_rows, max(2, 5 * tok_rows * topk // (2 * experts)))
    flat_ids = expert_ids.reshape(-1)
    onehot = (flat_ids[:, None] == jnp.arange(experts, dtype=jnp.int32)[None, :]).astype(jnp.int32)
    position = jnp.sum((jnp.cumsum(onehot, axis=0) - 1) * onehot, axis=1)
    slot = flat_ids * capacity + position
    repeated = jnp.repeat(tokens, topk, axis=0)
    outgoing = jnp.zeros((experts * capacity, width), tokens.dtype).at[slot].set(repeated)
    outgoing = outgoing.reshape(experts, capacity, width)
    doubled = jnp.tile(outgoing, (lax.axis_size("dp"), 1, 1))
    rows = lax.all_to_all(doubled, ("dp", "expert"), split_axis=0, concat_axis=0, tiled=True)
    shape = rows.shape
    flat = rows.reshape(-1, shape[-1])
    gate = jnp.dot(flat, w_gate[0], preferred_element_type=jnp.float32)
    up_value = jnp.dot(flat, w_up[0], preferred_element_type=jnp.float32)
    hidden = (jax.nn.silu(gate) * up_value).astype(jnp.bfloat16)
    partial_out = jnp.dot(hidden, w_down[0], preferred_element_type=jnp.float32)
    partial_value = partial_out.reshape(shape)
    returned = lax.all_to_all(
        partial_value, ("dp", "expert"), split_axis=0, concat_axis=0, tiled=True
    )
    back = jnp.sum(returned.reshape(-1, experts, capacity, width), axis=0).astype(jnp.bfloat16)
    picked = back.reshape(experts * capacity, width)[slot].reshape(tok_rows, topk, width)
    chosen = jax.nn.sigmoid(jnp.take_along_axis(scores, expert_ids, axis=1))
    weight = chosen / jnp.sum(chosen, axis=1, keepdims=True)
    mixed = 2.5 * jnp.sum(weight[:, :, None] * picked.astype(jnp.float32), axis=1)
    return mixed.astype(jnp.bfloat16)


def solution(mesh):
    in_specs = (
        P(("groups", "dp", "expert"), None),
        P(("groups", "dp", "expert"), None),
        P(("groups", "dp", "expert"), None),
        P("expert", None, "dp"),
        P("expert", None, "dp"),
        P("expert", "dp", None),
    )
    out_specs = P(("groups", "dp", "expert"), None)
    return jax.shard_map(
        per_device, mesh=mesh, in_specs=in_specs, out_specs=out_specs, check_vma=False
    )
```

profile of v0, /device:TPU:10, one launch (start us, length us, event | category | flops | bytes accessed | tf_op | source)
XLA Modules:
  0.0 678.7 jit_solution(6272114889885988516)
XLA Ops:
  0.0 0.0 copy-start
  0.0 0.8 copy.20
  0.8 0.1 eq.29
  0.9 0.1 eq.25
  1.1 0.7 broadcast_multiply_fusion
  1.8 0.6 reduce-window.6
  2.3 0.2 slice_reduce_fusion
  2.6 0.1 copy.19
  2.7 0.1 mul.43
  2.9 2.1 broadcast_in_dim.17
  5.0 1.7 reshape.117
  6.7 0.1 fusion.14
  6.8 7.0 %scatter_custom_fusion = bf16[640,3584]{1,0:T(8,128)(2,1)} fusion(s32[256]{0:T(256)S(1)} %bitcast.40, bf16[256,3584]{1,0:T(8,128)(2,1)} %reshape.117, bf16[]{:T(256)} %constant.34.clone.1), kind=kCustom, calls=%fused_computation.12 | custom fusion | bytes 4588032 | tf_op jit(solution)/shard_map/scatter | solution.py:17
  13.8 6.7 tile.11
  20.5 0.0 copy-start.2
  20.5 206.7 %all_to_all.10 = bf16[16,80,3584]{2,1,0:T(8,128)(2,1)S(1)} all-to-all(bf16[16,80,3584]{2,1,0:T(8,128)(2,1)} %bitcast.36), channel_id=1, replica_groups=mesh['groups'=2,'dp'=2,'expert'=8] {'dp','expert'}, dimensions={0} | all-to-all | bytes 18350080 | tf_op jit(solution)/shard_map/all_to_all | solution.py:20
  227.2 0.0 copy-done.2
  227.2 0.0 copy-start.3
  227.2 4.9 fusion.4
  232.1 0.0 copy-done.3
  232.1 0.0 copy-start.4
  232.2 5.4 fusion.9
  237.6 0.0 copy-done.4
  237.6 8.9 %fusion = f32[16,80,3584]{2,1,0:T(8,128)} fusion(bf16[16,80,512]{2,1,0:T(8,128)(2,1)S(1)} %bitcast.43, bf16[1,512,3584]{2,1,0:T(8,128)(2,1)S(1)} %copy-done.4), kind=kOutput, calls=%fused_computation.3 | convolution fusion | flops 4697620480 | bytes 23330816 | tf_op jit(solution)/shard_map/dot_general | solution.py:26
  246.5 0.0 copy-start.1
  246.5 6.4 all-to-all-start.1
  252.9 0.0 copy-done.1
  252.9 0.1 copy.16
  253.0 0.1 reshape.107
  253.2 0.0 copy-done
  253.2 1.4 gather_fusion.1
  254.6 0.1 reshape.110
  254.7 0.1 copy.17
  254.8 0.1 copy.18
  255.0 395.0 %all-to-all-done.1 = f32[16,80,3584]{2,1,0:T(8,128)} async-done(((f32[16,80,3584]{2,1,0:T(8,128)}), f32[16,80,3584]{2,1,0:T(8,128)}, u32[]{:S(2)}, u32[]{:S(2)}) %all-to-all-start.1) | async-done | bytes 18350112 | tf_op jit(solution)/shard_map/all_to_all | solution.py:28
  649.9 10.4 %reduce_sum.41 = bf16[8,80,3584]{2,1,0:T(8,128)(2,1)} reduce(f32[2,8,80,3584]{3,2,1,0:T(8,128)} %bitcast.13, f32[]{:T(128)} %constant.18.clone.1), dimensions={0}, to_apply=%region_5.6 | reduce | flops 2293760 | bytes 22937604 | tf_op jit(solution)/shard_map/reduce_sum | solution.py:31
  660.4 6.4 gather_fusion
  666.8 3.5 reshape.98
  670.3 7.4 %multiply_reduce_fusion = f32[128,3584]{1,0:T(8,128)S(1)} fusion(f32[128,2,3584]{2,1,0:T(2,128)} %reshape.98, f32[128,2]{1,0:T(8,128)S(1)} %copy.18), kind=kLoop, calls=%fused_computation.9 | loop fusion | flops 1376256 | bytes 5506048 | tf_op jit(solution)/shard_map/reduce_sum | solution.py:35
  677.7 1.0 multiply_convert_fusion
  (8 shorter events, 0.1 us)
Async XLA Ops:
  0.0 253.2 %copy-start = (f32[128,8]{0,1:T(8,128)S(1)}, f32[128,8]{0,1:T(8,128)}, u32[]{:S(2)}) copy-start(f32[128,8]{0,1:T(8,128)} %param.7) | copy-start | bytes 12292
  20.5 206.7 %copy-start.2 = (bf16[1,3584,512]{2,1,0:T(8,128)(2,1)S(1)}, bf16[1,3584,512]{2,1,0:T(8,128)(2,1)}, u32[]{:S(2)}) copy-start(bf16[1,3584,512]{2,1,0:T(8,128)(2,1)} %param.9) | copy-start | bytes 11010052
  227.2 4.9 copy-start.3
  232.1 5.4 copy-start.4
  246.5 6.4 copy-start.1
  246.5 403.4 %all-to-all-start.1 = ((f32[16,80,3584]{2,1,0:T(8,128)}), f32[16,80,3584]{2,1,0:T(8,128)}, u32[]{:S(2)}, u32[]{:S(2)}) async-start(f32[16,80,3584]{2,1,0:T(8,128)} %fusion), calls=%async_computation.1 | async-start | bytes 36700160 | tf_op jit(solution)/shard_map/all_to_all | solution.py:28
where the time goes:
time: 679 us
  waiting for transfers between devices  395 us (58%)
  blocking collectives  207 us (30%)
  local copies, waits for them, and re-layouts  30.9 us (5%)
  other arithmetic  20.3 us (3%)
  matrix products  19.3 us (3%)
    all_to_all x1, waiting for transfers between devices, per_device(): lax.all_to_all(partial_value, ('dp', 'expert'), split_axis=0, concat_axis...  395 us
    all_to_all x1, blocking collectives, per_device(): lax.all_to_all(doubled, ('dp', 'expert'), split_axis=0, concat_axis=0, ti...  207 us
  transfers between devices with their start and end apart: 1, of which 1 were waited for; matrix products, arithmetic and copies ran while one was open for 0% of the time, Pallas kernels for 0%

commit v1 on v0

v1 whole, which is shorter than its diff:
```python
import functools

import jax
import jax.numpy as jnp
from jax import lax
from jax.experimental import pallas as pl
from jax.experimental.pallas import tpu as pltpu
from jax.sharding import PartitionSpec as P

LANES = 128
ALIGN = 16
CHUNKS = 1
VMEM_LIMIT = 56 * 1024 * 1024
SCALE = 2.5


def up_to(value, step):
    return -(-value // step) * step


def dot32(a, b):
    return jnp.dot(a, b, preferred_element_type=jnp.float32)


def iota(shape, dim):
    return lax.broadcasted_iota(jnp.int32, shape, dim)


def flag(mask):
    return jnp.where(mask, 1.0, 0.0)


def pack_kernel(chunks, experts, ids_ref, scores_ref, tok_ref, out_ref):
    rows, width = tok_ref.shape
    topk = ids_ref.shape[1]
    ids = ids_ref[...]
    sig = 1.0 / (1.0 + jnp.exp(-scores_ref[...]))
    lane_e = iota((rows, experts), 1)
    chosen = [
        jnp.sum(jnp.where(ids[:, k : k + 1] == lane_e, sig, 0.0), axis=1, keepdims=True)
        for k in range(topk)
    ]
    total = sum(chosen[1:], chosen[0])
    lane = iota((rows, LANES), 1)
    expert_of_lane = lax.rem(lane, experts)
    weight = jnp.zeros((rows, LANES), jnp.float32)
    for k in range(topk):
        weight = weight + jnp.where(ids[:, k : k + 1] == expert_of_lane, chosen[k] / total, 0.0)
    high = weight.astype(jnp.bfloat16).astype(jnp.float32)
    rest = weight - high
    middle = rest.astype(jnp.bfloat16).astype(jnp.float32)
    low = rest - middle
    pieces = jnp.where(
        lane < experts,
        high,
        jnp.where(lane < 2 * experts, middle, jnp.where(lane < 3 * experts, low, 0.0)),
    ).astype(jnp.bfloat16)
    if chunks == 1:
        out_ref[0, :, :width] = tok_ref[...]
        out_ref[0, :, width:] = pieces
        return
    first = jnp.min(ids.astype(jnp.float32), axis=1, keepdims=True)
    last = jnp.max(ids.astype(jnp.float32), axis=1, keepdims=True)
    key = jnp.broadcast_to(first * experts + last, (rows, rows))
    key_t = key.T
    i, j = iota((rows, rows), 0), iota((rows, rows), 1)
    ahead = (key < key_t) | ((key == key_t) & (i < j))
    rank = jnp.sum(flag(ahead), axis=0, keepdims=True)
    per = rows // chunks
    for c in range(chunks):
        place = iota((per, rows), 0) * chunks + c
        take = flag(rank.astype(jnp.int32) == place).astype(jnp.bfloat16)
        out_ref[c, :, :width] = dot32(take, tok_ref[...]).astype(jnp.bfloat16)
        out_ref[c, :, width:] = dot32(take, pieces).astype(jnp.bfloat16)


def pack(ids, scores, tokens, chunks):
    rows, width = tokens.shape
    experts = scores.shape[1]
    return pl.pallas_call(
        functools.partial(pack_kernel, chunks, experts),
        out_shape=jax.ShapeDtypeStruct((chunks, rows // chunks, width + LANES), jnp.bfloat16),
        compiler_params=pltpu.CompilerParams(vmem_limit_bytes=VMEM_LIMIT),
        cost_estimate=pl.CostEstimate(
            flops=2 * rows * rows * width, bytes_accessed=4 * rows * width, transcendentals=0
        ),
        name="pack",
    )(ids, scores, tokens)


def weight_of(meta, expert, experts):
    lane = iota(meta.shape, 1)
    hit = (lax.rem(lane, experts) == expert) & (lane < 3 * experts)
    return jnp.sum(jnp.where(hit, meta, 0.0), axis=1, keepdims=True)


def named(meta, expert):
    return jnp.sum(jnp.where(iota(meta.shape, 1) == expert, meta, 0.0), axis=1, keepdims=True) > 0.0


def pick(meta, expert, cap):
    rows = meta.shape[0]
    mine = flag(named(meta, expert))
    i, j = iota((rows, rows), 0), iota((rows, rows), 1)
    position = jnp.sum(jnp.where(i < j, mine, 0.0), axis=0, keepdims=True)
    present = jnp.sum(jnp.where(i == j, mine, 0.0), axis=0, keepdims=True)
    place = iota((cap, rows), 0)
    return flag((position.astype(jnp.int32) == place) & (present > 0.0)).astype(jnp.bfloat16)


def spread(meta, expert, cap):
    rows = meta.shape[0]
    mine = flag(named(meta, expert))
    i, j = iota((rows, rows), 0), iota((rows, rows), 1)
    row_mine = jnp.sum(jnp.where(i == j, mine, 0.0), axis=0, keepdims=True)
    position = jnp.sum(jnp.where(j < i, row_mine, 0.0), axis=1, keepdims=True)
    place = iota((rows, cap), 1)
    return flag((position.astype(jnp.int32) == place) & (mine > 0.0)).astype(jnp.bfloat16)


def pick_kernel(sel_ref, x_ref, y_ref):
    cap, width = y_ref.shape
    take = pick(x_ref[:, width:].astype(jnp.float32), sel_ref[1], cap)
    y_ref[...] = dot32(take, x_ref[:, :width]).astype(jnp.bfloat16)


def merge_pick_kernel(sel_ref, end_ref, inner_ref, x_ref, y_ref):
    cap, width = y_ref.shape

    @pl.when(sel_ref[2] == 1)
    def _():
        x_ref[...] = end_ref[...]

    @pl.when(sel_ref[2] == 0)
    def _():
        x_ref[...] = inner_ref[...]

    take = pick(x_ref[:, width:].astype(jnp.float32), sel_ref[1], cap)
    y_ref[...] = dot32(take, x_ref[:, :width]).astype(jnp.bfloat16)


def pick_rows(sel, parts, cap):
    rows, wide = parts[0].shape
    width = wide - LANES
    outs = [jax.ShapeDtypeStruct((cap, width), jnp.bfloat16)]
    if len(parts) == 2:
        outs = [jax.ShapeDtypeStruct((rows, wide), jnp.bfloat16)] + outs
    got = pl.pallas_call(
        merge_pick_kernel if len(parts) == 2 else pick_kernel,
        in_specs=[pl.BlockSpec(memory_space=pltpu.SMEM)]
        + [pl.BlockSpec(memory_space=pltpu.VMEM)] * len(parts),
        out_specs=[pl.BlockSpec(memory_space=pltpu.VMEM)] * len(outs),
        out_shape=outs,
        compiler_params=pltpu.CompilerParams(vmem_limit_bytes=VMEM_LIMIT),
        cost_estimate=pl.CostEstimate(
            flops=2 * rows * cap * width, bytes_accessed=4 * rows * width, transcendentals=0
        ),
        name="pick",
    )(sel, *parts)
    return (parts[0], got[0]) if len(parts) == 1 else tuple(got)


def expert_kernel(sizes, steps_h, steps_d, *refs):
    count = len(sizes)
    x_refs, refs = refs[:count], refs[count:]
    gates, ups, downs, refs = refs[0:2], refs[2:4], refs[4:6], refs[6:]
    out_refs, (xs, hidden) = refs[:count], refs[count:]
    step = pl.program_id(0)
    width = xs.shape[1]
    block = gates[0].shape[1]
    half = steps_h // 2

    @pl.when(step == 0)
    def _():
        at = 0
        for ref, size in zip(x_refs, sizes):
            xs[at : at + size, :] = ref[:, :width]
            at += size

    for s in range(steps_h):

        @pl.when(step == s)
        def _(s=s):
            which = s // half
            rows = xs[...]
            gate = dot32(rows, gates[which][...])
            up = dot32(rows, ups[which][...])
            value = gate / (1.0 + jnp.exp(-gate)) * up
            hidden[:, s * block : (s + 1) * block] = value.astype(jnp.bfloat16)

    @pl.when(step >= steps_h)
    def _():
        depth = downs[0].shape[0]
        out = dot32(hidden[:, :depth], downs[0][...]) + dot32(hidden[:, depth:], downs[1][...])
        out = out.astype(jnp.bfloat16)
        at = 0
        for ref, size in zip(out_refs, sizes):
            ref[...] = out[at : at + size, :]
            at += size


def expert(blocks, gates, ups, downs):
    sizes = [b.shape[0] for b in blocks]
    total = sum(sizes)
    width, depth = gates[0].shape
    block_h = 256 if depth % 256 == 0 else depth
    block_d = 512 if width % 512 == 0 else width
    half = depth // block_h
    steps_h, steps_d = 2 * half, width // block_d

    def up_map(which):
        return lambda i: (0, jnp.clip(i - which * half, 0, half - 1))

    def down_map(i):
        return (0, jnp.maximum(i - steps_h, 0))

    return pl.pallas_call(
        functools.partial(expert_kernel, sizes, steps_h, steps_d),
        grid=(steps_h + steps_d,),
        in_specs=[pl.BlockSpec(b.shape, lambda i: (0, 0), pipeline_mode=pl.Buffered(1)) for b in blocks]
        + [pl.BlockSpec((width, block_h), up_map(0)), pl.BlockSpec((width, block_h), up_map(1))] * 2
        + [pl.BlockSpec((depth, block_d), down_map)] * 2,
        out_specs=[pl.BlockSpec((s, block_d), down_map) for s in sizes],
        out_shape=[jax.ShapeDtypeStruct((s, width), jnp.bfloat16) for s in sizes],
        scratch_shapes=[
            pltpu.VMEM((total, width), jnp.bfloat16),
            pltpu.VMEM((total, 2 * depth), jnp.bfloat16),
        ],
        compiler_params=pltpu.CompilerParams(vmem_limit_bytes=VMEM_LIMIT),
        cost_estimate=pl.CostEstimate(
            flops=12 * total * width * depth,
            bytes_accessed=12 * width * depth + 4 * total * width,
            transcendentals=2 * total * depth,
        ),
        name="expert",
    )(*blocks, *gates, *ups, *downs)


def combine_kernel(experts, scale, sel_ref, meta_ref, own_ref, other_ref, *refs):
    out_ref = refs[-1]
    cap = other_ref.shape[0]
    meta = meta_ref[...].astype(jnp.float32)
    back = dot32(spread(meta, sel_ref[1], cap), other_ref[...])
    value = weight_of(meta, sel_ref[0], experts) * own_ref[...].astype(jnp.float32)
    value = value + weight_of(meta, sel_ref[1], experts) * back
    for ref in refs[:-1]:
        value = value + ref[...].astype(jnp.float32)
    if scale is not None:
        value = value * scale
    out_ref[...] = value.astype(jnp.bfloat16)


def combine(sel, x, own, other, extra, experts, scale=None):
    rows, width = own.shape
    cap = other.shape[0]
    block = 896 if width % 896 == 0 else width
    col = pl.BlockSpec((rows, block), lambda i: (0, i))
    return pl.pallas_call(
        functools.partial(combine_kernel, experts, scale),
        grid=(width // block,),
        in_specs=[
            pl.BlockSpec(memory_space=pltpu.SMEM),
            pl.BlockSpec((rows, LANES), lambda i: (0, width // LANES)),
            col,
            pl.BlockSpec((cap, block), lambda i: (0, i)),
        ]
        + [col] * len(extra),
        out_specs=col,
        out_shape=jax.ShapeDtypeStruct((rows, width), jnp.bfloat16),
        compiler_params=pltpu.CompilerParams(vmem_limit_bytes=VMEM_LIMIT),
        cost_estimate=pl.CostEstimate(
            flops=2 * rows * cap * width, bytes_accessed=6 * rows * width, transcendentals=0
        ),
        name="combine",
    )(sel, x, own, other, *extra)


def capacity_of(tok_rows, topk, experts):
    return min(tok_rows, max(2, 5 * tok_rows * topk // (2 * experts)))


def on_levels(pairs):
    return [(2 * a + y, 2 * b + y) for a, b in pairs for y in range(2)]


OUTER = on_levels([(0, 1), (1, 0), (2, 3), (3, 2)])
INNER = on_levels([(1, 2), (2, 1)])
TO_ENDS = on_levels([(1, 0), (2, 3)])
FROM_ENDS = on_levels([(0, 1), (3, 2)])


def four_levels(tokens, scores, expert_ids, w_gate, w_up, w_down):
    experts = lax.axis_size("expert")
    tok_rows, width = tokens.shape
    topk = expert_ids.shape[1]
    capacity = capacity_of(tok_rows, topk, experts)
    cap = min(tok_rows // CHUNKS, up_to((capacity + (CHUNKS - 1) * (experts - 1)) // CHUNKS, ALIGN))
    me = lax.axis_index("expert")
    level = me // 2
    end = ((level == 0) | (level == 3)).astype(jnp.int32)
    sel = jnp.stack([me, me ^ 1, end]).astype(jnp.int32)
    across = [(i, i ^ 1) for i in range(experts)]

    def send(value, pairs):
        return lax.ppermute(value, "expert", pairs)

    def swap(value):
        return lax.ppermute(value, "dp", [(0, 1), (1, 0)])

    gates = (w_gate[0], swap(w_gate[0]))
    ups = (w_up[0], swap(w_up[0]))
    downs = (w_down[0], swap(w_down[0]))

    packed = pack(expert_ids, scores, tokens, CHUNKS)
    results = []
    for c in range(CHUNKS):
        own = packed[c]
        near = send(own, OUTER)
        inner = send(own, INNER)
        _, y_own = pick_rows(sel, [own], cap)
        y_own = send(y_own, across)
        far_inner = send(near, INNER)
        far_end = send(inner, TO_ENDS)
        _, y_near = pick_rows(sel, [near], cap)
        y_near = send(y_near, across)
        last_end = send(far_inner, TO_ENDS)
        far, y_far = pick_rows(sel, [far_end, far_inner], cap)
        y_far = send(y_far, across)
        last, y_last = pick_rows(sel, [last_end, inner], cap)
        y_last = send(y_last, across)

        o_own, o_near, o_far, oy_own, oy_near, oy_far = expert(
            [own, near, far, y_own, y_near, y_far], gates, ups, downs
        )
        o_last, oy_last = expert([last, y_last], gates, ups, downs)

        b_last = send(oy_last, across)
        b_far = send(oy_far, across)
        b_near = send(oy_near, across)
        b_own = send(oy_own, across)

        p_last = combine(sel, last, o_last, b_last, [], experts)
        r1 = send(p_last, FROM_ENDS)
        p_far = combine(sel, far, o_far, b_far, [r1], experts)
        r_cross = send(p_far, INNER)
        r_in = send(p_far, FROM_ENDS)
        p_near = combine(sel, near, o_near, b_near, [r_cross], experts)
        r_near = send(p_near, OUTER)
        r_mid = send((p_last.astype(jnp.float32) + r_in.astype(jnp.float32)).astype(jnp.bfloat16), INNER)
        results.append(combine(sel, own, o_own, b_own, [r_near, r_mid], experts, SCALE))
    return results, packed


def per_device(tokens, scores, expert_ids, w_gate, w_up, w_down):
    results, packed = four_levels(tokens, scores, expert_ids, w_gate, w_up, w_down)
    return results[0]


def all_to_all_form(tokens, scores, expert_ids, w_gate, w_up, w_down):
    experts = lax.axis_size("expert")
    tok_rows, width = tokens.shape
    topk = expert_ids.shape[1]
    capacity = capacity_of(tok_rows, topk, experts)
    flat_ids = expert_ids.reshape(-1)
    onehot = (flat_ids[:, None] == jnp.arange(experts, dtype=jnp.int32)[None, :]).astype(jnp.int32)
    position = jnp.sum((jnp.cumsum(onehot, axis=0) - 1) * onehot, axis=1)
    slot = flat_ids * capacity + position
    repeated = jnp.repeat(tokens, topk, axis=0)
    outgoing = jnp.zeros((experts * capacity, width), tokens.dtype).at[slot].set(repeated)
    outgoing = outgoing.reshape(experts, capacity, width)
    doubled = jnp.tile(outgoing, (lax.axis_size("dp"), 1, 1))
    rows = lax.all_to_all(doubled, ("dp", "expert"), split_axis=0, concat_axis=0, tiled=True)
    shape = rows.shape
    flat = rows.reshape(-1, shape[-1])
    gate = dot32(flat, w_gate[0])
    up_value = dot32(flat, w_up[0])
    hidden = (jax.nn.silu(gate) * up_value).astype(jnp.bfloat16)
    partial_value = dot32(hidden, w_down[0]).reshape(shape)
    returned = lax.all_to_all(
        partial_value, ("dp", "expert"), split_axis=0, concat_axis=0, tiled=True
    )
    back = jnp.sum(returned.reshape(-1, experts, capacity, width), axis=0).astype(jnp.bfloat16)
    picked = back.reshape(experts * capacity, width)[slot].reshape(tok_rows, topk, width)
    chosen = jax.nn.sigmoid(jnp.take_along_axis(scores, expert_ids, axis=1))
    weight = chosen / jnp.sum(chosen, axis=1, keepdims=True)
    mixed = SCALE * jnp.sum(weight[:, :, None] * picked.astype(jnp.float32), axis=1)
    return mixed.astype(jnp.bfloat16)


def solution(mesh):
    in_specs = (
        P(("groups", "dp", "expert"), None),
        P(("groups", "dp", "expert"), None),
        P(("groups", "dp", "expert"), None),
        P("expert", None, "dp"),
        P("expert", None, "dp"),
        P("expert", "dp", None),
    )
    out_specs = P(("groups", "dp", "expert"), None)
    short = mesh.shape["expert"] == 8 and mesh.shape["dp"] == 2
    body = per_device if short else all_to_all_form
    return jax.shard_map(
        body, mesh=mesh, in_specs=in_specs, out_specs=out_specs, check_vma=False
    )
```

time: 679 us -> 243 us (0.36)
  the two profiles are of different devices: /device:TPU:10 before, /device:TPU:0 now
where the time goes in v1:
time: 243 us; the launch traced here: 242 us
  waiting for transfers between devices  127 us (52%)
  Pallas kernels  70.3 us (29%)
  starting transfers between devices  35 us (14%)
  local copies, waits for them, and re-layouts  8.63 us (4%)
    ppermute x18, waiting for transfers between devices, send(): return lax.ppermute(value, 'expert', pairs)  127 us
    pallas_call x2, Pallas kernels, expert(): pl.pallas_call(functools.partial(expert_kernel, sizes, steps_h, steps_d),...  39.6 us
    ppermute x18, starting transfers between devices, send(): return lax.ppermute(value, 'expert', pairs)  34 us
    pallas_call x4, Pallas kernels, combine(): pl.pallas_call(functools.partial(combine_kernel, experts, scale), grid=(w...  17.9 us
    pallas_call x4, Pallas kernels, pick_rows(): pl.pallas_call(merge_pick_kernel if len(parts) == 2 else pick_kernel, in_...  10.4 us
    unnamed x40, local copies, waits for them, and re-layouts  8.63 us
  transfers between devices with their start and end apart: 21, of which 10 were waited for; matrix products, arithmetic and copies ran while one was open for 1% of the time, Pallas kernels for 25%

profile of v1, /device:TPU:0, one launch (start us, length us, event | category | flops | bytes accessed | tf_op | source)
XLA Modules:
  0.0 242.4 jit_solution(15782757376275110838)
XLA Ops:
  0.0 0.5 collective-permute-start.7
  0.5 0.1 collective-permute-start.8
  0.5 0.5 collective-permute-start.9
  1.0 1.4 copy.7.ids_ref
  2.4 1.4 copy.8.scores_ref
  3.8 2.4 pack.1
  6.2 2.6 %collective-permute-start = (bf16[128,3712]{1,0:T(8,128)(2,1)}, bf16[128,3712]{1,0:T(8,128)(2,1)S(1)}, u32[]{:S(2)}, u32[]{:S(2)}) collective-permute-start(bf16[128,3712]{1,0:T(8,128)(2,1)} %bitcast.7), channel_id=1, source_target_pairs={{0,2},{1,3},{2,0},{3,1},{4,6},{5,7},{6,4},{7,5},{8,10},{9,11},{10,... | collective-permute-start | bytes 2850824 | tf_op jit(solution)/shard_map/ppermute | solution.py:305
  8.8 21.9 %collective-permute-done.x_ref.refs_1_.meta_ref = bf16[128,3712]{1,0:T(8,128)(2,1)S(1)} collective-permute-done((bf16[128,3712]{1,0:T(8,128)(2,1)}, bf16[128,3712]{1,0:T(8,128)(2,1)S(1)}, u32[]{:S(2)}, u32[]{:S(2)}) %collective-permute-start) | collective-permute-done | bytes 950304 | tf_op jit(solution)/shard_map/ppermute | solution.py:305
  30.7 0.7 collective-permute-start.3
  31.4 0.7 collective-permute-start.1
  32.1 0.0 collective-permute-done.3.inner_ref
  32.2 1.3 collective-permute-start.13
  33.5 0.6 pad_add_fusion.sel_ref
  34.1 0.0 collective-permute-done.1.inner_ref
  34.1 44.3 %collective-permute-done.13.end_ref = bf16[128,3712]{1,0:T(8,128)(2,1)} collective-permute-done((bf16[128,3712]{1,0:T(8,128)(2,1)S(1)}, bf16[128,3712]{1,0:T(8,128)(2,1)}, u32[]{:S(2)}, u32[]{:S(2)}) %collective-permute-start.13) | collective-permute-done | bytes 950304 | tf_op jit(solution)/shard_map/ppermute | solution.py:305
  78.4 2.8 %pick.7 = (bf16[128,3712]{1,0:T(8,128)(2,1)}, bf16[80,3584]{1,0:T(8,128)(2,1)}) custom-call(s32[3]{0:T(128)} %pad_add_fusion.sel_ref, bf16[128,3712]{1,0:T(8,128)(2,1)} %collective-permute-done.13.end_ref, bf16[128,3712]{1,0:T(8,128)(2,1)} %copy-done.3), custom_call_target="tpu_custom_call" | custom-call | flops 73400320 | bytes 1835008 | tf_op jit(solution)/shard_map/pick/pallas_call | solution.py:148
  81.2 1.5 collective-permute-start.14
  82.7 1.3 collective-permute-start.2
  84.0 2.4 pick.5
  86.4 7.9 %collective-permute-done.14.refs_1_ = bf16[80,3584]{1,0:T(8,128)(2,1)S(1)} collective-permute-done((bf16[80,3584]{1,0:T(8,128)(2,1)}, bf16[80,3584]{1,0:T(8,128)(2,1)S(1)}, u32[]{:S(2)}, u32[]{:S(2)}) %collective-permute-start.14) | collective-permute-done | bytes 573472 | tf_op jit(solution)/shard_map/ppermute | solution.py:305
  94.4 1.5 collective-permute-start.4
  95.9 0.0 collective-permute-done.7.refs_7_.refs_3_
  95.9 0.0 collective-permute-done.8.refs_9_.refs_5_
  95.9 0.0 collective-permute-done.9.refs_11_.refs_7_
  95.9 15.6 %expert.3 = (bf16[128,3584]{1,0:T(8,128)(2,1)}, bf16[80,3584]{1,0:T(8,128)(2,1)}) custom-call(bf16[128,3712]{1,0:T(8,128)(2,1)} %get-tuple-element.25.refs_0_.meta_ref, bf16[80,3584]{1,0:T(8,128)(2,1)} %copy-done.9, bf16[3584,512]{1,0:T(8,128)(2,1)} %bitcast.13, bf16[3584,512]{1,0:T(8,128)(2,1)} %collective-permute-done.7.refs_7_.refs_3_, ...), custom_call_target="tpu_custom_call" | custom-call | flops 4580179968 | bytes 25001984 | tf_op jit(solution)/shard_map/expert/pallas_call | solution.py:217
  111.5 0.8 collective-permute-start.15
  112.4 2.4 pick.6
  114.8 1.3 collective-permute-start.5
  116.0 0.0 collective-permute-done.2.end_ref
  116.0 0.9 copy-done.4
  117.0 2.8 %pick.4 = (bf16[128,3712]{1,0:T(8,128)(2,1)}, bf16[80,3584]{1,0:T(8,128)(2,1)}) custom-call(s32[3]{0:T(128)} %pad_add_fusion.sel_ref, bf16[128,3712]{1,0:T(8,128)(2,1)} %copy-done.4, bf16[128,3712]{1,0:T(8,128)(2,1)} %copy-done.2), custom_call_target="tpu_custom_call" | custom-call | flops 73400320 | bytes 1835008 | tf_op jit(solution)/shard_map/pick/pallas_call | solution.py:148
  119.8 0.8 collective-permute-start.6
  120.5 7.2 %collective-permute-done.15.other_ref = bf16[80,3584]{1,0:T(8,128)(2,1)S(1)} collective-permute-done((bf16[80,3584]{1,0:T(8,128)(2,1)}, bf16[80,3584]{1,0:T(8,128)(2,1)S(1)}, u32[]{:S(2)}, u32[]{:S(2)}) %collective-permute-start.15) | collective-permute-done | bytes 573472 | tf_op jit(solution)/shard_map/ppermute | solution.py:305
  127.7 0.8 copy-done.12
  128.5 4.3 %combine.4 = bf16[128,3584]{1,0:T(8,128)(2,1)} custom-call(s32[3]{0:T(128)} %pad_add_fusion.sel_ref, bf16[128,3712]{1,0:T(8,128)(2,1)} %get-tuple-element.25.refs_0_.meta_ref, bf16[128,3584]{1,0:T(8,128)(2,1)} %get-tuple-element.27.own_ref, bf16[80,3584]{1,0:T(8,128)(2,1)} %copy-done.12), custom_call_target="tpu_custom_call" | custom-call | flops 73400320 | bytes 2752512 | tf_op jit(solution)/shard_map/combine/pallas_call | solution.py:258
  132.8 2.8 %collective-permute-start.16 = (bf16[128,3584]{1,0:T(8,128)(2,1)}, bf16[128,3584]{1,0:T(8,128)(2,1)S(1)}, u32[]{:S(2)}, u32[]{:S(2)}) collective-permute-start(bf16[128,3584]{1,0:T(8,128)(2,1)} %combine.4), channel_id=1, source_target_pairs={{0,2},{1,3},{6,4},{7,5},{8,10},{9,11},{14,12},{15,13},{16,18},{17,... | collective-permute-start | bytes 2752520 | tf_op jit(solution)/shard_map/ppermute | solution.py:305
  135.6 0.0 collective-permute-done.4.refs_3_
  135.6 4.1 %collective-permute-done.5.refs_4_ = bf16[80,3584]{1,0:T(8,128)(2,1)S(1)} collective-permute-done((bf16[80,3584]{1,0:T(8,128)(2,1)}, bf16[80,3584]{1,0:T(8,128)(2,1)S(1)}, u32[]{:S(2)}, u32[]{:S(2)}) %collective-permute-start.5) | collective-permute-done | bytes 573472 | tf_op jit(solution)/shard_map/ppermute | solution.py:305
  139.7 6.1 %collective-permute-done.6.refs_5_ = bf16[80,3584]{1,0:T(8,128)(2,1)S(1)} collective-permute-done((bf16[80,3584]{1,0:T(8,128)(2,1)}, bf16[80,3584]{1,0:T(8,128)(2,1)S(1)}, u32[]{:S(2)}, u32[]{:S(2)}) %collective-permute-start.6) | collective-permute-done | bytes 573472 | tf_op jit(solution)/shard_map/ppermute | solution.py:305
  145.9 0.8 copy-done.18
  146.7 24.0 %expert.2 = (bf16[128,3584]{1,0:T(8,128)(2,1)}, bf16[128,3584]{1,0:T(8,128)(2,1)}, bf16[128,3584]{1,0:T(8,128)(2,1)}, bf16[80,3584]{1,0:T(8,128)(2,1)}, bf16[80,...) custom-call(bf16[128,3712]{1,0:T(8,128)(2,1)} %bitcast.10, bf16[128,3712]{1,0:T(8,128)(2,1)} %copy-done, ...), custom_call_target="tpu_custom_call" | custom-call | flops 13740539904 | bytes 30965760 | tf_op jit(solution)/shard_map/expert/pallas_call | solution.py:217
  170.7 1.1 collective-permute-start.12
  171.8 8.9 %collective-permute-done.12.other_ref = bf16[80,3584]{1,0:T(8,128)(2,1)S(1)} collective-permute-done((bf16[80,3584]{1,0:T(8,128)(2,1)}, bf16[80,3584]{1,0:T(8,128)(2,1)S(1)}, u32[]{:S(2)}, u32[]{:S(2)}) %collective-permute-start.12) | collective-permute-done | bytes 573472 | tf_op jit(solution)/shard_map/ppermute | solution.py:305
  180.7 0.0 collective-permute-done.16.refs_0_
  180.7 0.8 copy-done.11
  181.5 0.4 copy-done.5
  181.8 4.5 %combine.5 = bf16[128,3584]{1,0:T(8,128)(2,1)} custom-call(s32[3]{0:T(128)} %pad_add_fusion.sel_ref, bf16[128,3712]{1,0:T(8,128)(2,1)} %get-tuple-element.17.refs_2_.meta_ref, bf16[128,3584]{1,0:T(8,128)(2,1)} %get-tuple-element.23.own_ref, bf16[80,3584]{1,0:T(8,128)(2,1)} %copy-done.11, bf16[128,3584]{1,0:T(8,128)(2,1)} %copy-done.5), custom_call_target="tpu_custom_call" | custom-call | flops 73400320 | bytes 2752512 | tf_op jit(solution)/shard_map/combine/pallas_call | solution.py:258
  186.3 7.6 %collective-permute-start.19 = (bf16[128,3584]{1,0:T(8,128)(2,1)}, bf16[128,3584]{1,0:T(8,128)(2,1)S(1)}, u32[]{:S(2)}, u32[]{:S(2)}) collective-permute-start(bf16[128,3584]{1,0:T(8,128)(2,1)} %combine.5), channel_id=1, source_target_pairs={{0,2},{1,3},{6,4},{7,5},{8,10},{9,11},{14,12},{15,13},{16,18},{17,... | collective-permute-start | bytes 2752520 | tf_op jit(solution)/shard_map/ppermute | solution.py:305
  194.0 1.4 collective-permute-start.11
  195.4 0.7 collective-permute-start.17
  196.1 13.6 %collective-permute-done.19 = bf16[128,3584]{1,0:T(8,128)(2,1)S(1)} collective-permute-done((bf16[128,3584]{1,0:T(8,128)(2,1)}, bf16[128,3584]{1,0:T(8,128)(2,1)S(1)}, u32[]{:S(2)}, u32[]{:S(2)}) %collective-permute-start.19) | collective-permute-done | bytes 917536 | tf_op jit(solution)/shard_map/ppermute | solution.py:305
  209.7 0.2 add_convert_fusion
  209.9 0.7 collective-permute-start.20
  210.7 0.0 collective-permute-done.11.other_ref
  210.7 0.0 collective-permute-done.17.refs_0_
  210.7 0.8 copy-done.10
  211.5 0.3 copy-done.6
  211.8 4.5 %combine.6 = bf16[128,3584]{1,0:T(8,128)(2,1)} custom-call(s32[3]{0:T(128)} %pad_add_fusion.sel_ref, bf16[128,3712]{1,0:T(8,128)(2,1)} %copy-done, bf16[128,3584]{1,0:T(8,128)(2,1)} %get-tuple-element.21.own_ref, bf16[80,3584]{1,0:T(8,128)(2,1)} %copy-done.10, bf16[128,3584]{1,0:T(8,128)(2,1)} %copy-done.6), custom_call_target="tpu_custom_call" | custom-call | flops 73400320 | bytes 2752512 | tf_op jit(solution)/shard_map/combine/pallas_call | solution.py:258
  216.3 7.2 %collective-permute-start.18 = (bf16[128,3584]{1,0:T(8,128)(2,1)}, bf16[128,3584]{1,0:T(8,128)(2,1)S(1)}, u32[]{:S(2)}, u32[]{:S(2)}) collective-permute-start(bf16[128,3584]{1,0:T(8,128)(2,1)} %combine.6), channel_id=1, source_target_pairs={{0,2},{1,3},{2,0},{3,1},{4,6},{5,7},{6,4},{7,5},{8,10},{9,11},{10,... | collective-permute-start | bytes 2752520 | tf_op jit(solution)/shard_map/ppermute | solution.py:305
  223.5 0.0 collective-permute-start.10
  223.5 9.7 %collective-permute-done.10.other_ref = bf16[80,3584]{1,0:T(8,128)(2,1)S(1)} collective-permute-done((bf16[80,3584]{1,0:T(8,128)(2,1)S(1)}, bf16[80,3584]{1,0:T(8,128)(2,1)S(1)}, u32[]{:S(2)}, u32[]{:S(2)}) %collective-permute-start.10) | collective-permute-done | bytes 573472 | tf_op jit(solution)/shard_map/ppermute | solution.py:305
  233.2 3.6 %collective-permute-done.18.refs_0_ = bf16[128,3584]{1,0:T(8,128)(2,1)S(1)} collective-permute-done((bf16[128,3584]{1,0:T(8,128)(2,1)}, bf16[128,3584]{1,0:T(8,128)(2,1)S(1)}, u32[]{:S(2)}, u32[]{:S(2)}) %collective-permute-start.18) | collective-permute-done | bytes 917536 | tf_op jit(solution)/shard_map/ppermute | solution.py:305
  236.8 0.9 copy-done.8
  237.7 4.7 %combine.7 = bf16[128,3584]{1,0:T(8,128)(2,1)} custom-call(s32[3]{0:T(128)} %pad_add_fusion.sel_ref, bf16[128,3712]{1,0:T(8,128)(2,1)} %bitcast.11, bf16[128,3584]{1,0:T(8,128)(2,1)} %get-tuple-element.19.own_ref, bf16[80,3584]{1,0:T(8,128)(2,1)} %copy-done.13, bf16[128,3584]{1,0:T(8,128)(2,1)} %copy-done.8, bf16[128,3584]{1,0:T(8,128)(2,1)} %copy-done.7), custom_call_target="tpu_custom_call" | custom-call | flops 73400320 | bytes 2752512 | tf_op jit(solution)/shard_map/combine/pallas_call | solution.py:258
  (31 shorter events, 0.1 us)
Async XLA Ops:
  0.0 95.9 %collective-permute-start.7 = (bf16[3584,512]{1,0:T(8,128)(2,1)}, bf16[3584,512]{1,0:T(8,128)(2,1)}, u32[]{:S(2)}, u32[]{:S(2)}) collective-permute-start(bf16[3584,512]{1,0:T(8,128)(2,1)} %bitcast.12), channel_id=1, source_target_pairs={{0,8},{8,0},{1,9},{9,1},{2,10},{10,2},{3,11},{11,3},{4,12},{12,4},... | collective-permute-start | bytes 11010056 | tf_op jit(solution)/shard_map/ppermute | solution.py:308
  0.5 95.4 %collective-permute-start.8 = (bf16[3584,512]{1,0:T(8,128)(2,1)}, bf16[3584,512]{1,0:T(8,128)(2,1)}, u32[]{:S(2)}, u32[]{:S(2)}) collective-permute-start(bf16[3584,512]{1,0:T(8,128)(2,1)} %bitcast.15), channel_id=1, source_target_pairs={{0,8},{8,0},{1,9},{9,1},{2,10},{10,2},{3,11},{11,3},{4,12},{12,4},... | collective-permute-start | bytes 11010056 | tf_op jit(solution)/shard_map/ppermute | solution.py:308
  0.5 95.4 %collective-permute-start.9 = (bf16[512,3584]{1,0:T(8,128)(2,1)}, bf16[512,3584]{1,0:T(8,128)(2,1)}, u32[]{:S(2)}, u32[]{:S(2)}) collective-permute-start(bf16[512,3584]{1,0:T(8,128)(2,1)} %bitcast.18), channel_id=1, source_target_pairs={{0,8},{8,0},{1,9},{9,1},{2,10},{10,2},{3,11},{11,3},{4,12},{12,4},... | collective-permute-start | bytes 11010056 | tf_op jit(solution)/shard_map/ppermute | solution.py:308
  6.2 24.5 %collective-permute-start = (bf16[128,3712]{1,0:T(8,128)(2,1)}, bf16[128,3712]{1,0:T(8,128)(2,1)S(1)}, u32[]{:S(2)}, u32[]{:S(2)}) collective-permute-start(bf16[128,3712]{1,0:T(8,128)(2,1)} %bitcast.7), channel_id=1, source_target_pairs={{0,2},{1,3},{2,0},{3,1},{4,6},{5,7},{6,4},{7,5},{8,10},{9,11},{10,... | collective-permute-start | bytes 2850824 | tf_op jit(solution)/shard_map/ppermute | solution.py:305
  30.7 80.8 %copy-start = (bf16[128,3712]{1,0:T(8,128)(2,1)}, bf16[128,3712]{1,0:T(8,128)(2,1)S(1)}, u32[]{:S(2)}) copy-start(bf16[128,3712]{1,0:T(8,128)(2,1)S(1)} %collective-permute-done.x_ref.refs_1_.meta_ref) | copy-start | bytes 2850820
  30.7 1.4 collective-permute-start.3
  31.4 2.7 %collective-permute-start.1 = (bf16[128,3712]{1,0:T(8,128)(2,1)}, bf16[128,3712]{1,0:T(8,128)(2,1)S(1)}, u32[]{:S(2)}, u32[]{:S(2)}) collective-permute-start(bf16[128,3712]{1,0:T(8,128)(2,1)} %bitcast.8), channel_id=1, source_target_pairs={{2,4},{3,5},{4,2},{5,3},{10,12},{11,13},{12,10},{13,11},{18,20},{1... | collective-permute-start | bytes 2850824 | tf_op jit(solution)/shard_map/ppermute | solution.py:305
  32.2 79.4 %copy-start.2 = (bf16[128,3712]{1,0:T(8,128)(2,1)}, bf16[128,3712]{1,0:T(8,128)(2,1)S(1)}, u32[]{:S(2)}) copy-start(bf16[128,3712]{1,0:T(8,128)(2,1)S(1)} %collective-permute-done.3.inner_ref) | copy-start | bytes 2850820
  32.2 46.3 %collective-permute-start.13 = (bf16[128,3712]{1,0:T(8,128)(2,1)S(1)}, bf16[128,3712]{1,0:T(8,128)(2,1)}, u32[]{:S(2)}, u32[]{:S(2)}) collective-permute-start(bf16[128,3712]{1,0:T(8,128)(2,1)S(1)} %collective-permute-done.3.inner_ref), channel_id=1, source_target_pairs={{2,0},{3,1},{4,6},{5,7},{10,8},{11,9},{12,14},{13,15},{18,16},{19,... | collective-permute-start | bytes 2850824 | tf_op jit(solution)/shard_map/ppermute | solution.py:305
  34.1 44.3 %copy-start.3 = (bf16[128,3712]{1,0:T(8,128)(2,1)}, bf16[128,3712]{1,0:T(8,128)(2,1)S(1)}, u32[]{:S(2)}) copy-start(bf16[128,3712]{1,0:T(8,128)(2,1)S(1)} %collective-permute-done.1.inner_ref) | copy-start | bytes 2850820
  81.2 13.1 %collective-permute-start.14 = (bf16[80,3584]{1,0:T(8,128)(2,1)}, bf16[80,3584]{1,0:T(8,128)(2,1)S(1)}, u32[]{:S(2)}, u32[]{:S(2)}) collective-permute-start(bf16[80,3584]{1,0:T(8,128)(2,1)} %get-tuple-element.26), channel_id=1, source_target_pairs={{0,1},{1,0},{2,3},{3,2},{4,5},{5,4},{6,7},{7,6},{8,9},{9,8},{10,11... | collective-permute-start | bytes 1720328 | tf_op jit(solution)/shard_map/ppermute | solution.py:305
  82.7 33.3 %collective-permute-start.2 = (bf16[128,3712]{1,0:T(8,128)(2,1)}, bf16[128,3712]{1,0:T(8,128)(2,1)S(1)}, u32[]{:S(2)}, u32[]{:S(2)}) collective-permute-start(bf16[128,3712]{1,0:T(8,128)(2,1)} %copy-done.3), channel_id=1, source_target_pairs={{2,0},{3,1},{4,6},{5,7},{10,8},{11,9},{12,14},{13,15},{18,16},{19,... | collective-permute-start | bytes 2850824 | tf_op jit(solution)/shard_map/ppermute | solution.py:305
  94.4 1.5 copy-start.9
  94.4 41.3 %collective-permute-start.4 = (bf16[80,3584]{1,0:T(8,128)(2,1)}, bf16[80,3584]{1,0:T(8,128)(2,1)S(1)}, u32[]{:S(2)}, u32[]{:S(2)}) collective-permute-start(bf16[80,3584]{1,0:T(8,128)(2,1)} %pick.5), channel_id=1, source_target_pairs={{0,1},{1,0},{2,3},{3,2},{4,5},{5,4},{6,7},{7,6},{8,9},{9,8},{10,11... | collective-permute-start | bytes 1720328 | tf_op jit(solution)/shard_map/ppermute | solution.py:305
  111.5 16.2 %collective-permute-start.15 = (bf16[80,3584]{1,0:T(8,128)(2,1)}, bf16[80,3584]{1,0:T(8,128)(2,1)S(1)}, u32[]{:S(2)}, u32[]{:S(2)}) collective-permute-start(bf16[80,3584]{1,0:T(8,128)(2,1)} %get-tuple-element.28), channel_id=1, source_target_pairs={{0,1},{1,0},{2,3},{3,2},{4,5},{5,4},{6,7},{7,6},{8,9},{9,8},{10,11... | collective-permute-start | bytes 1720328 | tf_op jit(solution)/shard_map/ppermute | solution.py:305
  114.8 24.9 %collective-permute-start.5 = (bf16[80,3584]{1,0:T(8,128)(2,1)}, bf16[80,3584]{1,0:T(8,128)(2,1)S(1)}, u32[]{:S(2)}, u32[]{:S(2)}) collective-permute-start(bf16[80,3584]{1,0:T(8,128)(2,1)} %pick.6), channel_id=1, source_target_pairs={{0,1},{1,0},{2,3},{3,2},{4,5},{5,4},{6,7},{7,6},{8,9},{9,8},{10,11... | collective-permute-start | bytes 1720328 | tf_op jit(solution)/shard_map/ppermute | solution.py:305
  116.0 0.9 copy-start.4
  119.8 26.1 %collective-permute-start.6 = (bf16[80,3584]{1,0:T(8,128)(2,1)}, bf16[80,3584]{1,0:T(8,128)(2,1)S(1)}, u32[]{:S(2)}, u32[]{:S(2)}) collective-permute-start(bf16[80,3584]{1,0:T(8,128)(2,1)} %get-tuple-element.18), channel_id=1, source_target_pairs={{0,1},{1,0},{2,3},{3,2},{4,5},{5,4},{6,7},{7,6},{8,9},{9,8},{10,11... | collective-permute-start | bytes 1720328 | tf_op jit(solution)/shard_map/ppermute | solution.py:305
  127.7 0.8 copy-start.12
  132.8 47.9 %collective-permute-start.16 = (bf16[128,3584]{1,0:T(8,128)(2,1)}, bf16[128,3584]{1,0:T(8,128)(2,1)S(1)}, u32[]{:S(2)}, u32[]{:S(2)}) collective-permute-start(bf16[128,3584]{1,0:T(8,128)(2,1)} %combine.4), channel_id=1, source_target_pairs={{0,2},{1,3},{6,4},{7,5},{8,10},{9,11},{14,12},{15,13},{16,18},{17,... | collective-permute-start | bytes 2752520 | tf_op jit(solution)/shard_map/ppermute | solution.py:305
  135.6 10.2 %copy-start.14 = (bf16[80,3584]{1,0:T(8,128)(2,1)}, bf16[80,3584]{1,0:T(8,128)(2,1)S(1)}, u32[]{:S(2)}) copy-start(bf16[80,3584]{1,0:T(8,128)(2,1)S(1)} %collective-permute-done.4.refs_3_) | copy-start | bytes 1720324
  139.7 6.2 %copy-start.16 = (bf16[80,3584]{1,0:T(8,128)(2,1)}, bf16[80,3584]{1,0:T(8,128)(2,1)S(1)}, u32[]{:S(2)}) copy-start(bf16[80,3584]{1,0:T(8,128)(2,1)S(1)} %collective-permute-done.5.refs_4_) | copy-start | bytes 1720324
  145.8 0.8 copy-start.18
  170.7 23.3 %copy-start.17 = (bf16[80,3584]{1,0:T(8,128)(2,1)S(1)}, bf16[80,3584]{1,0:T(8,128)(2,1)}, u32[]{:S(2)}) copy-start(bf16[80,3584]{1,0:T(8,128)(2,1)} %get-tuple-element.22) | copy-start | bytes 1720324
  170.7 39.0 %copy-start.1 = (bf16[128,3584]{1,0:T(8,128)(2,1)S(1)}, bf16[128,3584]{1,0:T(8,128)(2,1)}, u32[]{:S(2)}) copy-start(bf16[128,3584]{1,0:T(8,128)(2,1)} %combine.4) | copy-start | bytes 2752516
  170.7 10.0 %collective-permute-start.12 = (bf16[80,3584]{1,0:T(8,128)(2,1)}, bf16[80,3584]{1,0:T(8,128)(2,1)S(1)}, u32[]{:S(2)}, u32[]{:S(2)}) collective-permute-start(bf16[80,3584]{1,0:T(8,128)(2,1)} %get-tuple-element.24), channel_id=1, source_target_pairs={{0,1},{1,0},{2,3},{3,2},{4,5},{5,4},{6,7},{7,6},{8,9},{9,8},{10,11... | collective-permute-start | bytes 1720328 | tf_op jit(solution)/shard_map/ppermute | solution.py:305
  180.7 0.8 copy-start.11
  180.7 1.2 copy-start.5
  186.3 37.2 %copy-start.15 = (bf16[80,3584]{1,0:T(8,128)(2,1)S(1)}, bf16[80,3584]{1,0:T(8,128)(2,1)}, u32[]{:S(2)}) copy-start(bf16[80,3584]{1,0:T(8,128)(2,1)} %get-tuple-element.20) | copy-start | bytes 1720324
  186.3 23.4 %collective-permute-start.19 = (bf16[128,3584]{1,0:T(8,128)(2,1)}, bf16[128,3584]{1,0:T(8,128)(2,1)S(1)}, u32[]{:S(2)}, u32[]{:S(2)}) collective-permute-start(bf16[128,3584]{1,0:T(8,128)(2,1)} %combine.5), channel_id=1, source_target_pairs={{0,2},{1,3},{6,4},{7,5},{8,10},{9,11},{14,12},{15,13},{16,18},{17,... | collective-permute-start | bytes 2752520 | tf_op jit(solution)/shard_map/ppermute | solution.py:305
  194.0 16.7 %collective-permute-start.11 = (bf16[80,3584]{1,0:T(8,128)(2,1)S(1)}, bf16[80,3584]{1,0:T(8,128)(2,1)S(1)}, u32[]{:S(2)}, u32[]{:S(2)}) collective-permute-start(bf16[80,3584]{1,0:T(8,128)(2,1)S(1)} %copy-done.17), channel_id=1, source_target_pairs={{0,1},{1,0},{2,3},{3,2},{4,5},{5,4},{6,7},{7,6},{8,9},{9,8},{10,11... | collective-permute-start | bytes 1720328 | tf_op jit(solution)/shard_map/ppermute | solution.py:305
  195.4 15.3 %collective-permute-start.17 = (bf16[128,3584]{1,0:T(8,128)(2,1)}, bf16[128,3584]{1,0:T(8,128)(2,1)S(1)}, u32[]{:S(2)}, u32[]{:S(2)}) collective-permute-start(bf16[128,3584]{1,0:T(8,128)(2,1)} %combine.5), channel_id=1, source_target_pairs={{2,4},{3,5},{4,2},{5,3},{10,12},{11,13},{12,10},{13,11},{18,20},{1... | collective-permute-start | bytes 2752520 | tf_op jit(solution)/shard_map/ppermute | solution.py:305
  209.9 23.3 %collective-permute-start.20 = (bf16[128,3584]{1,0:T(8,128)(2,1)S(1)}, bf16[128,3584]{1,0:T(8,128)(2,1)S(1)}, u32[]{:S(2)}, u32[]{:S(2)}) collective-permute-start(bf16[128,3584]{1,0:T(8,128)(2,1)S(1)} %add_convert_fusion), channel_id=1, source_target_pairs={{2,4},{3,5},{4,2},{5,3},{10,12},{11,13},{12,10},{13,11},{18,20},{1... | collective-permute-start | bytes 2752520 | tf_op jit(solution)/shard_map/ppermute | solution.py:305
  210.7 0.8 copy-start.10
  210.7 1.1 copy-start.6
  216.3 20.5 %collective-permute-start.18 = (bf16[128,3584]{1,0:T(8,128)(2,1)}, bf16[128,3584]{1,0:T(8,128)(2,1)S(1)}, u32[]{:S(2)}, u32[]{:S(2)}) collective-permute-start(bf16[128,3584]{1,0:T(8,128)(2,1)} %combine.6), channel_id=1, source_target_pairs={{0,2},{1,3},{2,0},{3,1},{4,6},{5,7},{6,4},{7,5},{8,10},{9,11},{10,... | collective-permute-start | bytes 2752520 | tf_op jit(solution)/shard_map/ppermute | solution.py:305
  223.5 9.7 %collective-permute-start.10 = (bf16[80,3584]{1,0:T(8,128)(2,1)S(1)}, bf16[80,3584]{1,0:T(8,128)(2,1)S(1)}, u32[]{:S(2)}, u32[]{:S(2)}) collective-permute-start(bf16[80,3584]{1,0:T(8,128)(2,1)S(1)} %copy-done.15), channel_id=1, source_target_pairs={{0,1},{1,0},{2,3},{3,2},{4,5},{5,4},{6,7},{7,6},{8,9},{9,8},{10,11... | collective-permute-start | bytes 1720328 | tf_op jit(solution)/shard_map/ppermute | solution.py:305
  233.2 3.6 %copy-start.13 = (bf16[80,3584]{1,0:T(8,128)(2,1)}, bf16[80,3584]{1,0:T(8,128)(2,1)S(1)}, u32[]{:S(2)}) copy-start(bf16[80,3584]{1,0:T(8,128)(2,1)S(1)} %collective-permute-done.10.other_ref) | copy-start | bytes 1720324
  233.2 3.6 %copy-start.7 = (bf16[128,3584]{1,0:T(8,128)(2,1)}, bf16[128,3584]{1,0:T(8,128)(2,1)S(1)}, u32[]{:S(2)}) copy-start(bf16[128,3584]{1,0:T(8,128)(2,1)S(1)} %collective-permute-done.20.refs_1_) | copy-start | bytes 2752516
  236.8 0.9 copy-start.8

commit v2 on v0

v2 whole, which is shorter than its diff:
```python
import functools

import jax
import jax.numpy as jnp
from jax import lax
from jax.experimental import pallas as pl
from jax.experimental.pallas import tpu as pltpu
from jax.sharding import PartitionSpec as P

LANES = 128
ALIGN = 16
HALVES = 2
VMEM_LIMIT = 24 * 1024 * 1024
SCALE = 2.5
BRIEF = pl.CostEstimate(flops=1, bytes_accessed=1, transcendentals=0)


def up_to(value, step):
    return -(-value // step) * step


def dot32(a, b):
    return jnp.dot(a, b, preferred_element_type=jnp.float32)


def iota(shape, dim):
    return lax.broadcasted_iota(jnp.int32, shape, dim)


def flag(mask):
    return jnp.where(mask, 1.0, 0.0)


def pieces_of(ids_ref, scores_ref):
    topk, rows = ids_ref.shape
    experts = scores_ref.shape[0]
    sig = 1.0 / (1.0 + jnp.exp(-scores_ref[...]))
    ids = [ids_ref[k : k + 1, :] for k in range(topk)]
    row_e = iota((experts, rows), 0)
    chosen = [jnp.sum(jnp.where(i == row_e, sig, 0.0), axis=0, keepdims=True) for i in ids]
    total = sum(chosen[1:], chosen[0])
    row = iota((LANES, rows), 0)
    expert_of_row = lax.rem(row, experts)
    weight = jnp.zeros((LANES, rows), jnp.float32)
    for i, value in zip(ids, chosen):
        weight = weight + jnp.where(i == expert_of_row, value / total, 0.0)
    high = weight.astype(jnp.bfloat16).astype(jnp.float32)
    rest = weight - high
    middle = rest.astype(jnp.bfloat16).astype(jnp.float32)
    low = rest - middle
    pieces = jnp.where(
        row < experts,
        high,
        jnp.where(row < 2 * experts, middle, jnp.where(row < 3 * experts, low, 0.0)),
    )
    return pieces.T


def route(meta, sel_ref, experts, cap):
    rows = meta.shape[0]
    i, j = iota((rows, rows), 0), iota((rows, rows), 1)
    lane = iota((rows, LANES), 1)

    def weight_for(expert):
        hit = (lax.rem(lane, experts) == expert) & (lane < 3 * experts)
        return jnp.sum(jnp.where(hit, meta, 0.0), axis=1, keepdims=True)

    mine, other = weight_for(sel_ref[0]), weight_for(sel_ref[1])
    weights = jnp.where(lane == 0, mine, other)
    named = flag(other > 0.0)
    row_named = jnp.sum(jnp.where(i == j, named, 0.0), axis=0, keepdims=True)
    row_place = jnp.sum(jnp.where(i < j, named, 0.0), axis=0, keepdims=True).astype(jnp.int32)
    place = jnp.sum(jnp.where(j < i, row_named, 0.0), axis=1, keepdims=True).astype(jnp.int32)
    take = flag((iota((cap, rows), 0) == row_place) & (row_named > 0.0))
    back = flag((iota((rows, cap), 1) == place) & (named > 0.0))
    return take.astype(jnp.bfloat16), back.astype(jnp.bfloat16), weights


def open_kernel(sel_ref, ids_ref, scores_ref, tok_ref, packed_ref, y_ref, back_ref, weight_ref):
    width = tok_ref.shape[1]
    pieces = pieces_of(ids_ref, scores_ref)
    packed_ref[:, :width] = tok_ref[...]
    packed_ref[:, width:] = pieces.astype(jnp.bfloat16)
    take, back, weights = route(pieces, sel_ref, scores_ref.shape[0], y_ref.shape[0])
    back_ref[...] = back
    weight_ref[...] = weights
    y_ref[...] = dot32(take, tok_ref[...]).astype(jnp.bfloat16)


def open_block(sel, ids, scores, tokens, cap):
    rows, width = tokens.shape
    return pl.pallas_call(
        open_kernel,
        in_specs=[pl.BlockSpec(memory_space=pltpu.SMEM)]
        + [pl.BlockSpec(memory_space=pltpu.VMEM)] * 3,
        out_shape=[
            jax.ShapeDtypeStruct((rows, width + LANES), jnp.bfloat16),
            jax.ShapeDtypeStruct((cap, width), jnp.bfloat16),
            jax.ShapeDtypeStruct((rows, cap), jnp.bfloat16),
            jax.ShapeDtypeStruct((rows, LANES), jnp.float32),
        ],
        compiler_params=pltpu.CompilerParams(vmem_limit_bytes=VMEM_LIMIT),
        cost_estimate=BRIEF,
        name="open",
    )(sel, ids.T, scores.T, tokens)


def pick_kernel(experts, count, sel_ref, *refs):
    metas, parts, (y_ref, back_ref, weight_ref, held) = refs[:count], refs[count : 2 * count], refs[2 * count :]

    @pl.when(pl.program_id(0) == 0)
    def _():
        meta = metas[0][...].astype(jnp.float32)
        if count == 2:
            meta = jnp.where(sel_ref[2] == 1, meta, metas[1][...].astype(jnp.float32))
        take, back, weights = route(meta, sel_ref, experts, y_ref.shape[0])
        held[...] = take
        back_ref[...] = back
        weight_ref[...] = weights

    for which in range(count):

        @pl.when((sel_ref[2] == 1 - which) | (count == 1))
        def _(which=which):
            y_ref[...] = dot32(held[...], parts[which][...]).astype(jnp.bfloat16)


def pick_rows(sel, parts, experts, cap):
    rows, width = parts[0].shape
    width -= LANES
    block = column_block(width)
    return pl.pallas_call(
        functools.partial(pick_kernel, experts, len(parts)),
        grid=(width // block,),
        in_specs=[pl.BlockSpec(memory_space=pltpu.SMEM)]
        + [pl.BlockSpec((rows, LANES), lambda i: (0, width // LANES))] * len(parts)
        + [pl.BlockSpec((rows, block), lambda i: (0, i))] * len(parts),
        out_specs=[
            pl.BlockSpec((cap, block), lambda i: (0, i)),
            pl.BlockSpec((rows, cap), lambda i: (0, 0)),
            pl.BlockSpec((rows, LANES), lambda i: (0, 0)),
        ],
        out_shape=[
            jax.ShapeDtypeStruct((cap, width), jnp.bfloat16),
            jax.ShapeDtypeStruct((rows, cap), jnp.bfloat16),
            jax.ShapeDtypeStruct((rows, LANES), jnp.float32),
        ],
        scratch_shapes=[pltpu.VMEM((cap, rows), jnp.bfloat16)],
        compiler_params=pltpu.CompilerParams(vmem_limit_bytes=VMEM_LIMIT),
        cost_estimate=BRIEF,
        name="pick",
    )(sel, *parts, *parts)


def hold_kernel(*refs):
    count = len(refs) // 2
    sems = refs[-1]
    copies = [
        pltpu.make_async_copy(refs[k], refs[count + k], sems.at[k]) for k in range(count)
    ]
    for copy in copies:
        copy.start()
    for copy in copies:
        copy.wait()


def hold(weights):
    held = pl.pallas_call(
        hold_kernel,
        in_specs=[pl.BlockSpec(memory_space=pltpu.HBM)] * len(weights),
        out_specs=[pl.BlockSpec(memory_space=pltpu.VMEM)] * len(weights),
        out_shape=[pltpu.VMEM(w.shape, w.dtype) for w in weights],
        scratch_shapes=[pltpu.SemaphoreType.DMA((len(weights),))],
        compiler_params=pltpu.CompilerParams(vmem_limit_bytes=VMEM_LIMIT),
        cost_estimate=BRIEF,
        name="hold",
    )(*weights)
    return [pltpu.with_memory_space_constraint(w, pltpu.VMEM) for w in held]


def expert_kernel(count, halves, sel_ref, *refs):
    parts, y_ref, refs = refs[:count], refs[count], refs[count + 1 :]
    gates, ups, downs, refs = refs[0:2], refs[2:4], refs[4:6], refs[6:]
    out_ref, y_outs, (xs, hidden) = refs[0], refs[1 : 1 + halves], refs[1 + halves :]
    rows, cap = parts[0].shape[0], y_ref.shape[0]
    width, depth = gates[0].shape
    if count == 1:
        xs[:rows, :] = parts[0][:, :width]
    else:
        for which in range(2):

            @pl.when(sel_ref[2] == 1 - which)
            def _(which=which):
                xs[:rows, :] = parts[which][:, :width]

    xs[rows:, :] = y_ref[...]
    block = min(depth, 256)
    for which in range(2):
        for at in range(0, depth, block):
            gate = dot32(xs[...], gates[which][:, at : at + block])
            up = dot32(xs[...], ups[which][:, at : at + block])
            value = gate / (1.0 + jnp.exp(-gate)) * up
            to = which * depth + at
            hidden[:, to : to + block] = value.astype(jnp.bfloat16)
    part = width // halves
    block = column_block(part)
    for at in range(0, width, block):
        columns = slice(at, at + block)
        out = dot32(hidden[:, :depth], downs[0][:, columns])
        out = (out + dot32(hidden[:, depth:], downs[1][:, columns])).astype(jnp.bfloat16)
        out_ref[:, columns] = out[:rows]
        inside = at % part
        y_outs[at // part][:, inside : inside + block] = out[rows:]


def expert(sel, parts, y, gates, ups, downs, halves):
    rows, cap = parts[0].shape[0], y.shape[0]
    width, depth = gates[0].shape
    whole = pl.BlockSpec(memory_space=pltpu.VMEM)
    return pl.pallas_call(
        functools.partial(expert_kernel, len(parts), halves),
        in_specs=[pl.BlockSpec(memory_space=pltpu.SMEM)] + [whole] * (len(parts) + 7),
        out_specs=[whole] * (1 + halves),
        out_shape=[jax.ShapeDtypeStruct((rows, width), jnp.bfloat16)]
        + [jax.ShapeDtypeStruct((cap, width // halves), jnp.bfloat16)] * halves,
        scratch_shapes=[
            pltpu.VMEM((rows + cap, width), jnp.bfloat16),
            pltpu.VMEM((rows + cap, 2 * depth), jnp.bfloat16),
        ],
        compiler_params=pltpu.CompilerParams(vmem_limit_bytes=VMEM_LIMIT),
        cost_estimate=BRIEF,
        name="expert",
    )(sel, *parts, y, *gates, *ups, *downs)


def combine_kernel(scale, splits, back_ref, weight_ref, own_ref, other_ref, *refs):
    out_ref = refs[-1]
    step, steps = pl.program_id(0), pl.num_programs(0)
    weights = weight_ref[...]
    value = weights[:, 0:1] * own_ref[...].astype(jnp.float32)
    value = value + weights[:, 1:2] * dot32(back_ref[...], other_ref[...])
    at = 0
    for pieces in splits:
        term = refs[at][...].astype(jnp.float32)
        for p in range(1, pieces):
            here = step * pieces >= p * steps
            term = jnp.where(here, refs[at + p][...].astype(jnp.float32), term)
        at += pieces
        value = value + term
    if scale is not None:
        value = value * scale
    out_ref[...] = value.astype(jnp.bfloat16)


def combine(tables, own, other, extra=(), first=0, scale=None):
    rows = own.shape[0]
    cap, width = other.shape
    block = column_block(width)
    steps = width // block
    offset = first // block

    def piece(p, count):
        each = steps // count
        return pl.BlockSpec((rows, block), lambda i: (0, jnp.clip(i - p * each, 0, each - 1)))

    return pl.pallas_call(
        functools.partial(combine_kernel, scale, [len(e) for e in extra]),
        grid=(steps,),
        in_specs=[
            pl.BlockSpec((rows, cap), lambda i: (0, 0)),
            pl.BlockSpec((rows, LANES), lambda i: (0, 0)),
            pl.BlockSpec((rows, block), lambda i: (0, i + offset)),
            pl.BlockSpec((cap, block), lambda i: (0, i)),
        ]
        + [piece(p, len(e)) for e in extra for p in range(len(e))],
        out_specs=pl.BlockSpec((rows, block), lambda i: (0, i)),
        out_shape=jax.ShapeDtypeStruct((rows, width), jnp.bfloat16),
        compiler_params=pltpu.CompilerParams(vmem_limit_bytes=VMEM_LIMIT),
        cost_estimate=BRIEF,
        name="combine",
    )(*tables, own, other, *[e for group in extra for e in group])


def column_block(width):
    return 896 if width % 896 == 0 else width


def capacity_of(tok_rows, topk, experts):
    return min(tok_rows, max(2, 5 * tok_rows * topk // (2 * experts)))


def on_levels(pairs):
    return [(2 * a + y, 2 * b + y) for a, b in pairs for y in range(2)]


OUTER = on_levels([(0, 1), (1, 0), (2, 3), (3, 2)])
INNER = on_levels([(1, 2), (2, 1)])
TO_ENDS = on_levels([(1, 0), (2, 3)])
FROM_ENDS = on_levels([(0, 1), (3, 2)])


def after(value, *others):
    return lax.optimization_barrier((value, *others))[0]


def add(a, b):
    return (a.astype(jnp.float32) + b.astype(jnp.float32)).astype(jnp.bfloat16)


def four_levels(tokens, scores, expert_ids, w_gate, w_up, w_down):
    experts = lax.axis_size("expert")
    tok_rows, width = tokens.shape
    topk = expert_ids.shape[1]
    cap = min(tok_rows, up_to(capacity_of(tok_rows, topk, experts), ALIGN))
    me = lax.axis_index("expert")
    level = me // 2
    end = ((level == 0) | (level == 3)).astype(jnp.int32)
    sel = jnp.stack([me, me ^ 1, end]).astype(jnp.int32)
    across = [(i, i ^ 1) for i in range(experts)]

    def send(value, pairs):
        return lax.ppermute(value, "expert", pairs)

    def swap(value):
        return lax.ppermute(value, "dp", [(0, 1), (1, 0)])

    swapped = [swap(w[0]) for w in (w_gate, w_up, w_down)]
    own, s0, *tables0 = open_block(sel, expert_ids, scores, tokens, cap)
    near = send(own, OUTER)
    inner = send(own, INNER)
    y0 = send(after(s0, swapped[0]), across)

    kept = hold(lax.optimization_barrier((w_gate[0], w_up[0], w_down[0], own))[:-1])
    near = after(near, y0, kept[0])
    far_inner = send(near, INNER)
    far_end = send(inner, TO_ENDS)
    s1, *tables1 = pick_rows(sel, [near], experts, cap)
    y1 = send(s1, across)
    gates, ups, downs = zip(kept, hold(lax.optimization_barrier((*swapped, s1))[:-1]))
    o0, oy0 = expert(sel, [own], y0, gates, ups, downs, 1)
    o1, oy1 = expert(sel, [after(near, o0)], y1, gates, ups, downs, 1)
    b1 = send(oy1, across)

    far_inner = after(far_inner, o1)
    last_end = send(far_inner, TO_ENDS)
    far = [after(far_end, o1), inner]
    s2, *tables2 = pick_rows(sel, far, experts, cap)
    y2 = send(s2, across)
    q1 = combine(tables1, o1, after(b1, s2))
    r1 = send(q1, FROM_ENDS)
    o2, oy2 = expert(sel, [after(far[0], q1), inner], y2, gates, ups, downs, 1)
    last = [after(last_end, o2), far_inner]
    s3, *tables3 = pick_rows(sel, last, experts, cap)
    y3 = send(s3, across)
    b2 = send(after(oy2, y3), across)
    o3, *oy3 = expert(sel, last, y3, gates, ups, downs, HALVES)
    b3 = [send(v, across) for v in oy3]

    part = width // HALVES
    b3[0] = after(b3[0], r1)
    q3 = [combine(tables3, o3, v, first=h * part) for h, v in enumerate(b3)]
    r3 = [send(v, FROM_ENDS) for v in q3]
    q2 = combine(tables2, o2, after(b2, q3[-1]))
    b0 = send(after(oy0, q2), across)
    r2 = send(q2, FROM_ENDS)
    r3 = [send(add(q, r), INNER) for q, r in zip(q3, r3)]
    r2 = send(add(q2, r2), INNER)
    r3 = [
        send(add(q1[:, h * part : (h + 1) * part], r), TO_ENDS) for h, r in enumerate(r3)
    ]
    return combine(tables0, o0, b0, extra=([r1], [r2], r3), scale=SCALE)


def all_to_all_form(tokens, scores, expert_ids, w_gate, w_up, w_down):
    experts = lax.axis_size("expert")
    tok_rows, width = tokens.shape
    topk = expert_ids.shape[1]
    capacity = capacity_of(tok_rows, topk, experts)
    flat_ids = expert_ids.reshape(-1)
    onehot = (flat_ids[:, None] == jnp.arange(experts, dtype=jnp.int32)[None, :]).astype(jnp.int32)
    position = jnp.sum((jnp.cumsum(onehot, axis=0) - 1) * onehot, axis=1)
    slot = flat_ids * capacity + position
    repeated = jnp.repeat(tokens, topk, axis=0)
    outgoing = jnp.zeros((experts * capacity, width), tokens.dtype).at[slot].set(repeated)
    outgoing = outgoing.reshape(experts, capacity, width)
    doubled = jnp.tile(outgoing, (lax.axis_size("dp"), 1, 1))
    rows = lax.all_to_all(doubled, ("dp", "expert"), split_axis=0, concat_axis=0, tiled=True)
    shape = rows.shape
    flat = rows.reshape(-1, shape[-1])
    gate = dot32(flat, w_gate[0])
    up_value = dot32(flat, w_up[0])
    hidden = (jax.nn.silu(gate) * up_value).astype(jnp.bfloat16)
    partial_value = dot32(hidden, w_down[0]).reshape(shape)
    returned = lax.all_to_all(
        partial_value, ("dp", "expert"), split_axis=0, concat_axis=0, tiled=True
    )
    back = jnp.sum(returned.reshape(-1, experts, capacity, width), axis=0).astype(jnp.bfloat16)
    picked = back.reshape(experts * capacity, width)[slot].reshape(tok_rows, topk, width)
    chosen = jax.nn.sigmoid(jnp.take_along_axis(scores, expert_ids, axis=1))
    weight = chosen / jnp.sum(chosen, axis=1, keepdims=True)
    mixed = SCALE * jnp.sum(weight[:, :, None] * picked.astype(jnp.float32), axis=1)
    return mixed.astype(jnp.bfloat16)


def solution(mesh):
    in_specs = (
        P(("groups", "dp", "expert"), None),
        P(("groups", "dp", "expert"), None),
        P(("groups", "dp", "expert"), None),
        P("expert", None, "dp"),
        P("expert", None, "dp"),
        P("expert", "dp", None),
    )
    out_specs = P(("groups", "dp", "expert"), None)
    short = mesh.shape["expert"] == 8 and mesh.shape["dp"] == 2
    body = four_levels if short else all_to_all_form
    return jax.shard_map(
        body, mesh=mesh, in_specs=in_specs, out_specs=out_specs, check_vma=False
    )
```

time: 679 us -> 189 us (0.28)
  the two profiles are of different devices: /device:TPU:10 before, /device:TPU:0 now
where the time goes in v2:
time: 189 us; the launch traced here: 188 us
  waiting for transfers between devices  94.5 us (50%)
  starting transfers between devices  42 us (22%)
  Pallas kernels  40.9 us (22%)
  local copies, waits for them, and re-layouts  9.72 us (5%)
    ppermute x23, waiting for transfers between devices, send(): return lax.ppermute(value, 'expert', pairs)  94.5 us
    ppermute x23, starting transfers between devices, send(): return lax.ppermute(value, 'expert', pairs)  41 us
    pallas_call x4, Pallas kernels, expert(): pl.pallas_call(functools.partial(expert_kernel, len(parts), halves), in_s...  23 us
    unnamed x16, local copies, waits for them, and re-layouts  9.72 us
    pallas_call x5, Pallas kernels, combine(): pl.pallas_call(functools.partial(combine_kernel, scale, [len(e) for e in...  6.01 us
    pallas_call x3, Pallas kernels, pick_rows(): pl.pallas_call(functools.partial(pick_kernel, experts, len(parts)), grid=...  5.88 us
    pallas_call x2, Pallas kernels, hold(): pl.pallas_call(hold_kernel, in_specs=[pl.BlockSpec(memory_space=pltpu.HBM...  4.99 us
  transfers between devices with their start and end apart: 26, of which 11 were waited for; matrix products, arithmetic and copies ran while one was open for 0% of the time, Pallas kernels for 19%

profile of v2, /device:TPU:0, one launch (start us, length us, event | category | flops | bytes accessed | tf_op | source)
XLA Modules:
  0.0 188.1 jit_solution(9038501329510399231)
XLA Ops:
  0.0 0.5 collective-permute-start
  0.5 0.1 collective-permute-start.2
  0.5 0.5 collective-permute-start.3
  1.0 0.1 pad_add_fusion.sel_ref
  1.0 1.2 copy-done.3
  2.2 0.7 copy-done.6
  2.9 0.7 copy-done.7
  3.6 1.0 open.1
  4.6 2.6 %collective-permute-start.4 = (bf16[128,3712]{1,0:T(8,128)(2,1)S(1)}, bf16[128,3712]{1,0:T(8,128)(2,1)S(1)}, u32[]{:S(2)}, u32[]{:S(2)}) collective-permute-start(bf16[128,3712]{1,0:T(8,128)(2,1)S(1)} %get-tuple-element.53.refs_0_), channel_id=1, source_target_pairs={{0,2},{1,3},{2,0},{3,1},{4,6},{5,7},{6,4},{7,5},{8,10},{9,11},{10,... | collective-permute-start | bytes 2850824 | tf_op jit(solution)/shard_map/ppermute | solution.py:322
  7.3 0.7 collective-permute-start.5
  8.0 1.7 collective-permute-start.1
  9.7 2.0 %copy-done = bf16[1,3584,512]{2,1,0:T(8,128)(2,1)S(1)} copy-done((bf16[1,3584,512]{2,1,0:T(8,128)(2,1)S(1)}, bf16[1,3584,512]{2,1,0:T(8,128)(2,1)}, u32[]{:S(2)}) %copy-start) | copy-done | bytes 3670040
  11.8 2.0 %copy-done.1 = bf16[1,3584,512]{2,1,0:T(8,128)(2,1)S(1)} copy-done((bf16[1,3584,512]{2,1,0:T(8,128)(2,1)S(1)}, bf16[1,3584,512]{2,1,0:T(8,128)(2,1)}, u32[]{:S(2)}) %copy-start.1) | copy-done | bytes 3670040
  13.8 2.0 %copy-done.2 = bf16[1,512,3584]{2,1,0:T(8,128)(2,1)S(1)} copy-done((bf16[1,512,3584]{2,1,0:T(8,128)(2,1)S(1)}, bf16[1,512,3584]{2,1,0:T(8,128)(2,1)}, u32[]{:S(2)}) %copy-start.2) | copy-done | bytes 3670040
  15.8 0.8 hold.2
  16.6 12.4 %collective-permute-done.4.refs_0_.refs_1_ = bf16[128,3712]{1,0:T(8,128)(2,1)S(1)} collective-permute-done((bf16[128,3712]{1,0:T(8,128)(2,1)S(1)}, bf16[128,3712]{1,0:T(8,128)(2,1)S(1)}, u32[]{:S(2)}, u32[]{:S(2)}) %collective-permute-start.4) | collective-permute-done | bytes 950304 | tf_op jit(solution)/shard_map/ppermute | solution.py:322
  29.0 0.7 collective-permute-start.10
  29.7 1.3 collective-permute-start.6
  31.0 1.8 pick.3
  32.9 1.7 collective-permute-start.7
  34.6 4.2 %hold.3 = (bf16[3584,512]{1,0:T(8,128)(2,1)S(1)}, bf16[3584,512]{1,0:T(8,128)(2,1)S(1)}, bf16[512,3584]{1,0:T(8,128)(2,1)S(1)}) custom-call(bf16[3584,512]{1,0:T(8,128)(2,1)} %collective-permute-done.refs_0_, bf16[3584,512]{1,0:T(8,128)(2,1)} %collective-permute-done.2.refs_1_, bf16[512,3584]{1,0:T(8,128)(2,1)} %collective-permute-done.3.refs_2_), custom_call_target="tpu_custom_call" | custom-call | flops 1 | bytes 1 | tf_op jit(solution)/shard_map/hold/pallas_call | solution.py:168
  38.9 1.1 copy-done.5
  39.9 5.7 %expert.4 = (bf16[128,3584]{1,0:T(8,128)(2,1)S(1)}, bf16[80,3584]{1,0:T(8,128)(2,1)S(1)}) custom-call(s32[3]{0:T(128)S(1)} %pad_add_fusion.sel_ref, bf16[128,3712]{1,0:T(8,128)(2,1)S(1)} %get-tuple-element.53.refs_0_, bf16[80,3584]{1,0:T(8,128)(2,1)S(1)} %copy-done.5, bf16[3584,512]{1,0:T(8,128)(2,1)S(1)} %get-tuple-element.59.refs_2_.refs_3_, ...), custom_call_target="tpu_custom_call" | custom-call | flops 1 | bytes 1 | tf_op jit(solution)/shard_map/expert/pallas_call | solution.py:220
  45.6 2.1 %collective-permute-done.7.refs_1_ = bf16[80,3584]{1,0:T(8,128)(2,1)S(1)} collective-permute-done((bf16[80,3584]{1,0:T(8,128)(2,1)S(1)}, bf16[80,3584]{1,0:T(8,128)(2,1)S(1)}, u32[]{:S(2)}, u32[]{:S(2)}) %collective-permute-start.7) | collective-permute-done | bytes 573472 | tf_op jit(solution)/shard_map/ppermute | solution.py:322
  47.7 5.7 %expert.5 = (bf16[128,3584]{1,0:T(8,128)(2,1)S(1)}, bf16[80,3584]{1,0:T(8,128)(2,1)S(1)}) custom-call(s32[3]{0:T(128)S(1)} %pad_add_fusion.sel_ref, bf16[128,3712]{1,0:T(8,128)(2,1)S(1)} %collective-permute-done.4.refs_0_.refs_1_, bf16[80,3584]{1,0:T(8,128)(2,1)S(1)} %collective-permute-done.7.refs_1_, ...), custom_call_target="tpu_custom_call" | custom-call | flops 1 | bytes 1 | tf_op jit(solution)/shard_map/expert/pallas_call | solution.py:220
  53.4 1.3 collective-permute-start.11
  54.7 1.5 collective-permute-start.8
  56.3 2.0 %pick.4 = (bf16[80,3584]{1,0:T(8,128)(2,1)S(1)}, bf16[128,80]{1,0:T(8,128)(2,1)S(1)}, f32[128,128]{1,0:T(8,128)S(1)}) custom-call(s32[3]{0:T(128)S(1)} %pad_add_fusion.sel_ref, bf16[128,3712]{1,0:T(8,128)(2,1)S(1)} %collective-permute-done.6.refs_0_.refs_2_, bf16[128,3712]{1,0:T(8,128)(2,1)S(1)} %collective-permute-done.5.refs_1_.refs_3_, ...), custom_call_target="tpu_custom_call" | custom-call | flops 1 | bytes 1 | tf_op jit(solution)/shard_map/pick/pallas_call | solution.py:132
  58.3 1.5 collective-permute-start.9
  59.8 10.9 %collective-permute-done.8.other_ref = bf16[80,3584]{1,0:T(8,128)(2,1)S(1)} collective-permute-done((bf16[80,3584]{1,0:T(8,128)(2,1)S(1)}, bf16[80,3584]{1,0:T(8,128)(2,1)S(1)}, u32[]{:S(2)}, u32[]{:S(2)}) %collective-permute-start.8) | collective-permute-done | bytes 573472 | tf_op jit(solution)/shard_map/ppermute | solution.py:322
  70.7 1.1 combine.5
  71.8 9.2 %collective-permute-done.9.refs_2_ = bf16[80,3584]{1,0:T(8,128)(2,1)S(1)} collective-permute-done((bf16[80,3584]{1,0:T(8,128)(2,1)S(1)}, bf16[80,3584]{1,0:T(8,128)(2,1)S(1)}, u32[]{:S(2)}, u32[]{:S(2)}) %collective-permute-start.9) | collective-permute-done | bytes 573472 | tf_op jit(solution)/shard_map/ppermute | solution.py:322
  81.0 5.9 %expert.6 = (bf16[128,3584]{1,0:T(8,128)(2,1)S(1)}, bf16[80,3584]{1,0:T(8,128)(2,1)S(1)}) custom-call(s32[3]{0:T(128)S(1)} %pad_add_fusion.sel_ref, bf16[128,3712]{1,0:T(8,128)(2,1)S(1)} %collective-permute-done.6.refs_0_.refs_2_, bf16[128,3712]{1,0:T(8,128)(2,1)S(1)} %collective-permute-done.5.refs_1_.refs_3_, ...), custom_call_target="tpu_custom_call" | custom-call | flops 1 | bytes 1 | tf_op jit(solution)/shard_map/expert/pallas_call | solution.py:220
  87.0 2.1 %pick.5 = (bf16[80,3584]{1,0:T(8,128)(2,1)S(1)}, bf16[128,80]{1,0:T(8,128)(2,1)S(1)}, f32[128,128]{1,0:T(8,128)S(1)}) custom-call(s32[3]{0:T(128)S(1)} %pad_add_fusion.sel_ref, bf16[128,3712]{1,0:T(8,128)(2,1)S(1)} %collective-permute-done.11.refs_0_.refs_2_, bf16[128,3712]{1,0:T(8,128)(2,1)S(1)} %collective-permute-done.10.refs_1_.refs_3_, ...), custom_call_target="tpu_custom_call" | custom-call | flops 1 | bytes 1 | tf_op jit(solution)/shard_map/pick/pallas_call | solution.py:132
  89.0 1.3 collective-permute-start.12
  90.3 5.9 %collective-permute-start.16 = (bf16[128,3584]{1,0:T(8,128)(2,1)S(1)}, bf16[128,3584]{1,0:T(8,128)(2,1)S(1)}, u32[]{:S(2)}, u32[]{:S(2)}) collective-permute-start(bf16[128,3584]{1,0:T(8,128)(2,1)S(1)} %combine.5), channel_id=1, source_target_pairs={{0,2},{1,3},{6,4},{7,5},{8,10},{9,11},{14,12},{15,13},{16,18},{17,... | collective-permute-start | bytes 2752520 | tf_op jit(solution)/shard_map/ppermute | solution.py:322
  96.2 5.9 %collective-permute-done.12.refs_2_ = bf16[80,3584]{1,0:T(8,128)(2,1)S(1)} collective-permute-done((bf16[80,3584]{1,0:T(8,128)(2,1)S(1)}, bf16[80,3584]{1,0:T(8,128)(2,1)S(1)}, u32[]{:S(2)}, u32[]{:S(2)}) %collective-permute-start.12) | collective-permute-done | bytes 573472 | tf_op jit(solution)/shard_map/ppermute | solution.py:322
  102.1 5.8 %expert.7 = (bf16[128,3584]{1,0:T(8,128)(2,1)S(1)}, bf16[80,1792]{1,0:T(8,128)(2,1)S(1)}, bf16[80,1792]{1,0:T(8,128)(2,1)S(1)}) custom-call(s32[3]{0:T(128)S(1)} %pad_add_fusion.sel_ref, bf16[128,3712]{1,0:T(8,128)(2,1)S(1)} %collective-permute-done.11.refs_0_.refs_2_, bf16[128,3712]{1,0:T(8,128)(2,1)S(1)} %collective-permute-done.10.refs_1_.refs_3_, ...), custom_call_target="tpu_custom_call" | custom-call | flops 1 | bytes 1 | tf_op jit(solution)/shard_map/expert/pallas_call | solution.py:220
  107.9 1.0 collective-permute-start.14
  108.9 1.1 collective-permute-start.13
  110.0 7.7 %collective-permute-done.14.other_ref = bf16[80,1792]{1,0:T(8,128)(2,1)S(1)} collective-permute-done((bf16[80,1792]{1,0:T(8,128)(2,1)S(1)}, bf16[80,1792]{1,0:T(8,128)(2,1)S(1)}, u32[]{:S(2)}, u32[]{:S(2)}) %collective-permute-start.14) | collective-permute-done | bytes 286752 | tf_op jit(solution)/shard_map/ppermute | solution.py:322
  117.7 0.6 combine.6
  118.3 5.0 %collective-permute-start.23 = (bf16[128,1792]{1,0:T(8,128)(2,1)S(1)}, bf16[128,1792]{1,0:T(8,128)(2,1)S(1)}, u32[]{:S(2)}, u32[]{:S(2)}) collective-permute-start(bf16[128,1792]{1,0:T(8,128)(2,1)S(1)} %combine.6), channel_id=1, source_target_pairs={{0,2},{1,3},{6,4},{7,5},{8,10},{9,11},{14,12},{15,13},{16,18},{17,... | collective-permute-start | bytes 1376264 | tf_op jit(solution)/shard_map/ppermute | solution.py:322
  123.3 1.6 collective-permute-start.19
  124.9 7.5 %collective-permute-done.19.other_ref = bf16[80,1792]{1,0:T(8,128)(2,1)S(1)} collective-permute-done((bf16[80,1792]{1,0:T(8,128)(2,1)S(1)}, bf16[80,1792]{1,0:T(8,128)(2,1)S(1)}, u32[]{:S(2)}, u32[]{:S(2)}) %collective-permute-start.19) | collective-permute-done | bytes 286752 | tf_op jit(solution)/shard_map/ppermute | solution.py:322
  132.4 0.6 combine.8
  132.9 4.4 %collective-permute-start.20 = (bf16[128,1792]{1,0:T(8,128)(2,1)S(1)}, bf16[128,1792]{1,0:T(8,128)(2,1)S(1)}, u32[]{:S(2)}, u32[]{:S(2)}) collective-permute-start(bf16[128,1792]{1,0:T(8,128)(2,1)S(1)} %combine.8), channel_id=1, source_target_pairs={{0,2},{1,3},{6,4},{7,5},{8,10},{9,11},{14,12},{15,13},{16,18},{17,... | collective-permute-start | bytes 1376264 | tf_op jit(solution)/shard_map/ppermute | solution.py:322
  137.4 1.1 combine.7
  138.5 1.3 collective-permute-start.17
  139.9 1.6 collective-permute-start.15
  141.5 0.1 add_convert_fusion.2
  141.6 0.7 collective-permute-start.24
  142.3 6.1 %collective-permute-done.20 = bf16[128,1792]{1,0:T(8,128)(2,1)S(1)} collective-permute-done((bf16[128,1792]{1,0:T(8,128)(2,1)S(1)}, bf16[128,1792]{1,0:T(8,128)(2,1)S(1)}, u32[]{:S(2)}, u32[]{:S(2)}) %collective-permute-start.20) | collective-permute-done | bytes 458784 | tf_op jit(solution)/shard_map/ppermute | solution.py:322
  148.3 0.1 add_convert_fusion.4
  148.4 0.7 collective-permute-start.21
  149.1 13.6 %collective-permute-done.17 = bf16[128,3584]{1,0:T(8,128)(2,1)S(1)} collective-permute-done((bf16[128,3584]{1,0:T(8,128)(2,1)S(1)}, bf16[128,3584]{1,0:T(8,128)(2,1)S(1)}, u32[]{:S(2)}, u32[]{:S(2)}) %collective-permute-start.17) | collective-permute-done | bytes 917536 | tf_op jit(solution)/shard_map/ppermute | solution.py:322
  162.7 0.2 add_convert_fusion
  162.9 0.7 collective-permute-start.18
  163.7 0.2 add_convert_fusion.1
  163.9 1.3 collective-permute-start.22
  165.2 1.3 collective-permute-start.25
  166.5 14.0 %collective-permute-done.22.refs_2_ = bf16[128,1792]{1,0:T(8,128)(2,1)S(1)} collective-permute-done((bf16[128,1792]{1,0:T(8,128)(2,1)S(1)}, bf16[128,1792]{1,0:T(8,128)(2,1)S(1)}, u32[]{:S(2)}, u32[]{:S(2)}) %collective-permute-start.22) | collective-permute-done | bytes 458784 | tf_op jit(solution)/shard_map/ppermute | solution.py:322
  180.6 4.9 %collective-permute-done.25.refs_3_ = bf16[128,1792]{1,0:T(8,128)(2,1)S(1)} collective-permute-done((bf16[128,1792]{1,0:T(8,128)(2,1)S(1)}, bf16[128,1792]{1,0:T(8,128)(2,1)S(1)}, u32[]{:S(2)}, u32[]{:S(2)}) %collective-permute-start.25) | collective-permute-done | bytes 458784 | tf_op jit(solution)/shard_map/ppermute | solution.py:322
  185.5 2.7 %combine.9 = bf16[128,3584]{1,0:T(8,128)(2,1)} custom-call(bf16[128,80]{1,0:T(8,128)(2,1)S(1)} %get-tuple-element.51.back_ref, f32[128,128]{1,0:T(8,128)S(1)} %get-tuple-element.52.weight_ref, bf16[128,3584]{1,0:T(8,128)(2,1)S(1)} %get-tuple-element.70.own_ref, bf16[80,3584]{1,0:T(8,128)(2,1)S(1)} %collective-permute-done.15.other_ref, ...), custom_call_target="tpu_custom_call" | custom-call | flops 1 | bytes 1 | tf_op jit(solution)/shard_map/combine/pallas_call | solution.py:266
  (24 shorter events, 0.1 us)
Async XLA Ops:
  0.0 8.0 %collective-permute-start = (bf16[3584,512]{1,0:T(8,128)(2,1)}, bf16[3584,512]{1,0:T(8,128)(2,1)}, u32[]{:S(2)}, u32[]{:S(2)}) collective-permute-start(bf16[3584,512]{1,0:T(8,128)(2,1)} %bitcast.8), channel_id=1, source_target_pairs={{0,8},{8,0},{1,9},{9,1},{2,10},{10,2},{3,11},{11,3},{4,12},{12,4},... | collective-permute-start | bytes 11010056 | tf_op jit(solution)/shard_map/ppermute | solution.py:325
  0.5 34.2 %collective-permute-start.2 = (bf16[3584,512]{1,0:T(8,128)(2,1)}, bf16[3584,512]{1,0:T(8,128)(2,1)}, u32[]{:S(2)}, u32[]{:S(2)}) collective-permute-start(bf16[3584,512]{1,0:T(8,128)(2,1)} %bitcast.10), channel_id=1, source_target_pairs={{0,8},{8,0},{1,9},{9,1},{2,10},{10,2},{3,11},{11,3},{4,12},{12,4},... | collective-permute-start | bytes 11010056 | tf_op jit(solution)/shard_map/ppermute | solution.py:325
  0.5 34.1 %collective-permute-start.3 = (bf16[512,3584]{1,0:T(8,128)(2,1)}, bf16[512,3584]{1,0:T(8,128)(2,1)}, u32[]{:S(2)}, u32[]{:S(2)}) collective-permute-start(bf16[512,3584]{1,0:T(8,128)(2,1)} %bitcast.12), channel_id=1, source_target_pairs={{0,8},{8,0},{1,9},{9,1},{2,10},{10,2},{3,11},{11,3},{4,12},{12,4},... | collective-permute-start | bytes 11010056 | tf_op jit(solution)/shard_map/ppermute | solution.py:325
  1.0 1.2 copy-start.3
  2.2 0.7 copy-start.6
  2.9 0.7 copy-start.7
  4.6 24.4 %collective-permute-start.4 = (bf16[128,3712]{1,0:T(8,128)(2,1)S(1)}, bf16[128,3712]{1,0:T(8,128)(2,1)S(1)}, u32[]{:S(2)}, u32[]{:S(2)}) collective-permute-start(bf16[128,3712]{1,0:T(8,128)(2,1)S(1)} %get-tuple-element.53.refs_0_), channel_id=1, source_target_pairs={{0,2},{1,3},{2,0},{3,1},{4,6},{5,7},{6,4},{7,5},{8,10},{9,11},{10,... | collective-permute-start | bytes 2850824 | tf_op jit(solution)/shard_map/ppermute | solution.py:322
  7.3 22.4 %collective-permute-start.5 = (bf16[128,3712]{1,0:T(8,128)(2,1)S(1)}, bf16[128,3712]{1,0:T(8,128)(2,1)S(1)}, u32[]{:S(2)}, u32[]{:S(2)}) collective-permute-start(bf16[128,3712]{1,0:T(8,128)(2,1)S(1)} %get-tuple-element.53.refs_0_), channel_id=1, source_target_pairs={{2,4},{3,5},{4,2},{5,3},{10,12},{11,13},{12,10},{13,11},{18,20},{1... | collective-permute-start | bytes 2850824 | tf_op jit(solution)/shard_map/ppermute | solution.py:322
  8.0 21.0 %collective-permute-start.1 = (bf16[80,3584]{1,0:T(8,128)(2,1)S(1)}, bf16[80,3584]{1,0:T(8,128)(2,1)S(1)}, u32[]{:S(2)}, u32[]{:S(2)}) collective-permute-start(bf16[80,3584]{1,0:T(8,128)(2,1)S(1)} %get-tuple-element.55), channel_id=1, source_target_pairs={{0,1},{1,0},{2,3},{3,2},{4,5},{5,4},{6,7},{7,6},{8,9},{9,8},{10,11... | collective-permute-start | bytes 1720328 | tf_op jit(solution)/shard_map/ppermute | solution.py:322
  9.7 2.0 %copy-start = (bf16[1,3584,512]{2,1,0:T(8,128)(2,1)S(1)}, bf16[1,3584,512]{2,1,0:T(8,128)(2,1)}, u32[]{:S(2)}) copy-start(bf16[1,3584,512]{2,1,0:T(8,128)(2,1)} %param.9) | copy-start | bytes 11010052
  11.8 2.0 %copy-start.1 = (bf16[1,3584,512]{2,1,0:T(8,128)(2,1)S(1)}, bf16[1,3584,512]{2,1,0:T(8,128)(2,1)}, u32[]{:S(2)}) copy-start(bf16[1,3584,512]{2,1,0:T(8,128)(2,1)} %param.10) | copy-start | bytes 11010052
  13.8 2.0 %copy-start.2 = (bf16[1,512,3584]{2,1,0:T(8,128)(2,1)S(1)}, bf16[1,512,3584]{2,1,0:T(8,128)(2,1)}, u32[]{:S(2)}) copy-start(bf16[1,512,3584]{2,1,0:T(8,128)(2,1)} %param.11) | copy-start | bytes 11010052
  29.0 9.8 %copy-start.4 = (bf16[80,3584]{1,0:T(8,128)(2,1)}, bf16[80,3584]{1,0:T(8,128)(2,1)S(1)}, u32[]{:S(2)}) copy-start(bf16[80,3584]{1,0:T(8,128)(2,1)S(1)} %collective-permute-done.1.refs_1_) | copy-start | bytes 1720324
  29.0 24.4 %collective-permute-start.10 = (bf16[128,3712]{1,0:T(8,128)(2,1)S(1)}, bf16[128,3712]{1,0:T(8,128)(2,1)S(1)}, u32[]{:S(2)}, u32[]{:S(2)}) collective-permute-start(bf16[128,3712]{1,0:T(8,128)(2,1)S(1)} %collective-permute-done.4.refs_0_.refs_1_), channel_id=1, source_target_pairs={{2,4},{3,5},{4,2},{5,3},{10,12},{11,13},{12,10},{13,11},{18,20},{1... | collective-permute-start | bytes 2850824 | tf_op jit(solution)/shard_map/ppermute | solution.py:322
  29.7 26.5 %collective-permute-start.6 = (bf16[128,3712]{1,0:T(8,128)(2,1)S(1)}, bf16[128,3712]{1,0:T(8,128)(2,1)S(1)}, u32[]{:S(2)}, u32[]{:S(2)}) collective-permute-start(bf16[128,3712]{1,0:T(8,128)(2,1)S(1)} %collective-permute-done.5.refs_1_.refs_3_), channel_id=1, source_target_pairs={{2,0},{3,1},{4,6},{5,7},{10,8},{11,9},{12,14},{13,15},{18,16},{19,... | collective-permute-start | bytes 2850824 | tf_op jit(solution)/shard_map/ppermute | solution.py:322
  32.9 14.9 %collective-permute-start.7 = (bf16[80,3584]{1,0:T(8,128)(2,1)S(1)}, bf16[80,3584]{1,0:T(8,128)(2,1)S(1)}, u32[]{:S(2)}, u32[]{:S(2)}) collective-permute-start(bf16[80,3584]{1,0:T(8,128)(2,1)S(1)} %get-tuple-element.61), channel_id=1, source_target_pairs={{0,1},{1,0},{2,3},{3,2},{4,5},{5,4},{6,7},{7,6},{8,9},{9,8},{10,11... | collective-permute-start | bytes 1720328 | tf_op jit(solution)/shard_map/ppermute | solution.py:322
  38.9 1.1 copy-start.5
  53.4 33.6 %collective-permute-start.11 = (bf16[128,3712]{1,0:T(8,128)(2,1)S(1)}, bf16[128,3712]{1,0:T(8,128)(2,1)S(1)}, u32[]{:S(2)}, u32[]{:S(2)}) collective-permute-start(bf16[128,3712]{1,0:T(8,128)(2,1)S(1)} %collective-permute-done.10.refs_1_.refs_3_), channel_id=1, source_target_pairs={{2,0},{3,1},{4,6},{5,7},{10,8},{11,9},{12,14},{13,15},{18,16},{19,... | collective-permute-start | bytes 2850824 | tf_op jit(solution)/shard_map/ppermute | solution.py:322
  54.7 16.0 %collective-permute-start.8 = (bf16[80,3584]{1,0:T(8,128)(2,1)S(1)}, bf16[80,3584]{1,0:T(8,128)(2,1)S(1)}, u32[]{:S(2)}, u32[]{:S(2)}) collective-permute-start(bf16[80,3584]{1,0:T(8,128)(2,1)S(1)} %get-tuple-element.79), channel_id=1, source_target_pairs={{0,1},{1,0},{2,3},{3,2},{4,5},{5,4},{6,7},{7,6},{8,9},{9,8},{10,11... | collective-permute-start | bytes 1720328 | tf_op jit(solution)/shard_map/ppermute | solution.py:322
  58.3 22.8 %collective-permute-start.9 = (bf16[80,3584]{1,0:T(8,128)(2,1)S(1)}, bf16[80,3584]{1,0:T(8,128)(2,1)S(1)}, u32[]{:S(2)}, u32[]{:S(2)}) collective-permute-start(bf16[80,3584]{1,0:T(8,128)(2,1)S(1)} %get-tuple-element.80), channel_id=1, source_target_pairs={{0,1},{1,0},{2,3},{3,2},{4,5},{5,4},{6,7},{7,6},{8,9},{9,8},{10,11... | collective-permute-start | bytes 1720328 | tf_op jit(solution)/shard_map/ppermute | solution.py:322
  89.0 13.1 %collective-permute-start.12 = (bf16[80,3584]{1,0:T(8,128)(2,1)S(1)}, bf16[80,3584]{1,0:T(8,128)(2,1)S(1)}, u32[]{:S(2)}, u32[]{:S(2)}) collective-permute-start(bf16[80,3584]{1,0:T(8,128)(2,1)S(1)} %get-tuple-element.87), channel_id=1, source_target_pairs={{0,1},{1,0},{2,3},{3,2},{4,5},{5,4},{6,7},{7,6},{8,9},{9,8},{10,11... | collective-permute-start | bytes 1720328 | tf_op jit(solution)/shard_map/ppermute | solution.py:322
  90.3 34.6 %collective-permute-start.16 = (bf16[128,3584]{1,0:T(8,128)(2,1)S(1)}, bf16[128,3584]{1,0:T(8,128)(2,1)S(1)}, u32[]{:S(2)}, u32[]{:S(2)}) collective-permute-start(bf16[128,3584]{1,0:T(8,128)(2,1)S(1)} %combine.5), channel_id=1, source_target_pairs={{0,2},{1,3},{6,4},{7,5},{8,10},{9,11},{14,12},{15,13},{16,18},{17,... | collective-permute-start | bytes 2752520 | tf_op jit(solution)/shard_map/ppermute | solution.py:322
  107.9 9.8 %collective-permute-start.14 = (bf16[80,1792]{1,0:T(8,128)(2,1)S(1)}, bf16[80,1792]{1,0:T(8,128)(2,1)S(1)}, u32[]{:S(2)}, u32[]{:S(2)}) collective-permute-start(bf16[80,1792]{1,0:T(8,128)(2,1)S(1)} %get-tuple-element.92), channel_id=1, source_target_pairs={{0,1},{1,0},{2,3},{3,2},{4,5},{5,4},{6,7},{7,6},{8,9},{9,8},{10,11... | collective-permute-start | bytes 860168 | tf_op jit(solution)/shard_map/ppermute | solution.py:322
  108.9 28.5 %collective-permute-start.13 = (bf16[80,3584]{1,0:T(8,128)(2,1)S(1)}, bf16[80,3584]{1,0:T(8,128)(2,1)S(1)}, u32[]{:S(2)}, u32[]{:S(2)}) collective-permute-start(bf16[80,3584]{1,0:T(8,128)(2,1)S(1)} %get-tuple-element.88), channel_id=1, source_target_pairs={{0,1},{1,0},{2,3},{3,2},{4,5},{5,4},{6,7},{7,6},{8,9},{9,8},{10,11... | collective-permute-start | bytes 1720328 | tf_op jit(solution)/shard_map/ppermute | solution.py:322
  118.3 23.1 %collective-permute-start.23 = (bf16[128,1792]{1,0:T(8,128)(2,1)S(1)}, bf16[128,1792]{1,0:T(8,128)(2,1)S(1)}, u32[]{:S(2)}, u32[]{:S(2)}) collective-permute-start(bf16[128,1792]{1,0:T(8,128)(2,1)S(1)} %combine.6), channel_id=1, source_target_pairs={{0,2},{1,3},{6,4},{7,5},{8,10},{9,11},{14,12},{15,13},{16,18},{17,... | collective-permute-start | bytes 1376264 | tf_op jit(solution)/shard_map/ppermute | solution.py:322
  123.3 9.1 %collective-permute-start.19 = (bf16[80,1792]{1,0:T(8,128)(2,1)S(1)}, bf16[80,1792]{1,0:T(8,128)(2,1)S(1)}, u32[]{:S(2)}, u32[]{:S(2)}) collective-permute-start(bf16[80,1792]{1,0:T(8,128)(2,1)S(1)} %get-tuple-element.95), channel_id=1, source_target_pairs={{0,1},{1,0},{2,3},{3,2},{4,5},{5,4},{6,7},{7,6},{8,9},{9,8},{10,11... | collective-permute-start | bytes 860168 | tf_op jit(solution)/shard_map/ppermute | solution.py:322
  132.9 15.4 %collective-permute-start.20 = (bf16[128,1792]{1,0:T(8,128)(2,1)S(1)}, bf16[128,1792]{1,0:T(8,128)(2,1)S(1)}, u32[]{:S(2)}, u32[]{:S(2)}) collective-permute-start(bf16[128,1792]{1,0:T(8,128)(2,1)S(1)} %combine.8), channel_id=1, source_target_pairs={{0,2},{1,3},{6,4},{7,5},{8,10},{9,11},{14,12},{15,13},{16,18},{17,... | collective-permute-start | bytes 1376264 | tf_op jit(solution)/shard_map/ppermute | solution.py:322
  138.5 24.2 %collective-permute-start.17 = (bf16[128,3584]{1,0:T(8,128)(2,1)S(1)}, bf16[128,3584]{1,0:T(8,128)(2,1)S(1)}, u32[]{:S(2)}, u32[]{:S(2)}) collective-permute-start(bf16[128,3584]{1,0:T(8,128)(2,1)S(1)} %combine.7), channel_id=1, source_target_pairs={{0,2},{1,3},{6,4},{7,5},{8,10},{9,11},{14,12},{15,13},{16,18},{17,... | collective-permute-start | bytes 2752520 | tf_op jit(solution)/shard_map/ppermute | solution.py:322
  139.9 26.6 %collective-permute-start.15 = (bf16[80,3584]{1,0:T(8,128)(2,1)S(1)}, bf16[80,3584]{1,0:T(8,128)(2,1)S(1)}, u32[]{:S(2)}, u32[]{:S(2)}) collective-permute-start(bf16[80,3584]{1,0:T(8,128)(2,1)S(1)} %get-tuple-element.94), channel_id=1, source_target_pairs={{0,1},{1,0},{2,3},{3,2},{4,5},{5,4},{6,7},{7,6},{8,9},{9,8},{10,11... | collective-permute-start | bytes 1720328 | tf_op jit(solution)/shard_map/ppermute | solution.py:322
  141.6 22.1 %collective-permute-start.24 = (bf16[128,1792]{1,0:T(8,128)(2,1)S(1)}, bf16[128,1792]{1,0:T(8,128)(2,1)S(1)}, u32[]{:S(2)}, u32[]{:S(2)}) collective-permute-start(bf16[128,1792]{1,0:T(8,128)(2,1)S(1)} %add_convert_fusion.2), channel_id=1, source_target_pairs={{2,4},{3,5},{4,2},{5,3},{10,12},{11,13},{12,10},{13,11},{18,20},{1... | collective-permute-start | bytes 1376264 | tf_op jit(solution)/shard_map/ppermute | solution.py:322
  148.4 15.2 %collective-permute-start.21 = (bf16[128,1792]{1,0:T(8,128)(2,1)S(1)}, bf16[128,1792]{1,0:T(8,128)(2,1)S(1)}, u32[]{:S(2)}, u32[]{:S(2)}) collective-permute-start(bf16[128,1792]{1,0:T(8,128)(2,1)S(1)} %add_convert_fusion.4), channel_id=1, source_target_pairs={{2,4},{3,5},{4,2},{5,3},{10,12},{11,13},{12,10},{13,11},{18,20},{1... | collective-permute-start | bytes 1376264 | tf_op jit(solution)/shard_map/ppermute | solution.py:322
  162.9 22.5 %collective-permute-start.18 = (bf16[128,3584]{1,0:T(8,128)(2,1)S(1)}, bf16[128,3584]{1,0:T(8,128)(2,1)S(1)}, u32[]{:S(2)}, u32[]{:S(2)}) collective-permute-start(bf16[128,3584]{1,0:T(8,128)(2,1)S(1)} %add_convert_fusion), channel_id=1, source_target_pairs={{2,4},{3,5},{4,2},{5,3},{10,12},{11,13},{12,10},{13,11},{18,20},{1... | collective-permute-start | bytes 2752520 | tf_op jit(solution)/shard_map/ppermute | solution.py:322
  163.9 16.7 %collective-permute-start.22 = (bf16[128,1792]{1,0:T(8,128)(2,1)S(1)}, bf16[128,1792]{1,0:T(8,128)(2,1)S(1)}, u32[]{:S(2)}, u32[]{:S(2)}) collective-permute-start(bf16[128,1792]{1,0:T(8,128)(2,1)S(1)} %get-tuple-element.98), channel_id=1, source_target_pairs={{2,0},{3,1},{4,6},{5,7},{10,8},{11,9},{12,14},{13,15},{18,16},{19,... | collective-permute-start | bytes 1376264 | tf_op jit(solution)/shard_map/ppermute | solution.py:322
  165.2 20.3 %collective-permute-start.25 = (bf16[128,1792]{1,0:T(8,128)(2,1)S(1)}, bf16[128,1792]{1,0:T(8,128)(2,1)S(1)}, u32[]{:S(2)}, u32[]{:S(2)}) collective-permute-start(bf16[128,1792]{1,0:T(8,128)(2,1)S(1)} %get-tuple-element.97), channel_id=1, source_target_pairs={{2,0},{3,1},{4,6},{5,7},{10,8},{11,9},{12,14},{13,15},{18,16},{19,... | collective-permute-start | bytes 1376264 | tf_op jit(solution)/shard_map/ppermute | solution.py:322

commit v3 on v2

--- a/solution.py
+++ b/solution.py
@@ -348,27 +348,37 @@
     y2 = send(s2, across)
     q1 = combine(tables1, o1, after(b1, s2))
     r1 = send(q1, FROM_ENDS)
-    o2, oy2 = expert(sel, [after(far[0], q1), inner], y2, gates, ups, downs, 1)
-    last = [after(last_end, o2), far_inner]
+    last = [after(last_end, y2, q1), far_inner]
     s3, *tables3 = pick_rows(sel, last, experts, cap)
     y3 = send(s3, across)
-    b2 = send(after(oy2, y3), across)
-    o3, *oy3 = expert(sel, last, y3, gates, ups, downs, HALVES)
+    o2, *oy2 = expert(sel, far, after(y2, s3), gates, ups, downs, HALVES)
+    b2 = [send(after(v, y3), across) for v in oy2]
+    o3, *oy3 = expert(sel, last, after(y3, o2, r1), gates, ups, downs, HALVES)
     b3 = [send(v, across) for v in oy3]
 
     part = width // HALVES
-    b3[0] = after(b3[0], r1)
-    q3 = [combine(tables3, o3, v, first=h * part) for h, v in enumerate(b3)]
-    r3 = [send(v, FROM_ENDS) for v in q3]
-    q2 = combine(tables2, o2, after(b2, q3[-1]))
-    b0 = send(after(oy0, q2), across)
-    r2 = send(q2, FROM_ENDS)
-    r3 = [send(add(q, r), INNER) for q, r in zip(q3, r3)]
-    r2 = send(add(q2, r2), INNER)
-    r3 = [
-        send(add(q1[:, h * part : (h + 1) * part], r), TO_ENDS) for h, r in enumerate(r3)
-    ]
-    return combine(tables0, o0, b0, extra=([r1], [r2], r3), scale=SCALE)
+    q20 = combine(tables2, o2, after(b2[0], o3), first=0)
+    r20 = send(q20, FROM_ENDS)
+    q30 = combine(tables3, o3, after(b3[0], q20), first=0)
+    r30 = send(q30, FROM_ENDS)
+    p20 = add(q20, after(r20, q30))
+    r20 = send(p20, INNER)
+    q31 = combine(tables3, o3, after(b3[1], p20), first=part)
+    r31 = send(q31, FROM_ENDS)
+    q21 = combine(tables2, o2, after(b2[1], q31), first=part)
+    r21 = send(q21, FROM_ENDS)
+    b0 = send(after(oy0, q21), across)
+    p30 = add(q30, after(r30, q21))
+    r30 = send(p30, INNER)
+    p31 = add(q31, after(r31, p30))
+    r31 = send(p31, INNER)
+    e0 = add(q1[:, :part], after(r30, p31))
+    r30 = send(e0, TO_ENDS)
+    p21 = add(q21, after(r21, e0))
+    r21 = send(p21, INNER)
+    e1 = add(q1[:, part:], after(r31, p21))
+    r31 = send(e1, TO_ENDS)
+    return combine(tables0, o0, b0, extra=([r1], [r20, r21], [r30, r31]), scale=SCALE)
 
 
 def all_to_all_form(tokens, scores, expert_ids, w_gate, w_up, w_down):

time: 189 us -> 166 us (0.88)
  waiting for transfers between devices: 94.5 us -> 70.5 us
    ppermute x23 -> x26, waiting for transfers between devices: 94.5 us -> 70.5 us  [send(): return lax.ppermute(value, 'expert', pairs)]
    ppermute x23 -> x26, starting transfers between devices: 41 us -> 41.9 us  [send(): return lax.ppermute(value, 'expert', pairs)]
    pallas_call x5 -> x6, Pallas kernels: 6.01 us -> 6.13 us  [combine(): pl.pallas_call(functools.partial(combine_kernel, scale, [len(e) for e in...]
  transfers between devices with their start and end apart: 26 -> 29, of which waited for: 11 -> 12; matrix products, arithmetic and copies ran while one was open for 0% -> 0% of each run, Pallas kernels for 19% -> 23%
where the time goes in v3:
time: 166 us; the launch traced here: 165 us
  waiting for transfers between devices  70.5 us (42%)
  starting transfers between devices  42.8 us (26%)
  Pallas kernels  41 us (25%)
  local copies, waits for them, and re-layouts  9.71 us (6%)
    ppermute x26, waiting for transfers between devices, send(): return lax.ppermute(value, 'expert', pairs)  70.5 us
    ppermute x26, starting transfers between devices, send(): return lax.ppermute(value, 'expert', pairs)  41.9 us
    pallas_call x4, Pallas kernels, expert(): pl.pallas_call(functools.partial(expert_kernel, len(parts), halves), in_s...  23 us
    unnamed x16, local copies, waits for them, and re-layouts  9.71 us
    pallas_call x6, Pallas kernels, combine(): pl.pallas_call(functools.partial(combine_kernel, scale, [len(e) for e in...  6.13 us
    pallas_call x3, Pallas kernels, pick_rows(): pl.pallas_call(functools.partial(pick_kernel, experts, len(parts)), grid=...  5.83 us
    pallas_call x2, Pallas kernels, hold(): pl.pallas_call(hold_kernel, in_specs=[pl.BlockSpec(memory_space=pltpu.HBM...  4.99 us
  transfers between devices with their start and end apart: 29, of which 12 were waited for; matrix products, arithmetic and copies ran while one was open for 0% of the time, Pallas kernels for 23%

profile of v3, /device:TPU:0, one launch (start us, length us, event | category | flops | bytes accessed | tf_op | source)
XLA Modules:
  0.0 165.2 jit_solution(10759961515040485882)
XLA Ops:
  0.0 0.5 collective-permute-start
  0.5 0.5 collective-permute-start.3
  1.0 1.2 copy-done.3
  2.2 0.7 copy-done.6
  2.9 0.7 copy-done.7
  3.6 1.0 open.1
  4.6 2.6 %collective-permute-start.4 = (bf16[128,3712]{1,0:T(8,128)(2,1)S(1)}, bf16[128,3712]{1,0:T(8,128)(2,1)S(1)}, u32[]{:S(2)}, u32[]{:S(2)}) collective-permute-start(bf16[128,3712]{1,0:T(8,128)(2,1)S(1)} %get-tuple-element.64.refs_0_), channel_id=1, source_target_pairs={{0,2},{1,3},{2,0},{3,1},{4,6},{5,7},{6,4},{7,5},{8,10},{9,11},{10,... | collective-permute-start | bytes 2850824 | tf_op jit(solution)/shard_map/ppermute | solution.py:322
  7.3 2.4 %collective-permute-start.1 = (bf16[80,3584]{1,0:T(8,128)(2,1)S(1)}, bf16[80,3584]{1,0:T(8,128)(2,1)S(1)}, u32[]{:S(2)}, u32[]{:S(2)}) collective-permute-start(bf16[80,3584]{1,0:T(8,128)(2,1)S(1)} %get-tuple-element.66), channel_id=1, source_target_pairs={{0,1},{1,0},{2,3},{3,2},{4,5},{5,4},{6,7},{7,6},{8,9},{9,8},{10,11... | collective-permute-start | bytes 1720328 | tf_op jit(solution)/shard_map/ppermute | solution.py:322
  9.7 0.7 collective-permute-start.5
  10.4 2.0 %copy-done = bf16[1,3584,512]{2,1,0:T(8,128)(2,1)S(1)} copy-done((bf16[1,3584,512]{2,1,0:T(8,128)(2,1)S(1)}, bf16[1,3584,512]{2,1,0:T(8,128)(2,1)}, u32[]{:S(2)}) %copy-start) | copy-done | bytes 3670040
  12.5 2.0 %copy-done.1 = bf16[1,3584,512]{2,1,0:T(8,128)(2,1)S(1)} copy-done((bf16[1,3584,512]{2,1,0:T(8,128)(2,1)S(1)}, bf16[1,3584,512]{2,1,0:T(8,128)(2,1)}, u32[]{:S(2)}) %copy-start.1) | copy-done | bytes 3670040
  14.5 2.0 %copy-done.2 = bf16[1,512,3584]{2,1,0:T(8,128)(2,1)S(1)} copy-done((bf16[1,512,3584]{2,1,0:T(8,128)(2,1)S(1)}, bf16[1,512,3584]{2,1,0:T(8,128)(2,1)}, u32[]{:S(2)}) %copy-start.2) | copy-done | bytes 3670040
  16.6 0.8 hold.2
  17.3 11.7 %collective-permute-done.4.refs_0_.refs_1_ = bf16[128,3712]{1,0:T(8,128)(2,1)S(1)} collective-permute-done((bf16[128,3712]{1,0:T(8,128)(2,1)S(1)}, bf16[128,3712]{1,0:T(8,128)(2,1)S(1)}, u32[]{:S(2)}, u32[]{:S(2)}) %collective-permute-start.4) | collective-permute-done | bytes 950304 | tf_op jit(solution)/shard_map/ppermute | solution.py:322
  29.0 0.7 collective-permute-start.9
  29.7 1.8 %pick.3 = (bf16[80,3584]{1,0:T(8,128)(2,1)S(1)}, bf16[128,80]{1,0:T(8,128)(2,1)S(1)}, f32[128,128]{1,0:T(8,128)S(1)}) custom-call(s32[3]{0:T(128)S(1)} %pad_add_fusion.sel_ref, bf16[128,3712]{1,0:T(8,128)(2,1)S(1)} %collective-permute-done.4.refs_0_.refs_1_, bf16[128,3712]{1,0:T(8,128)(2,1)S(1)} %collective-permute-done.4.refs_0_.refs_1_), custom_call_target="tpu_custom_call" | custom-call | flops 1 | bytes 1 | tf_op jit(solution)/shard_map/pick/pallas_call | solution.py:132
  31.5 1.7 %collective-permute-start.7 = (bf16[80,3584]{1,0:T(8,128)(2,1)S(1)}, bf16[80,3584]{1,0:T(8,128)(2,1)S(1)}, u32[]{:S(2)}, u32[]{:S(2)}) collective-permute-start(bf16[80,3584]{1,0:T(8,128)(2,1)S(1)} %get-tuple-element.72), channel_id=1, source_target_pairs={{0,1},{1,0},{2,3},{3,2},{4,5},{5,4},{6,7},{7,6},{8,9},{9,8},{10,11... | collective-permute-start | bytes 1720328 | tf_op jit(solution)/shard_map/ppermute | solution.py:322
  33.3 1.3 collective-permute-start.6
  34.6 4.2 %hold.3 = (bf16[3584,512]{1,0:T(8,128)(2,1)S(1)}, bf16[3584,512]{1,0:T(8,128)(2,1)S(1)}, bf16[512,3584]{1,0:T(8,128)(2,1)S(1)}) custom-call(bf16[3584,512]{1,0:T(8,128)(2,1)} %collective-permute-done.refs_0_, bf16[3584,512]{1,0:T(8,128)(2,1)} %collective-permute-done.2.refs_1_, bf16[512,3584]{1,0:T(8,128)(2,1)} %collective-permute-done.3.refs_2_), custom_call_target="tpu_custom_call" | custom-call | flops 1 | bytes 1 | tf_op jit(solution)/shard_map/hold/pallas_call | solution.py:168
  38.9 1.1 copy-done.5
  39.9 5.7 %expert.4 = (bf16[128,3584]{1,0:T(8,128)(2,1)S(1)}, bf16[80,3584]{1,0:T(8,128)(2,1)S(1)}) custom-call(s32[3]{0:T(128)S(1)} %pad_add_fusion.sel_ref, bf16[128,3712]{1,0:T(8,128)(2,1)S(1)} %get-tuple-element.64.refs_0_, bf16[80,3584]{1,0:T(8,128)(2,1)S(1)} %copy-done.5, bf16[3584,512]{1,0:T(8,128)(2,1)S(1)} %get-tuple-element.70.refs_2_.refs_3_, ...), custom_call_target="tpu_custom_call" | custom-call | flops 1 | bytes 1 | tf_op jit(solution)/shard_map/expert/pallas_call | solution.py:220
  45.6 0.8 collective-permute-done.7.refs_1_
  46.4 5.7 %expert.5 = (bf16[128,3584]{1,0:T(8,128)(2,1)S(1)}, bf16[80,3584]{1,0:T(8,128)(2,1)S(1)}) custom-call(s32[3]{0:T(128)S(1)} %pad_add_fusion.sel_ref, bf16[128,3712]{1,0:T(8,128)(2,1)S(1)} %collective-permute-done.4.refs_0_.refs_1_, bf16[80,3584]{1,0:T(8,128)(2,1)S(1)} %collective-permute-done.7.refs_1_, ...), custom_call_target="tpu_custom_call" | custom-call | flops 1 | bytes 1 | tf_op jit(solution)/shard_map/expert/pallas_call | solution.py:220
  52.1 1.3 collective-permute-start.10
  53.4 1.5 collective-permute-start.11
  54.9 5.9 %collective-permute-done.6.refs_0_.refs_2_ = bf16[128,3712]{1,0:T(8,128)(2,1)S(1)} collective-permute-done((bf16[128,3712]{1,0:T(8,128)(2,1)S(1)}, bf16[128,3712]{1,0:T(8,128)(2,1)S(1)}, u32[]{:S(2)}, u32[]{:S(2)}) %collective-permute-start.6) | collective-permute-done | bytes 950304 | tf_op jit(solution)/shard_map/ppermute | solution.py:322
  60.9 2.0 %pick.4 = (bf16[80,3584]{1,0:T(8,128)(2,1)S(1)}, bf16[128,80]{1,0:T(8,128)(2,1)S(1)}, f32[128,128]{1,0:T(8,128)S(1)}) custom-call(s32[3]{0:T(128)S(1)} %pad_add_fusion.sel_ref, bf16[128,3712]{1,0:T(8,128)(2,1)S(1)} %collective-permute-done.6.refs_0_.refs_2_, bf16[128,3712]{1,0:T(8,128)(2,1)S(1)} %collective-permute-done.5.refs_1_.refs_3_, ...), custom_call_target="tpu_custom_call" | custom-call | flops 1 | bytes 1 | tf_op jit(solution)/shard_map/pick/pallas_call | solution.py:132
  62.9 0.4 collective-permute-start.8
  63.3 6.1 %collective-permute-done.11.other_ref = bf16[80,3584]{1,0:T(8,128)(2,1)S(1)} collective-permute-done((bf16[80,3584]{1,0:T(8,128)(2,1)S(1)}, bf16[80,3584]{1,0:T(8,128)(2,1)S(1)}, u32[]{:S(2)}, u32[]{:S(2)}) %collective-permute-start.11) | collective-permute-done | bytes 573472 | tf_op jit(solution)/shard_map/ppermute | solution.py:322
  69.4 1.1 combine.6
  70.5 6.2 %collective-permute-start.14 = (bf16[128,3584]{1,0:T(8,128)(2,1)S(1)}, bf16[128,3584]{1,0:T(8,128)(2,1)S(1)}, u32[]{:S(2)}, u32[]{:S(2)}) collective-permute-start(bf16[128,3584]{1,0:T(8,128)(2,1)S(1)} %combine.6), channel_id=1, source_target_pairs={{0,2},{1,3},{6,4},{7,5},{8,10},{9,11},{14,12},{15,13},{16,18},{17,... | collective-permute-start | bytes 2752520 | tf_op jit(solution)/shard_map/ppermute | solution.py:322
  76.8 3.0 %collective-permute-done.8.refs_2_ = bf16[80,3584]{1,0:T(8,128)(2,1)S(1)} collective-permute-done((bf16[80,3584]{1,0:T(8,128)(2,1)S(1)}, bf16[80,3584]{1,0:T(8,128)(2,1)S(1)}, u32[]{:S(2)}, u32[]{:S(2)}) %collective-permute-start.8) | collective-permute-done | bytes 573472 | tf_op jit(solution)/shard_map/ppermute | solution.py:322
  79.7 2.0 %pick.5 = (bf16[80,3584]{1,0:T(8,128)(2,1)S(1)}, bf16[128,80]{1,0:T(8,128)(2,1)S(1)}, f32[128,128]{1,0:T(8,128)S(1)}) custom-call(s32[3]{0:T(128)S(1)} %pad_add_fusion.sel_ref, bf16[128,3712]{1,0:T(8,128)(2,1)S(1)} %collective-permute-done.10.refs_0_.refs_2_, bf16[128,3712]{1,0:T(8,128)(2,1)S(1)} %collective-permute-done.9.refs_1_.refs_3_, ...), custom_call_target="tpu_custom_call" | custom-call | flops 1 | bytes 1 | tf_op jit(solution)/shard_map/pick/pallas_call | solution.py:132
  81.7 1.3 collective-permute-start.12
  83.0 5.9 %expert.6 = (bf16[128,3584]{1,0:T(8,128)(2,1)S(1)}, bf16[80,1792]{1,0:T(8,128)(2,1)S(1)}, bf16[80,1792]{1,0:T(8,128)(2,1)S(1)}) custom-call(s32[3]{0:T(128)S(1)} %pad_add_fusion.sel_ref, bf16[128,3712]{1,0:T(8,128)(2,1)S(1)} %collective-permute-done.6.refs_0_.refs_2_, bf16[128,3712]{1,0:T(8,128)(2,1)S(1)} %collective-permute-done.5.refs_1_.refs_3_, ...), custom_call_target="tpu_custom_call" | custom-call | flops 1 | bytes 1 | tf_op jit(solution)/shard_map/expert/pallas_call | solution.py:220
  89.0 6.2 %collective-permute-done.12.refs_2_ = bf16[80,3584]{1,0:T(8,128)(2,1)S(1)} collective-permute-done((bf16[80,3584]{1,0:T(8,128)(2,1)S(1)}, bf16[80,3584]{1,0:T(8,128)(2,1)S(1)}, u32[]{:S(2)}, u32[]{:S(2)}) %collective-permute-start.12) | collective-permute-done | bytes 573472 | tf_op jit(solution)/shard_map/ppermute | solution.py:322
  95.1 0.9 collective-permute-start.16
  96.0 5.8 %expert.7 = (bf16[128,3584]{1,0:T(8,128)(2,1)S(1)}, bf16[80,1792]{1,0:T(8,128)(2,1)S(1)}, bf16[80,1792]{1,0:T(8,128)(2,1)S(1)}) custom-call(s32[3]{0:T(128)S(1)} %pad_add_fusion.sel_ref, bf16[128,3712]{1,0:T(8,128)(2,1)S(1)} %collective-permute-done.10.refs_0_.refs_2_, bf16[128,3712]{1,0:T(8,128)(2,1)S(1)} %collective-permute-done.9.refs_1_.refs_3_, ...), custom_call_target="tpu_custom_call" | custom-call | flops 1 | bytes 1 | tf_op jit(solution)/shard_map/expert/pallas_call | solution.py:220
  101.8 0.6 combine.7
  102.4 6.1 %collective-permute-start.17 = (bf16[128,1792]{1,0:T(8,128)(2,1)S(1)}, bf16[128,1792]{1,0:T(8,128)(2,1)S(1)}, u32[]{:S(2)}, u32[]{:S(2)}) collective-permute-start(bf16[128,1792]{1,0:T(8,128)(2,1)S(1)} %combine.7), channel_id=1, source_target_pairs={{0,2},{1,3},{6,4},{7,5},{8,10},{9,11},{14,12},{15,13},{16,18},{17,... | collective-permute-start | bytes 1376264 | tf_op jit(solution)/shard_map/ppermute | solution.py:322
  108.5 1.2 collective-permute-start.18
  109.7 0.9 collective-permute-start.13
  110.6 1.2 collective-permute-start.15
  111.7 6.6 %collective-permute-done.18.other_ref = bf16[80,1792]{1,0:T(8,128)(2,1)S(1)} collective-permute-done((bf16[80,1792]{1,0:T(8,128)(2,1)S(1)}, bf16[80,1792]{1,0:T(8,128)(2,1)S(1)}, u32[]{:S(2)}, u32[]{:S(2)}) %collective-permute-start.18) | collective-permute-done | bytes 286752 | tf_op jit(solution)/shard_map/ppermute | solution.py:322
  118.3 0.6 combine.8
  118.9 1.3 collective-permute-start.22
  120.3 0.7 collective-permute-start.20
  121.0 4.6 %collective-permute-done.15.other_ref = bf16[80,1792]{1,0:T(8,128)(2,1)S(1)} collective-permute-done((bf16[80,1792]{1,0:T(8,128)(2,1)S(1)}, bf16[80,1792]{1,0:T(8,128)(2,1)S(1)}, u32[]{:S(2)}, u32[]{:S(2)}) %collective-permute-start.15) | collective-permute-done | bytes 286752 | tf_op jit(solution)/shard_map/ppermute | solution.py:322
  125.7 0.6 combine.9
  126.2 1.6 collective-permute-start.24
  127.8 0.6 combine.10
  128.4 1.3 collective-permute-start.21
  129.8 1.8 %collective-permute-start.19 = (bf16[80,3584]{1,0:T(8,128)(2,1)S(1)}, bf16[80,3584]{1,0:T(8,128)(2,1)S(1)}, u32[]{:S(2)}, u32[]{:S(2)}) collective-permute-start(bf16[80,3584]{1,0:T(8,128)(2,1)S(1)} %get-tuple-element.113), channel_id=1, source_target_pairs={{0,1},{1,0},{2,3},{3,2},{4,5},{5,4},{6,7},{7,6},{8,9},{9,8},{10,11... | collective-permute-start | bytes 1720328 | tf_op jit(solution)/shard_map/ppermute | solution.py:322
  131.7 0.7 collective-permute-start.23
  132.4 6.3 %collective-permute-done.24 = bf16[128,1792]{1,0:T(8,128)(2,1)S(1)} collective-permute-done((bf16[128,1792]{1,0:T(8,128)(2,1)S(1)}, bf16[128,1792]{1,0:T(8,128)(2,1)S(1)}, u32[]{:S(2)}, u32[]{:S(2)}) %collective-permute-start.24) | collective-permute-done | bytes 458784 | tf_op jit(solution)/shard_map/ppermute | solution.py:322
  138.8 0.7 collective-permute-start.27
  139.7 1.3 collective-permute-start.26
  141.0 4.9 %collective-permute-done.21 = bf16[128,1792]{1,0:T(8,128)(2,1)S(1)} collective-permute-done((bf16[128,1792]{1,0:T(8,128)(2,1)S(1)}, bf16[128,1792]{1,0:T(8,128)(2,1)S(1)}, u32[]{:S(2)}, u32[]{:S(2)}) %collective-permute-start.21) | collective-permute-done | bytes 458784 | tf_op jit(solution)/shard_map/ppermute | solution.py:322
  145.8 0.1 add_convert_fusion.1
  146.0 0.7 collective-permute-start.25
  146.8 1.3 collective-permute-start.28
  148.1 5.8 %collective-permute-done.26.refs_3_ = bf16[128,1792]{1,0:T(8,128)(2,1)S(1)} collective-permute-done((bf16[128,1792]{1,0:T(8,128)(2,1)S(1)}, bf16[128,1792]{1,0:T(8,128)(2,1)S(1)}, u32[]{:S(2)}, u32[]{:S(2)}) %collective-permute-start.26) | collective-permute-done | bytes 458784 | tf_op jit(solution)/shard_map/ppermute | solution.py:322
  153.9 8.6 %collective-permute-done.28.refs_4_ = bf16[128,1792]{1,0:T(8,128)(2,1)S(1)} collective-permute-done((bf16[128,1792]{1,0:T(8,128)(2,1)S(1)}, bf16[128,1792]{1,0:T(8,128)(2,1)S(1)}, u32[]{:S(2)}, u32[]{:S(2)}) %collective-permute-start.28) | collective-permute-done | bytes 458784 | tf_op jit(solution)/shard_map/ppermute | solution.py:322
  162.5 2.8 %combine.11 = bf16[128,3584]{1,0:T(8,128)(2,1)} custom-call(bf16[128,80]{1,0:T(8,128)(2,1)S(1)} %get-tuple-element.62.back_ref, f32[128,128]{1,0:T(8,128)S(1)} %get-tuple-element.63.weight_ref, bf16[128,3584]{1,0:T(8,128)(2,1)S(1)} %get-tuple-element.81.own_ref, bf16[80,3584]{1,0:T(8,128)(2,1)S(1)} %collective-permute-done.19.other_ref, ...), custom_call_target="tpu_custom_call" | custom-call | flops 1 | bytes 1 | tf_op jit(solution)/shard_map/combine/pallas_call | solution.py:266
  (33 shorter events, 0.8 us)
Async XLA Ops:
  0.0 7.3 %collective-permute-start = (bf16[3584,512]{1,0:T(8,128)(2,1)}, bf16[3584,512]{1,0:T(8,128)(2,1)}, u32[]{:S(2)}, u32[]{:S(2)}) collective-permute-start(bf16[3584,512]{1,0:T(8,128)(2,1)} %bitcast.8), channel_id=1, source_target_pairs={{0,8},{8,0},{1,9},{9,1},{2,10},{10,2},{3,11},{11,3},{4,12},{12,4},... | collective-permute-start | bytes 11010056 | tf_op jit(solution)/shard_map/ppermute | solution.py:325
  0.5 34.1 %collective-permute-start.2 = (bf16[3584,512]{1,0:T(8,128)(2,1)}, bf16[3584,512]{1,0:T(8,128)(2,1)}, u32[]{:S(2)}, u32[]{:S(2)}) collective-permute-start(bf16[3584,512]{1,0:T(8,128)(2,1)} %bitcast.10), channel_id=1, source_target_pairs={{0,8},{8,0},{1,9},{9,1},{2,10},{10,2},{3,11},{11,3},{4,12},{12,4},... | collective-permute-start | bytes 11010056 | tf_op jit(solution)/shard_map/ppermute | solution.py:325
  0.5 34.1 %collective-permute-start.3 = (bf16[512,3584]{1,0:T(8,128)(2,1)}, bf16[512,3584]{1,0:T(8,128)(2,1)}, u32[]{:S(2)}, u32[]{:S(2)}) collective-permute-start(bf16[512,3584]{1,0:T(8,128)(2,1)} %bitcast.12), channel_id=1, source_target_pairs={{0,8},{8,0},{1,9},{9,1},{2,10},{10,2},{3,11},{11,3},{4,12},{12,4},... | collective-permute-start | bytes 11010056 | tf_op jit(solution)/shard_map/ppermute | solution.py:325
  1.0 1.2 copy-start.3
  2.2 0.7 copy-start.6
  2.9 0.7 copy-start.7
  4.6 24.4 %collective-permute-start.4 = (bf16[128,3712]{1,0:T(8,128)(2,1)S(1)}, bf16[128,3712]{1,0:T(8,128)(2,1)S(1)}, u32[]{:S(2)}, u32[]{:S(2)}) collective-permute-start(bf16[128,3712]{1,0:T(8,128)(2,1)S(1)} %get-tuple-element.64.refs_0_), channel_id=1, source_target_pairs={{0,2},{1,3},{2,0},{3,1},{4,6},{5,7},{6,4},{7,5},{8,10},{9,11},{10,... | collective-permute-start | bytes 2850824 | tf_op jit(solution)/shard_map/ppermute | solution.py:322
  7.3 21.7 %collective-permute-start.1 = (bf16[80,3584]{1,0:T(8,128)(2,1)S(1)}, bf16[80,3584]{1,0:T(8,128)(2,1)S(1)}, u32[]{:S(2)}, u32[]{:S(2)}) collective-permute-start(bf16[80,3584]{1,0:T(8,128)(2,1)S(1)} %get-tuple-element.66), channel_id=1, source_target_pairs={{0,1},{1,0},{2,3},{3,2},{4,5},{5,4},{6,7},{7,6},{8,9},{9,8},{10,11... | collective-permute-start | bytes 1720328 | tf_op jit(solution)/shard_map/ppermute | solution.py:322
  9.7 23.6 %collective-permute-start.5 = (bf16[128,3712]{1,0:T(8,128)(2,1)S(1)}, bf16[128,3712]{1,0:T(8,128)(2,1)S(1)}, u32[]{:S(2)}, u32[]{:S(2)}) collective-permute-start(bf16[128,3712]{1,0:T(8,128)(2,1)S(1)} %get-tuple-element.64.refs_0_), channel_id=1, source_target_pairs={{2,4},{3,5},{4,2},{5,3},{10,12},{11,13},{12,10},{13,11},{18,20},{1... | collective-permute-start | bytes 2850824 | tf_op jit(solution)/shard_map/ppermute | solution.py:322
  10.4 2.0 %copy-start = (bf16[1,3584,512]{2,1,0:T(8,128)(2,1)S(1)}, bf16[1,3584,512]{2,1,0:T(8,128)(2,1)}, u32[]{:S(2)}) copy-start(bf16[1,3584,512]{2,1,0:T(8,128)(2,1)} %param.9) | copy-start | bytes 11010052
  12.5 2.0 %copy-start.1 = (bf16[1,3584,512]{2,1,0:T(8,128)(2,1)S(1)}, bf16[1,3584,512]{2,1,0:T(8,128)(2,1)}, u32[]{:S(2)}) copy-start(bf16[1,3584,512]{2,1,0:T(8,128)(2,1)} %param.10) | copy-start | bytes 11010052
  14.5 2.0 %copy-start.2 = (bf16[1,512,3584]{2,1,0:T(8,128)(2,1)S(1)}, bf16[1,512,3584]{2,1,0:T(8,128)(2,1)}, u32[]{:S(2)}) copy-start(bf16[1,512,3584]{2,1,0:T(8,128)(2,1)} %param.11) | copy-start | bytes 11010052
  29.0 9.8 %copy-start.4 = (bf16[80,3584]{1,0:T(8,128)(2,1)}, bf16[80,3584]{1,0:T(8,128)(2,1)S(1)}, u32[]{:S(2)}) copy-start(bf16[80,3584]{1,0:T(8,128)(2,1)S(1)} %collective-permute-done.1.refs_1_) | copy-start | bytes 1720324
  29.0 23.1 %collective-permute-start.9 = (bf16[128,3712]{1,0:T(8,128)(2,1)S(1)}, bf16[128,3712]{1,0:T(8,128)(2,1)S(1)}, u32[]{:S(2)}, u32[]{:S(2)}) collective-permute-start(bf16[128,3712]{1,0:T(8,128)(2,1)S(1)} %collective-permute-done.4.refs_0_.refs_1_), channel_id=1, source_target_pairs={{2,4},{3,5},{4,2},{5,3},{10,12},{11,13},{12,10},{13,11},{18,20},{1... | collective-permute-start | bytes 2850824 | tf_op jit(solution)/shard_map/ppermute | solution.py:322
  31.5 14.9 %collective-permute-start.7 = (bf16[80,3584]{1,0:T(8,128)(2,1)S(1)}, bf16[80,3584]{1,0:T(8,128)(2,1)S(1)}, u32[]{:S(2)}, u32[]{:S(2)}) collective-permute-start(bf16[80,3584]{1,0:T(8,128)(2,1)S(1)} %get-tuple-element.72), channel_id=1, source_target_pairs={{0,1},{1,0},{2,3},{3,2},{4,5},{5,4},{6,7},{7,6},{8,9},{9,8},{10,11... | collective-permute-start | bytes 1720328 | tf_op jit(solution)/shard_map/ppermute | solution.py:322
  33.3 27.6 %collective-permute-start.6 = (bf16[128,3712]{1,0:T(8,128)(2,1)S(1)}, bf16[128,3712]{1,0:T(8,128)(2,1)S(1)}, u32[]{:S(2)}, u32[]{:S(2)}) collective-permute-start(bf16[128,3712]{1,0:T(8,128)(2,1)S(1)} %collective-permute-done.5.refs_1_.refs_3_), channel_id=1, source_target_pairs={{2,0},{3,1},{4,6},{5,7},{10,8},{11,9},{12,14},{13,15},{18,16},{19,... | collective-permute-start | bytes 2850824 | tf_op jit(solution)/shard_map/ppermute | solution.py:322
  38.9 1.1 copy-start.5
  52.1 27.6 %collective-permute-start.10 = (bf16[128,3712]{1,0:T(8,128)(2,1)S(1)}, bf16[128,3712]{1,0:T(8,128)(2,1)S(1)}, u32[]{:S(2)}, u32[]{:S(2)}) collective-permute-start(bf16[128,3712]{1,0:T(8,128)(2,1)S(1)} %collective-permute-done.9.refs_1_.refs_3_), channel_id=1, source_target_pairs={{2,0},{3,1},{4,6},{5,7},{10,8},{11,9},{12,14},{13,15},{18,16},{19,... | collective-permute-start | bytes 2850824 | tf_op jit(solution)/shard_map/ppermute | solution.py:322
  53.4 16.0 %collective-permute-start.11 = (bf16[80,3584]{1,0:T(8,128)(2,1)S(1)}, bf16[80,3584]{1,0:T(8,128)(2,1)S(1)}, u32[]{:S(2)}, u32[]{:S(2)}) collective-permute-start(bf16[80,3584]{1,0:T(8,128)(2,1)S(1)} %get-tuple-element.92), channel_id=1, source_target_pairs={{0,1},{1,0},{2,3},{3,2},{4,5},{5,4},{6,7},{7,6},{8,9},{9,8},{10,11... | collective-permute-start | bytes 1720328 | tf_op jit(solution)/shard_map/ppermute | solution.py:322
  62.9 16.8 %collective-permute-start.8 = (bf16[80,3584]{1,0:T(8,128)(2,1)S(1)}, bf16[80,3584]{1,0:T(8,128)(2,1)S(1)}, u32[]{:S(2)}, u32[]{:S(2)}) collective-permute-start(bf16[80,3584]{1,0:T(8,128)(2,1)S(1)} %get-tuple-element.88), channel_id=1, source_target_pairs={{0,1},{1,0},{2,3},{3,2},{4,5},{5,4},{6,7},{7,6},{8,9},{9,8},{10,11... | collective-permute-start | bytes 1720328 | tf_op jit(solution)/shard_map/ppermute | solution.py:322
  70.5 25.5 %collective-permute-start.14 = (bf16[128,3584]{1,0:T(8,128)(2,1)S(1)}, bf16[128,3584]{1,0:T(8,128)(2,1)S(1)}, u32[]{:S(2)}, u32[]{:S(2)}) collective-permute-start(bf16[128,3584]{1,0:T(8,128)(2,1)S(1)} %combine.6), channel_id=1, source_target_pairs={{0,2},{1,3},{6,4},{7,5},{8,10},{9,11},{14,12},{15,13},{16,18},{17,... | collective-permute-start | bytes 2752520 | tf_op jit(solution)/shard_map/ppermute | solution.py:322
  81.7 13.4 %collective-permute-start.12 = (bf16[80,3584]{1,0:T(8,128)(2,1)S(1)}, bf16[80,3584]{1,0:T(8,128)(2,1)S(1)}, u32[]{:S(2)}, u32[]{:S(2)}) collective-permute-start(bf16[80,3584]{1,0:T(8,128)(2,1)S(1)} %get-tuple-element.95), channel_id=1, source_target_pairs={{0,1},{1,0},{2,3},{3,2},{4,5},{5,4},{6,7},{7,6},{8,9},{9,8},{10,11... | collective-permute-start | bytes 1720328 | tf_op jit(solution)/shard_map/ppermute | solution.py:322
  95.1 6.6 %collective-permute-start.16 = (bf16[80,1792]{1,0:T(8,128)(2,1)S(1)}, bf16[80,1792]{1,0:T(8,128)(2,1)S(1)}, u32[]{:S(2)}, u32[]{:S(2)}) collective-permute-start(bf16[80,1792]{1,0:T(8,128)(2,1)S(1)} %get-tuple-element.106), channel_id=1, source_target_pairs={{0,1},{1,0},{2,3},{3,2},{4,5},{5,4},{6,7},{7,6},{8,9},{9,8},{10,11... | collective-permute-start | bytes 860168 | tf_op jit(solution)/shard_map/ppermute | solution.py:322
  102.4 17.8 %collective-permute-start.17 = (bf16[128,1792]{1,0:T(8,128)(2,1)S(1)}, bf16[128,1792]{1,0:T(8,128)(2,1)S(1)}, u32[]{:S(2)}, u32[]{:S(2)}) collective-permute-start(bf16[128,1792]{1,0:T(8,128)(2,1)S(1)} %combine.7), channel_id=1, source_target_pairs={{0,2},{1,3},{6,4},{7,5},{8,10},{9,11},{14,12},{15,13},{16,18},{17,... | collective-permute-start | bytes 1376264 | tf_op jit(solution)/shard_map/ppermute | solution.py:322
  108.5 9.8 %collective-permute-start.18 = (bf16[80,1792]{1,0:T(8,128)(2,1)S(1)}, bf16[80,1792]{1,0:T(8,128)(2,1)S(1)}, u32[]{:S(2)}, u32[]{:S(2)}) collective-permute-start(bf16[80,1792]{1,0:T(8,128)(2,1)S(1)} %get-tuple-element.108), channel_id=1, source_target_pairs={{0,1},{1,0},{2,3},{3,2},{4,5},{5,4},{6,7},{7,6},{8,9},{9,8},{10,11... | collective-permute-start | bytes 860168 | tf_op jit(solution)/shard_map/ppermute | solution.py:322
  109.7 18.1 %collective-permute-start.13 = (bf16[80,1792]{1,0:T(8,128)(2,1)S(1)}, bf16[80,1792]{1,0:T(8,128)(2,1)S(1)}, u32[]{:S(2)}, u32[]{:S(2)}) collective-permute-start(bf16[80,1792]{1,0:T(8,128)(2,1)S(1)} %get-tuple-element.99), channel_id=1, source_target_pairs={{0,1},{1,0},{2,3},{3,2},{4,5},{5,4},{6,7},{7,6},{8,9},{9,8},{10,11... | collective-permute-start | bytes 860168 | tf_op jit(solution)/shard_map/ppermute | solution.py:322
  110.6 15.1 %collective-permute-start.15 = (bf16[80,1792]{1,0:T(8,128)(2,1)S(1)}, bf16[80,1792]{1,0:T(8,128)(2,1)S(1)}, u32[]{:S(2)}, u32[]{:S(2)}) collective-permute-start(bf16[80,1792]{1,0:T(8,128)(2,1)S(1)} %get-tuple-element.104), channel_id=1, source_target_pairs={{0,1},{1,0},{2,3},{3,2},{4,5},{5,4},{6,7},{7,6},{8,9},{9,8},{10,11... | collective-permute-start | bytes 860168 | tf_op jit(solution)/shard_map/ppermute | solution.py:322
  118.9 12.7 %collective-permute-start.22 = (bf16[128,1792]{1,0:T(8,128)(2,1)S(1)}, bf16[128,1792]{1,0:T(8,128)(2,1)S(1)}, u32[]{:S(2)}, u32[]{:S(2)}) collective-permute-start(bf16[128,1792]{1,0:T(8,128)(2,1)S(1)} %combine.8), channel_id=1, source_target_pairs={{0,2},{1,3},{6,4},{7,5},{8,10},{9,11},{14,12},{15,13},{16,18},{17,... | collective-permute-start | bytes 1376264 | tf_op jit(solution)/shard_map/ppermute | solution.py:322
  120.3 27.8 %collective-permute-start.20 = (bf16[128,1792]{1,0:T(8,128)(2,1)S(1)}, bf16[128,1792]{1,0:T(8,128)(2,1)S(1)}, u32[]{:S(2)}, u32[]{:S(2)}) collective-permute-start(bf16[128,1792]{1,0:T(8,128)(2,1)S(1)} %add_convert_fusion.5), channel_id=1, source_target_pairs={{2,4},{3,5},{4,2},{5,3},{10,12},{11,13},{12,10},{13,11},{18,20},{1... | collective-permute-start | bytes 1376264 | tf_op jit(solution)/shard_map/ppermute | solution.py:322
  126.2 12.5 %collective-permute-start.24 = (bf16[128,1792]{1,0:T(8,128)(2,1)S(1)}, bf16[128,1792]{1,0:T(8,128)(2,1)S(1)}, u32[]{:S(2)}, u32[]{:S(2)}) collective-permute-start(bf16[128,1792]{1,0:T(8,128)(2,1)S(1)} %combine.9), channel_id=1, source_target_pairs={{0,2},{1,3},{6,4},{7,5},{8,10},{9,11},{14,12},{15,13},{16,18},{17,... | collective-permute-start | bytes 1376264 | tf_op jit(solution)/shard_map/ppermute | solution.py:322
  128.4 17.4 %collective-permute-start.21 = (bf16[128,1792]{1,0:T(8,128)(2,1)S(1)}, bf16[128,1792]{1,0:T(8,128)(2,1)S(1)}, u32[]{:S(2)}, u32[]{:S(2)}) collective-permute-start(bf16[128,1792]{1,0:T(8,128)(2,1)S(1)} %combine.10), channel_id=1, source_target_pairs={{0,2},{1,3},{6,4},{7,5},{8,10},{9,11},{14,12},{15,13},{16,18},{17,... | collective-permute-start | bytes 1376264 | tf_op jit(solution)/shard_map/ppermute | solution.py:322
  129.8 18.4 %collective-permute-start.19 = (bf16[80,3584]{1,0:T(8,128)(2,1)S(1)}, bf16[80,3584]{1,0:T(8,128)(2,1)S(1)}, u32[]{:S(2)}, u32[]{:S(2)}) collective-permute-start(bf16[80,3584]{1,0:T(8,128)(2,1)S(1)} %get-tuple-element.113), channel_id=1, source_target_pairs={{0,1},{1,0},{2,3},{3,2},{4,5},{5,4},{6,7},{7,6},{8,9},{9,8},{10,11... | collective-permute-start | bytes 1720328 | tf_op jit(solution)/shard_map/ppermute | solution.py:322
  131.7 7.8 %collective-permute-start.23 = (bf16[128,1792]{1,0:T(8,128)(2,1)S(1)}, bf16[128,1792]{1,0:T(8,128)(2,1)S(1)}, u32[]{:S(2)}, u32[]{:S(2)}) collective-permute-start(bf16[128,1792]{1,0:T(8,128)(2,1)S(1)} %add_convert_fusion.4), channel_id=1, source_target_pairs={{2,4},{3,5},{4,2},{5,3},{10,12},{11,13},{12,10},{13,11},{18,20},{1... | collective-permute-start | bytes 1376264 | tf_op jit(solution)/shard_map/ppermute | solution.py:322
  138.8 7.8 %collective-permute-start.27 = (bf16[128,1792]{1,0:T(8,128)(2,1)S(1)}, bf16[128,1792]{1,0:T(8,128)(2,1)S(1)}, u32[]{:S(2)}, u32[]{:S(2)}) collective-permute-start(bf16[128,1792]{1,0:T(8,128)(2,1)S(1)} %add_convert_fusion.3), channel_id=1, source_target_pairs={{2,4},{3,5},{4,2},{5,3},{10,12},{11,13},{12,10},{13,11},{18,20},{1... | collective-permute-start | bytes 1376264 | tf_op jit(solution)/shard_map/ppermute | solution.py:322
  139.7 14.3 %collective-permute-start.26 = (bf16[128,1792]{1,0:T(8,128)(2,1)S(1)}, bf16[128,1792]{1,0:T(8,128)(2,1)S(1)}, u32[]{:S(2)}, u32[]{:S(2)}) collective-permute-start(bf16[128,1792]{1,0:T(8,128)(2,1)S(1)} %add_convert_fusion.2), channel_id=1, source_target_pairs={{2,0},{3,1},{4,6},{5,7},{10,8},{11,9},{12,14},{13,15},{18,16},{19,... | collective-permute-start | bytes 1376264 | tf_op jit(solution)/shard_map/ppermute | solution.py:322
  146.0 2.2 %collective-permute-start.25 = (bf16[128,1792]{1,0:T(8,128)(2,1)S(1)}, bf16[128,1792]{1,0:T(8,128)(2,1)S(1)}, u32[]{:S(2)}, u32[]{:S(2)}) collective-permute-start(bf16[128,1792]{1,0:T(8,128)(2,1)S(1)} %add_convert_fusion.1), channel_id=1, source_target_pairs={{2,4},{3,5},{4,2},{5,3},{10,12},{11,13},{12,10},{13,11},{18,20},{1... | collective-permute-start | bytes 1376264 | tf_op jit(solution)/shard_map/ppermute | solution.py:322
  146.8 15.7 %collective-permute-start.28 = (bf16[128,1792]{1,0:T(8,128)(2,1)S(1)}, bf16[128,1792]{1,0:T(8,128)(2,1)S(1)}, u32[]{:S(2)}, u32[]{:S(2)}) collective-permute-start(bf16[128,1792]{1,0:T(8,128)(2,1)S(1)} %add_convert_fusion), channel_id=1, source_target_pairs={{2,0},{3,1},{4,6},{5,7},{10,8},{11,9},{12,14},{13,15},{18,16},{19,... | collective-permute-start | bytes 1376264 | tf_op jit(solution)/shard_map/ppermute | solution.py:322

commit v4 on v3

--- a/solution.py
+++ b/solution.py
@@ -233,52 +233,57 @@
     )(sel, *parts, y, *gates, *ups, *downs)
 
 
-def combine_kernel(scale, splits, back_ref, weight_ref, own_ref, other_ref, *refs):
-    out_ref = refs[-1]
-    step, steps = pl.program_id(0), pl.num_programs(0)
+def combine_kernel(scale, back_ref, weight_ref, own_ref, other_ref, *refs):
     weights = weight_ref[...]
     value = weights[:, 0:1] * own_ref[...].astype(jnp.float32)
     value = value + weights[:, 1:2] * dot32(back_ref[...], other_ref[...])
-    at = 0
-    for pieces in splits:
-        term = refs[at][...].astype(jnp.float32)
-        for p in range(1, pieces):
-            here = step * pieces >= p * steps
-            term = jnp.where(here, refs[at + p][...].astype(jnp.float32), term)
-        at += pieces
-        value = value + term
+    for ref in refs[:-1]:
+        value = value + ref[...].astype(jnp.float32)
     if scale is not None:
         value = value * scale
-    out_ref[...] = value.astype(jnp.bfloat16)
-
-
-def combine(tables, own, other, extra=(), first=0, scale=None):
-    rows = own.shape[0]
+    refs[-1][...] = value.astype(jnp.bfloat16)
+
+
+def into_kernel(scale, *refs):
+    combine_kernel(scale, *refs[:-2], refs[-1])
+
+
+def combine(tables, own, other, extra=(), first=0, count=None, scale=None, into=None):
+    rows, full = own.shape
     cap, width = other.shape
-    block = column_block(width)
-    steps = width // block
+    count = count or width
+    block = column_block(count)
     offset = first // block
 
-    def piece(p, count):
-        each = steps // count
-        return pl.BlockSpec((rows, block), lambda i: (0, jnp.clip(i - p * each, 0, each - 1)))
-
+    def columns(array):
+        shift = offset if array.shape[1] == full else 0
+        return pl.BlockSpec((array.shape[0], block), lambda i: (0, i + shift))
+
+    whole = full if scale is not None else count
+    shift = offset if scale is not None else 0
+    operands = [*tables, own, other, *extra]
+    in_specs = [
+        pl.BlockSpec((rows, cap), lambda i: (0, 0)),
+        pl.BlockSpec((rows, LANES), lambda i: (0, 0)),
+    ] + [columns(array) for array in operands[2:]]
+    body = combine_kernel
+    aliases = {}
+    if into is not None:
+        aliases = {len(operands): 0}
+        operands.append(into)
+        in_specs.append(pl.BlockSpec(memory_space=pl.ANY))
+        body = into_kernel
     return pl.pallas_call(
-        functools.partial(combine_kernel, scale, [len(e) for e in extra]),
-        grid=(steps,),
-        in_specs=[
-            pl.BlockSpec((rows, cap), lambda i: (0, 0)),
-            pl.BlockSpec((rows, LANES), lambda i: (0, 0)),
-            pl.BlockSpec((rows, block), lambda i: (0, i + offset)),
-            pl.BlockSpec((cap, block), lambda i: (0, i)),
-        ]
-        + [piece(p, len(e)) for e in extra for p in range(len(e))],
-        out_specs=pl.BlockSpec((rows, block), lambda i: (0, i)),
-        out_shape=jax.ShapeDtypeStruct((rows, width), jnp.bfloat16),
+        functools.partial(body, scale),
+        grid=(count // block,),
+        in_specs=in_specs,
+        out_specs=pl.BlockSpec((rows, block), lambda i: (0, i + shift)),
+        out_shape=jax.ShapeDtypeStruct((rows, whole), jnp.bfloat16),
+        input_output_aliases=aliases,
         compiler_params=pltpu.CompilerParams(vmem_limit_bytes=VMEM_LIMIT),
         cost_estimate=BRIEF,
         name="combine",
-    )(*tables, own, other, *[e for group in extra for e in group])
+    )(*operands)
 
 
 def column_block(width):
@@ -378,7 +383,10 @@
     r21 = send(p21, INNER)
     e1 = add(q1[:, part:], after(r31, p21))
     r31 = send(e1, TO_ENDS)
-    return combine(tables0, o0, b0, extra=([r1], [r20, r21], [r30, r31]), scale=SCALE)
+    mixed = combine(tables0, o0, b0, (r1, r20, r30), first=0, count=part, scale=SCALE)
+    return combine(
+        tables0, o0, b0, (r1, r21, after(r31, mixed)), first=part, count=part, scale=SCALE, into=mixed
+    )
 
 
 def all_to_all_form(tokens, scores, expert_ids, w_gate, w_up, w_down):

time: 166 us -> 165 us (level)
    pallas_call x6 -> x7, Pallas kernels: 6.13 us -> 6.34 us  [combine(): pl.pallas_call(functools.partial(body, scale), grid=(count // block,), in...]
  transfers between devices with their start and end apart: 29 -> 29, of which waited for: 12 -> 12; matrix products, arithmetic and copies ran while one was open for 0% -> 0% of each run, Pallas kernels for 23% -> 24%
where the time goes in v4:
time: 165 us; the launch traced here: 164 us
  waiting for transfers between devices  69.1 us (42%)
  starting transfers between devices  42.8 us (26%)
  Pallas kernels  41.2 us (25%)
  local copies, waits for them, and re-layouts  9.71 us (6%)
    ppermute x26, waiting for transfers between devices, send(): return lax.ppermute(value, 'expert', pairs)  69.1 us
    ppermute x26, starting transfers between devices, send(): return lax.ppermute(value, 'expert', pairs)  41.9 us
    pallas_call x4, Pallas kernels, expert(): pl.pallas_call(functools.partial(expert_kernel, len(parts), halves), in_s...  23 us
    unnamed x16, local copies, waits for them, and re-layouts  9.71 us
    pallas_call x7, Pallas kernels, combine(): pl.pallas_call(functools.partial(body, scale), grid=(count // block,), in...  6.34 us
    pallas_call x3, Pallas kernels, pick_rows(): pl.pallas_call(functools.partial(pick_kernel, experts, len(parts)), grid=...  5.83 us
    pallas_call x2, Pallas kernels, hold(): pl.pallas_call(hold_kernel, in_specs=[pl.BlockSpec(memory_space=pltpu.HBM...  4.99 us
  transfers between devices with their start and end apart: 29, of which 12 were waited for; matrix products, arithmetic and copies ran while one was open for 0% of the time, Pallas kernels for 24%

profile of v4, /device:TPU:0, one launch (start us, length us, event | category | flops | bytes accessed | tf_op | source)
XLA Modules:
  0.0 164.0 jit_solution(8346062030587983278)
XLA Ops:
  0.0 0.5 collective-permute-start
  0.5 0.5 collective-permute-start.3
  1.0 1.2 copy-done.3
  2.2 0.7 copy-done.6
  2.9 0.7 copy-done.7
  3.6 1.0 open.1
  4.6 2.6 %collective-permute-start.4 = (bf16[128,3712]{1,0:T(8,128)(2,1)S(1)}, bf16[128,3712]{1,0:T(8,128)(2,1)S(1)}, u32[]{:S(2)}, u32[]{:S(2)}) collective-permute-start(bf16[128,3712]{1,0:T(8,128)(2,1)S(1)} %get-tuple-element.65.refs_0_), channel_id=1, source_target_pairs={{0,2},{1,3},{2,0},{3,1},{4,6},{5,7},{6,4},{7,5},{8,10},{9,11},{10,... | collective-permute-start | bytes 2850824 | tf_op jit(solution)/shard_map/ppermute | solution.py:327
  7.3 2.4 %collective-permute-start.1 = (bf16[80,3584]{1,0:T(8,128)(2,1)S(1)}, bf16[80,3584]{1,0:T(8,128)(2,1)S(1)}, u32[]{:S(2)}, u32[]{:S(2)}) collective-permute-start(bf16[80,3584]{1,0:T(8,128)(2,1)S(1)} %get-tuple-element.67), channel_id=1, source_target_pairs={{0,1},{1,0},{2,3},{3,2},{4,5},{5,4},{6,7},{7,6},{8,9},{9,8},{10,11... | collective-permute-start | bytes 1720328 | tf_op jit(solution)/shard_map/ppermute | solution.py:327
  9.7 0.7 collective-permute-start.5
  10.4 2.0 %copy-done = bf16[1,3584,512]{2,1,0:T(8,128)(2,1)S(1)} copy-done((bf16[1,3584,512]{2,1,0:T(8,128)(2,1)S(1)}, bf16[1,3584,512]{2,1,0:T(8,128)(2,1)}, u32[]{:S(2)}) %copy-start) | copy-done | bytes 3670040
  12.5 2.0 %copy-done.1 = bf16[1,3584,512]{2,1,0:T(8,128)(2,1)S(1)} copy-done((bf16[1,3584,512]{2,1,0:T(8,128)(2,1)S(1)}, bf16[1,3584,512]{2,1,0:T(8,128)(2,1)}, u32[]{:S(2)}) %copy-start.1) | copy-done | bytes 3670040
  14.5 2.0 %copy-done.2 = bf16[1,512,3584]{2,1,0:T(8,128)(2,1)S(1)} copy-done((bf16[1,512,3584]{2,1,0:T(8,128)(2,1)S(1)}, bf16[1,512,3584]{2,1,0:T(8,128)(2,1)}, u32[]{:S(2)}) %copy-start.2) | copy-done | bytes 3670040
  16.6 0.8 hold.2
  17.3 11.7 %collective-permute-done.4.refs_0_.refs_1_ = bf16[128,3712]{1,0:T(8,128)(2,1)S(1)} collective-permute-done((bf16[128,3712]{1,0:T(8,128)(2,1)S(1)}, bf16[128,3712]{1,0:T(8,128)(2,1)S(1)}, u32[]{:S(2)}, u32[]{:S(2)}) %collective-permute-start.4) | collective-permute-done | bytes 950304 | tf_op jit(solution)/shard_map/ppermute | solution.py:327
  29.0 0.7 collective-permute-start.9
  29.7 1.8 %pick.3 = (bf16[80,3584]{1,0:T(8,128)(2,1)S(1)}, bf16[128,80]{1,0:T(8,128)(2,1)S(1)}, f32[128,128]{1,0:T(8,128)S(1)}) custom-call(s32[3]{0:T(128)S(1)} %pad_add_fusion.sel_ref, bf16[128,3712]{1,0:T(8,128)(2,1)S(1)} %collective-permute-done.4.refs_0_.refs_1_, bf16[128,3712]{1,0:T(8,128)(2,1)S(1)} %collective-permute-done.4.refs_0_.refs_1_), custom_call_target="tpu_custom_call" | custom-call | flops 1 | bytes 1 | tf_op jit(solution)/shard_map/pick/pallas_call | solution.py:132
  31.5 1.7 %collective-permute-start.7 = (bf16[80,3584]{1,0:T(8,128)(2,1)S(1)}, bf16[80,3584]{1,0:T(8,128)(2,1)S(1)}, u32[]{:S(2)}, u32[]{:S(2)}) collective-permute-start(bf16[80,3584]{1,0:T(8,128)(2,1)S(1)} %get-tuple-element.73), channel_id=1, source_target_pairs={{0,1},{1,0},{2,3},{3,2},{4,5},{5,4},{6,7},{7,6},{8,9},{9,8},{10,11... | collective-permute-start | bytes 1720328 | tf_op jit(solution)/shard_map/ppermute | solution.py:327
  33.3 1.3 collective-permute-start.6
  34.6 4.2 %hold.3 = (bf16[3584,512]{1,0:T(8,128)(2,1)S(1)}, bf16[3584,512]{1,0:T(8,128)(2,1)S(1)}, bf16[512,3584]{1,0:T(8,128)(2,1)S(1)}) custom-call(bf16[3584,512]{1,0:T(8,128)(2,1)} %collective-permute-done.refs_0_, bf16[3584,512]{1,0:T(8,128)(2,1)} %collective-permute-done.2.refs_1_, bf16[512,3584]{1,0:T(8,128)(2,1)} %collective-permute-done.3.refs_2_), custom_call_target="tpu_custom_call" | custom-call | flops 1 | bytes 1 | tf_op jit(solution)/shard_map/hold/pallas_call | solution.py:168
  38.9 1.1 copy-done.5
  39.9 5.7 %expert.4 = (bf16[128,3584]{1,0:T(8,128)(2,1)S(1)}, bf16[80,3584]{1,0:T(8,128)(2,1)S(1)}) custom-call(s32[3]{0:T(128)S(1)} %pad_add_fusion.sel_ref, bf16[128,3712]{1,0:T(8,128)(2,1)S(1)} %get-tuple-element.65.refs_0_, bf16[80,3584]{1,0:T(8,128)(2,1)S(1)} %copy-done.5, bf16[3584,512]{1,0:T(8,128)(2,1)S(1)} %get-tuple-element.71.refs_2_.refs_3_, ...), custom_call_target="tpu_custom_call" | custom-call | flops 1 | bytes 1 | tf_op jit(solution)/shard_map/expert/pallas_call | solution.py:220
  45.6 0.8 collective-permute-done.7.refs_1_
  46.4 5.7 %expert.5 = (bf16[128,3584]{1,0:T(8,128)(2,1)S(1)}, bf16[80,3584]{1,0:T(8,128)(2,1)S(1)}) custom-call(s32[3]{0:T(128)S(1)} %pad_add_fusion.sel_ref, bf16[128,3712]{1,0:T(8,128)(2,1)S(1)} %collective-permute-done.4.refs_0_.refs_1_, bf16[80,3584]{1,0:T(8,128)(2,1)S(1)} %collective-permute-done.7.refs_1_, ...), custom_call_target="tpu_custom_call" | custom-call | flops 1 | bytes 1 | tf_op jit(solution)/shard_map/expert/pallas_call | solution.py:220
  52.1 1.3 collective-permute-start.10
  53.4 1.5 collective-permute-start.11
  54.9 5.9 %collective-permute-done.6.refs_0_.refs_2_ = bf16[128,3712]{1,0:T(8,128)(2,1)S(1)} collective-permute-done((bf16[128,3712]{1,0:T(8,128)(2,1)S(1)}, bf16[128,3712]{1,0:T(8,128)(2,1)S(1)}, u32[]{:S(2)}, u32[]{:S(2)}) %collective-permute-start.6) | collective-permute-done | bytes 950304 | tf_op jit(solution)/shard_map/ppermute | solution.py:327
  60.9 2.0 %pick.4 = (bf16[80,3584]{1,0:T(8,128)(2,1)S(1)}, bf16[128,80]{1,0:T(8,128)(2,1)S(1)}, f32[128,128]{1,0:T(8,128)S(1)}) custom-call(s32[3]{0:T(128)S(1)} %pad_add_fusion.sel_ref, bf16[128,3712]{1,0:T(8,128)(2,1)S(1)} %collective-permute-done.6.refs_0_.refs_2_, bf16[128,3712]{1,0:T(8,128)(2,1)S(1)} %collective-permute-done.5.refs_1_.refs_3_, ...), custom_call_target="tpu_custom_call" | custom-call | flops 1 | bytes 1 | tf_op jit(solution)/shard_map/pick/pallas_call | solution.py:132
  62.9 0.4 collective-permute-start.8
  63.3 6.1 %collective-permute-done.11.other_ref = bf16[80,3584]{1,0:T(8,128)(2,1)S(1)} collective-permute-done((bf16[80,3584]{1,0:T(8,128)(2,1)S(1)}, bf16[80,3584]{1,0:T(8,128)(2,1)S(1)}, u32[]{:S(2)}, u32[]{:S(2)}) %collective-permute-start.11) | collective-permute-done | bytes 573472 | tf_op jit(solution)/shard_map/ppermute | solution.py:327
  69.4 1.1 combine.7
  70.5 6.2 %collective-permute-start.14 = (bf16[128,3584]{1,0:T(8,128)(2,1)S(1)}, bf16[128,3584]{1,0:T(8,128)(2,1)S(1)}, u32[]{:S(2)}, u32[]{:S(2)}) collective-permute-start(bf16[128,3584]{1,0:T(8,128)(2,1)S(1)} %combine.7), channel_id=1, source_target_pairs={{0,2},{1,3},{6,4},{7,5},{8,10},{9,11},{14,12},{15,13},{16,18},{17,... | collective-permute-start | bytes 2752520 | tf_op jit(solution)/shard_map/ppermute | solution.py:327
  76.8 3.0 %collective-permute-done.8.refs_2_ = bf16[80,3584]{1,0:T(8,128)(2,1)S(1)} collective-permute-done((bf16[80,3584]{1,0:T(8,128)(2,1)S(1)}, bf16[80,3584]{1,0:T(8,128)(2,1)S(1)}, u32[]{:S(2)}, u32[]{:S(2)}) %collective-permute-start.8) | collective-permute-done | bytes 573472 | tf_op jit(solution)/shard_map/ppermute | solution.py:327
  79.7 2.0 %pick.5 = (bf16[80,3584]{1,0:T(8,128)(2,1)S(1)}, bf16[128,80]{1,0:T(8,128)(2,1)S(1)}, f32[128,128]{1,0:T(8,128)S(1)}) custom-call(s32[3]{0:T(128)S(1)} %pad_add_fusion.sel_ref, bf16[128,3712]{1,0:T(8,128)(2,1)S(1)} %collective-permute-done.10.refs_0_.refs_2_, bf16[128,3712]{1,0:T(8,128)(2,1)S(1)} %collective-permute-done.9.refs_1_.refs_3_, ...), custom_call_target="tpu_custom_call" | custom-call | flops 1 | bytes 1 | tf_op jit(solution)/shard_map/pick/pallas_call | solution.py:132
  81.7 1.3 collective-permute-start.12
  83.0 5.9 %expert.6 = (bf16[128,3584]{1,0:T(8,128)(2,1)S(1)}, bf16[80,1792]{1,0:T(8,128)(2,1)S(1)}, bf16[80,1792]{1,0:T(8,128)(2,1)S(1)}) custom-call(s32[3]{0:T(128)S(1)} %pad_add_fusion.sel_ref, bf16[128,3712]{1,0:T(8,128)(2,1)S(1)} %collective-permute-done.6.refs_0_.refs_2_, bf16[128,3712]{1,0:T(8,128)(2,1)S(1)} %collective-permute-done.5.refs_1_.refs_3_, ...), custom_call_target="tpu_custom_call" | custom-call | flops 1 | bytes 1 | tf_op jit(solution)/shard_map/expert/pallas_call | solution.py:220
  88.9 6.2 %collective-permute-done.12.refs_2_ = bf16[80,3584]{1,0:T(8,128)(2,1)S(1)} collective-permute-done((bf16[80,3584]{1,0:T(8,128)(2,1)S(1)}, bf16[80,3584]{1,0:T(8,128)(2,1)S(1)}, u32[]{:S(2)}, u32[]{:S(2)}) %collective-permute-start.12) | collective-permute-done | bytes 573472 | tf_op jit(solution)/shard_map/ppermute | solution.py:327
  95.1 0.9 collective-permute-start.16
  96.0 5.8 %expert.7 = (bf16[128,3584]{1,0:T(8,128)(2,1)S(1)}, bf16[80,1792]{1,0:T(8,128)(2,1)S(1)}, bf16[80,1792]{1,0:T(8,128)(2,1)S(1)}) custom-call(s32[3]{0:T(128)S(1)} %pad_add_fusion.sel_ref, bf16[128,3712]{1,0:T(8,128)(2,1)S(1)} %collective-permute-done.10.refs_0_.refs_2_, bf16[128,3712]{1,0:T(8,128)(2,1)S(1)} %collective-permute-done.9.refs_1_.refs_3_, ...), custom_call_target="tpu_custom_call" | custom-call | flops 1 | bytes 1 | tf_op jit(solution)/shard_map/expert/pallas_call | solution.py:220
  101.8 0.6 combine.8
  102.4 6.1 %collective-permute-start.17 = (bf16[128,1792]{1,0:T(8,128)(2,1)S(1)}, bf16[128,1792]{1,0:T(8,128)(2,1)S(1)}, u32[]{:S(2)}, u32[]{:S(2)}) collective-permute-start(bf16[128,1792]{1,0:T(8,128)(2,1)S(1)} %combine.8), channel_id=1, source_target_pairs={{0,2},{1,3},{6,4},{7,5},{8,10},{9,11},{14,12},{15,13},{16,18},{17,... | collective-permute-start | bytes 1376264 | tf_op jit(solution)/shard_map/ppermute | solution.py:327
  108.5 1.2 collective-permute-start.18
  109.7 0.9 collective-permute-start.13
  110.6 1.2 collective-permute-start.15
  111.7 6.6 %collective-permute-done.18.other_ref = bf16[80,1792]{1,0:T(8,128)(2,1)S(1)} collective-permute-done((bf16[80,1792]{1,0:T(8,128)(2,1)S(1)}, bf16[80,1792]{1,0:T(8,128)(2,1)S(1)}, u32[]{:S(2)}, u32[]{:S(2)}) %collective-permute-start.18) | collective-permute-done | bytes 286752 | tf_op jit(solution)/shard_map/ppermute | solution.py:327
  118.3 0.6 combine.9
  118.9 1.3 collective-permute-start.21
  120.3 0.7 collective-permute-start.27
  121.0 4.6 %collective-permute-done.15.other_ref = bf16[80,1792]{1,0:T(8,128)(2,1)S(1)} collective-permute-done((bf16[80,1792]{1,0:T(8,128)(2,1)S(1)}, bf16[80,1792]{1,0:T(8,128)(2,1)S(1)}, u32[]{:S(2)}, u32[]{:S(2)}) %collective-permute-start.15) | collective-permute-done | bytes 286752 | tf_op jit(solution)/shard_map/ppermute | solution.py:327
  125.7 0.6 combine.10
  126.2 1.6 collective-permute-start.23
  127.8 0.6 combine.11
  128.4 1.3 collective-permute-start.20
  129.8 1.8 %collective-permute-start.19 = (bf16[80,3584]{1,0:T(8,128)(2,1)S(1)}, bf16[80,3584]{1,0:T(8,128)(2,1)S(1)}, u32[]{:S(2)}, u32[]{:S(2)}) collective-permute-start(bf16[80,3584]{1,0:T(8,128)(2,1)S(1)} %get-tuple-element.114), channel_id=1, source_target_pairs={{0,1},{1,0},{2,3},{3,2},{4,5},{5,4},{6,7},{7,6},{8,9},{9,8},{10,11... | collective-permute-start | bytes 1720328 | tf_op jit(solution)/shard_map/ppermute | solution.py:327
  131.7 0.7 collective-permute-start.22
  132.4 6.3 %collective-permute-done.23 = bf16[128,1792]{1,0:T(8,128)(2,1)S(1)} collective-permute-done((bf16[128,1792]{1,0:T(8,128)(2,1)S(1)}, bf16[128,1792]{1,0:T(8,128)(2,1)S(1)}, u32[]{:S(2)}, u32[]{:S(2)}) %collective-permute-start.23) | collective-permute-done | bytes 458784 | tf_op jit(solution)/shard_map/ppermute | solution.py:327
  138.8 0.7 collective-permute-start.25
  139.6 1.3 collective-permute-start.28
  140.9 4.9 %collective-permute-done.20 = bf16[128,1792]{1,0:T(8,128)(2,1)S(1)} collective-permute-done((bf16[128,1792]{1,0:T(8,128)(2,1)S(1)}, bf16[128,1792]{1,0:T(8,128)(2,1)S(1)}, u32[]{:S(2)}, u32[]{:S(2)}) %collective-permute-start.20) | collective-permute-done | bytes 458784 | tf_op jit(solution)/shard_map/ppermute | solution.py:327
  146.1 1.3 collective-permute-start.26
  147.4 0.7 collective-permute-start.24
  148.1 8.1 %collective-permute-done.28.refs_2_ = bf16[128,1792]{1,0:T(8,128)(2,1)S(1)} collective-permute-done((bf16[128,1792]{1,0:T(8,128)(2,1)S(1)}, bf16[128,1792]{1,0:T(8,128)(2,1)S(1)}, u32[]{:S(2)}, u32[]{:S(2)}) %collective-permute-start.28) | collective-permute-done | bytes 458784 | tf_op jit(solution)/shard_map/ppermute | solution.py:327
  156.1 1.5 combine.12.refs_7_
  157.6 4.9 %collective-permute-done.26.refs_6_ = bf16[128,1792]{1,0:T(8,128)(2,1)S(1)} collective-permute-done((bf16[128,1792]{1,0:T(8,128)(2,1)S(1)}, bf16[128,1792]{1,0:T(8,128)(2,1)S(1)}, u32[]{:S(2)}, u32[]{:S(2)}) %collective-permute-start.26) | collective-permute-done | bytes 458784 | tf_op jit(solution)/shard_map/ppermute | solution.py:327
  162.5 1.5 combine.13
  (34 shorter events, 0.9 us)
Async XLA Ops:
  0.0 7.3 %collective-permute-start = (bf16[3584,512]{1,0:T(8,128)(2,1)}, bf16[3584,512]{1,0:T(8,128)(2,1)}, u32[]{:S(2)}, u32[]{:S(2)}) collective-permute-start(bf16[3584,512]{1,0:T(8,128)(2,1)} %bitcast.8), channel_id=1, source_target_pairs={{0,8},{8,0},{1,9},{9,1},{2,10},{10,2},{3,11},{11,3},{4,12},{12,4},... | collective-permute-start | bytes 11010056 | tf_op jit(solution)/shard_map/ppermute | solution.py:330
  0.5 34.1 %collective-permute-start.2 = (bf16[3584,512]{1,0:T(8,128)(2,1)}, bf16[3584,512]{1,0:T(8,128)(2,1)}, u32[]{:S(2)}, u32[]{:S(2)}) collective-permute-start(bf16[3584,512]{1,0:T(8,128)(2,1)} %bitcast.10), channel_id=1, source_target_pairs={{0,8},{8,0},{1,9},{9,1},{2,10},{10,2},{3,11},{11,3},{4,12},{12,4},... | collective-permute-start | bytes 11010056 | tf_op jit(solution)/shard_map/ppermute | solution.py:330
  0.5 34.1 %collective-permute-start.3 = (bf16[512,3584]{1,0:T(8,128)(2,1)}, bf16[512,3584]{1,0:T(8,128)(2,1)}, u32[]{:S(2)}, u32[]{:S(2)}) collective-permute-start(bf16[512,3584]{1,0:T(8,128)(2,1)} %bitcast.12), channel_id=1, source_target_pairs={{0,8},{8,0},{1,9},{9,1},{2,10},{10,2},{3,11},{11,3},{4,12},{12,4},... | collective-permute-start | bytes 11010056 | tf_op jit(solution)/shard_map/ppermute | solution.py:330
  1.0 1.2 copy-start.3
  2.2 0.7 copy-start.6
  2.9 0.7 copy-start.7
  4.6 24.4 %collective-permute-start.4 = (bf16[128,3712]{1,0:T(8,128)(2,1)S(1)}, bf16[128,3712]{1,0:T(8,128)(2,1)S(1)}, u32[]{:S(2)}, u32[]{:S(2)}) collective-permute-start(bf16[128,3712]{1,0:T(8,128)(2,1)S(1)} %get-tuple-element.65.refs_0_), channel_id=1, source_target_pairs={{0,2},{1,3},{2,0},{3,1},{4,6},{5,7},{6,4},{7,5},{8,10},{9,11},{10,... | collective-permute-start | bytes 2850824 | tf_op jit(solution)/shard_map/ppermute | solution.py:327
  7.3 21.7 %collective-permute-start.1 = (bf16[80,3584]{1,0:T(8,128)(2,1)S(1)}, bf16[80,3584]{1,0:T(8,128)(2,1)S(1)}, u32[]{:S(2)}, u32[]{:S(2)}) collective-permute-start(bf16[80,3584]{1,0:T(8,128)(2,1)S(1)} %get-tuple-element.67), channel_id=1, source_target_pairs={{0,1},{1,0},{2,3},{3,2},{4,5},{5,4},{6,7},{7,6},{8,9},{9,8},{10,11... | collective-permute-start | bytes 1720328 | tf_op jit(solution)/shard_map/ppermute | solution.py:327
  9.7 23.6 %collective-permute-start.5 = (bf16[128,3712]{1,0:T(8,128)(2,1)S(1)}, bf16[128,3712]{1,0:T(8,128)(2,1)S(1)}, u32[]{:S(2)}, u32[]{:S(2)}) collective-permute-start(bf16[128,3712]{1,0:T(8,128)(2,1)S(1)} %get-tuple-element.65.refs_0_), channel_id=1, source_target_pairs={{2,4},{3,5},{4,2},{5,3},{10,12},{11,13},{12,10},{13,11},{18,20},{1... | collective-permute-start | bytes 2850824 | tf_op jit(solution)/shard_map/ppermute | solution.py:327
  10.4 2.0 %copy-start = (bf16[1,3584,512]{2,1,0:T(8,128)(2,1)S(1)}, bf16[1,3584,512]{2,1,0:T(8,128)(2,1)}, u32[]{:S(2)}) copy-start(bf16[1,3584,512]{2,1,0:T(8,128)(2,1)} %param.9) | copy-start | bytes 11010052
  12.5 2.0 %copy-start.1 = (bf16[1,3584,512]{2,1,0:T(8,128)(2,1)S(1)}, bf16[1,3584,512]{2,1,0:T(8,128)(2,1)}, u32[]{:S(2)}) copy-start(bf16[1,3584,512]{2,1,0:T(8,128)(2,1)} %param.10) | copy-start | bytes 11010052
  14.5 2.0 %copy-start.2 = (bf16[1,512,3584]{2,1,0:T(8,128)(2,1)S(1)}, bf16[1,512,3584]{2,1,0:T(8,128)(2,1)}, u32[]{:S(2)}) copy-start(bf16[1,512,3584]{2,1,0:T(8,128)(2,1)} %param.11) | copy-start | bytes 11010052
  29.0 9.8 %copy-start.4 = (bf16[80,3584]{1,0:T(8,128)(2,1)}, bf16[80,3584]{1,0:T(8,128)(2,1)S(1)}, u32[]{:S(2)}) copy-start(bf16[80,3584]{1,0:T(8,128)(2,1)S(1)} %collective-permute-done.1.refs_1_) | copy-start | bytes 1720324
  29.0 23.1 %collective-permute-start.9 = (bf16[128,3712]{1,0:T(8,128)(2,1)S(1)}, bf16[128,3712]{1,0:T(8,128)(2,1)S(1)}, u32[]{:S(2)}, u32[]{:S(2)}) collective-permute-start(bf16[128,3712]{1,0:T(8,128)(2,1)S(1)} %collective-permute-done.4.refs_0_.refs_1_), channel_id=1, source_target_pairs={{2,4},{3,5},{4,2},{5,3},{10,12},{11,13},{12,10},{13,11},{18,20},{1... | collective-permute-start | bytes 2850824 | tf_op jit(solution)/shard_map/ppermute | solution.py:327
  31.5 14.9 %collective-permute-start.7 = (bf16[80,3584]{1,0:T(8,128)(2,1)S(1)}, bf16[80,3584]{1,0:T(8,128)(2,1)S(1)}, u32[]{:S(2)}, u32[]{:S(2)}) collective-permute-start(bf16[80,3584]{1,0:T(8,128)(2,1)S(1)} %get-tuple-element.73), channel_id=1, source_target_pairs={{0,1},{1,0},{2,3},{3,2},{4,5},{5,4},{6,7},{7,6},{8,9},{9,8},{10,11... | collective-permute-start | bytes 1720328 | tf_op jit(solution)/shard_map/ppermute | solution.py:327
  33.3 27.6 %collective-permute-start.6 = (bf16[128,3712]{1,0:T(8,128)(2,1)S(1)}, bf16[128,3712]{1,0:T(8,128)(2,1)S(1)}, u32[]{:S(2)}, u32[]{:S(2)}) collective-permute-start(bf16[128,3712]{1,0:T(8,128)(2,1)S(1)} %collective-permute-done.5.refs_1_.refs_3_), channel_id=1, source_target_pairs={{2,0},{3,1},{4,6},{5,7},{10,8},{11,9},{12,14},{13,15},{18,16},{19,... | collective-permute-start | bytes 2850824 | tf_op jit(solution)/shard_map/ppermute | solution.py:327
  38.9 1.1 copy-start.5
  52.1 27.6 %collective-permute-start.10 = (bf16[128,3712]{1,0:T(8,128)(2,1)S(1)}, bf16[128,3712]{1,0:T(8,128)(2,1)S(1)}, u32[]{:S(2)}, u32[]{:S(2)}) collective-permute-start(bf16[128,3712]{1,0:T(8,128)(2,1)S(1)} %collective-permute-done.9.refs_1_.refs_3_), channel_id=1, source_target_pairs={{2,0},{3,1},{4,6},{5,7},{10,8},{11,9},{12,14},{13,15},{18,16},{19,... | collective-permute-start | bytes 2850824 | tf_op jit(solution)/shard_map/ppermute | solution.py:327
  53.4 16.0 %collective-permute-start.11 = (bf16[80,3584]{1,0:T(8,128)(2,1)S(1)}, bf16[80,3584]{1,0:T(8,128)(2,1)S(1)}, u32[]{:S(2)}, u32[]{:S(2)}) collective-permute-start(bf16[80,3584]{1,0:T(8,128)(2,1)S(1)} %get-tuple-element.93), channel_id=1, source_target_pairs={{0,1},{1,0},{2,3},{3,2},{4,5},{5,4},{6,7},{7,6},{8,9},{9,8},{10,11... | collective-permute-start | bytes 1720328 | tf_op jit(solution)/shard_map/ppermute | solution.py:327
  62.9 16.8 %collective-permute-start.8 = (bf16[80,3584]{1,0:T(8,128)(2,1)S(1)}, bf16[80,3584]{1,0:T(8,128)(2,1)S(1)}, u32[]{:S(2)}, u32[]{:S(2)}) collective-permute-start(bf16[80,3584]{1,0:T(8,128)(2,1)S(1)} %get-tuple-element.89), channel_id=1, source_target_pairs={{0,1},{1,0},{2,3},{3,2},{4,5},{5,4},{6,7},{7,6},{8,9},{9,8},{10,11... | collective-permute-start | bytes 1720328 | tf_op jit(solution)/shard_map/ppermute | solution.py:327
  70.5 25.5 %collective-permute-start.14 = (bf16[128,3584]{1,0:T(8,128)(2,1)S(1)}, bf16[128,3584]{1,0:T(8,128)(2,1)S(1)}, u32[]{:S(2)}, u32[]{:S(2)}) collective-permute-start(bf16[128,3584]{1,0:T(8,128)(2,1)S(1)} %combine.7), channel_id=1, source_target_pairs={{0,2},{1,3},{6,4},{7,5},{8,10},{9,11},{14,12},{15,13},{16,18},{17,... | collective-permute-start | bytes 2752520 | tf_op jit(solution)/shard_map/ppermute | solution.py:327
  81.7 13.4 %collective-permute-start.12 = (bf16[80,3584]{1,0:T(8,128)(2,1)S(1)}, bf16[80,3584]{1,0:T(8,128)(2,1)S(1)}, u32[]{:S(2)}, u32[]{:S(2)}) collective-permute-start(bf16[80,3584]{1,0:T(8,128)(2,1)S(1)} %get-tuple-element.96), channel_id=1, source_target_pairs={{0,1},{1,0},{2,3},{3,2},{4,5},{5,4},{6,7},{7,6},{8,9},{9,8},{10,11... | collective-permute-start | bytes 1720328 | tf_op jit(solution)/shard_map/ppermute | solution.py:327
  95.1 6.6 %collective-permute-start.16 = (bf16[80,1792]{1,0:T(8,128)(2,1)S(1)}, bf16[80,1792]{1,0:T(8,128)(2,1)S(1)}, u32[]{:S(2)}, u32[]{:S(2)}) collective-permute-start(bf16[80,1792]{1,0:T(8,128)(2,1)S(1)} %get-tuple-element.107), channel_id=1, source_target_pairs={{0,1},{1,0},{2,3},{3,2},{4,5},{5,4},{6,7},{7,6},{8,9},{9,8},{10,11... | collective-permute-start | bytes 860168 | tf_op jit(solution)/shard_map/ppermute | solution.py:327
  102.4 17.8 %collective-permute-start.17 = (bf16[128,1792]{1,0:T(8,128)(2,1)S(1)}, bf16[128,1792]{1,0:T(8,128)(2,1)S(1)}, u32[]{:S(2)}, u32[]{:S(2)}) collective-permute-start(bf16[128,1792]{1,0:T(8,128)(2,1)S(1)} %combine.8), channel_id=1, source_target_pairs={{0,2},{1,3},{6,4},{7,5},{8,10},{9,11},{14,12},{15,13},{16,18},{17,... | collective-permute-start | bytes 1376264 | tf_op jit(solution)/shard_map/ppermute | solution.py:327
  108.5 9.8 %collective-permute-start.18 = (bf16[80,1792]{1,0:T(8,128)(2,1)S(1)}, bf16[80,1792]{1,0:T(8,128)(2,1)S(1)}, u32[]{:S(2)}, u32[]{:S(2)}) collective-permute-start(bf16[80,1792]{1,0:T(8,128)(2,1)S(1)} %get-tuple-element.109), channel_id=1, source_target_pairs={{0,1},{1,0},{2,3},{3,2},{4,5},{5,4},{6,7},{7,6},{8,9},{9,8},{10,11... | collective-permute-start | bytes 860168 | tf_op jit(solution)/shard_map/ppermute | solution.py:327
  109.7 18.1 %collective-permute-start.13 = (bf16[80,1792]{1,0:T(8,128)(2,1)S(1)}, bf16[80,1792]{1,0:T(8,128)(2,1)S(1)}, u32[]{:S(2)}, u32[]{:S(2)}) collective-permute-start(bf16[80,1792]{1,0:T(8,128)(2,1)S(1)} %get-tuple-element.100), channel_id=1, source_target_pairs={{0,1},{1,0},{2,3},{3,2},{4,5},{5,4},{6,7},{7,6},{8,9},{9,8},{10,11... | collective-permute-start | bytes 860168 | tf_op jit(solution)/shard_map/ppermute | solution.py:327
  110.6 15.1 %collective-permute-start.15 = (bf16[80,1792]{1,0:T(8,128)(2,1)S(1)}, bf16[80,1792]{1,0:T(8,128)(2,1)S(1)}, u32[]{:S(2)}, u32[]{:S(2)}) collective-permute-start(bf16[80,1792]{1,0:T(8,128)(2,1)S(1)} %get-tuple-element.105), channel_id=1, source_target_pairs={{0,1},{1,0},{2,3},{3,2},{4,5},{5,4},{6,7},{7,6},{8,9},{9,8},{10,11... | collective-permute-start | bytes 860168 | tf_op jit(solution)/shard_map/ppermute | solution.py:327
  118.9 12.7 %collective-permute-start.21 = (bf16[128,1792]{1,0:T(8,128)(2,1)S(1)}, bf16[128,1792]{1,0:T(8,128)(2,1)S(1)}, u32[]{:S(2)}, u32[]{:S(2)}) collective-permute-start(bf16[128,1792]{1,0:T(8,128)(2,1)S(1)} %combine.9), channel_id=1, source_target_pairs={{0,2},{1,3},{6,4},{7,5},{8,10},{9,11},{14,12},{15,13},{16,18},{17,... | collective-permute-start | bytes 1376264 | tf_op jit(solution)/shard_map/ppermute | solution.py:327
  120.3 27.7 %collective-permute-start.27 = (bf16[128,1792]{1,0:T(8,128)(2,1)S(1)}, bf16[128,1792]{1,0:T(8,128)(2,1)S(1)}, u32[]{:S(2)}, u32[]{:S(2)}) collective-permute-start(bf16[128,1792]{1,0:T(8,128)(2,1)S(1)} %add_convert_fusion.5), channel_id=1, source_target_pairs={{2,4},{3,5},{4,2},{5,3},{10,12},{11,13},{12,10},{13,11},{18,20},{1... | collective-permute-start | bytes 1376264 | tf_op jit(solution)/shard_map/ppermute | solution.py:327
  126.2 12.5 %collective-permute-start.23 = (bf16[128,1792]{1,0:T(8,128)(2,1)S(1)}, bf16[128,1792]{1,0:T(8,128)(2,1)S(1)}, u32[]{:S(2)}, u32[]{:S(2)}) collective-permute-start(bf16[128,1792]{1,0:T(8,128)(2,1)S(1)} %combine.10), channel_id=1, source_target_pairs={{0,2},{1,3},{6,4},{7,5},{8,10},{9,11},{14,12},{15,13},{16,18},{17,... | collective-permute-start | bytes 1376264 | tf_op jit(solution)/shard_map/ppermute | solution.py:327
  128.4 17.4 %collective-permute-start.20 = (bf16[128,1792]{1,0:T(8,128)(2,1)S(1)}, bf16[128,1792]{1,0:T(8,128)(2,1)S(1)}, u32[]{:S(2)}, u32[]{:S(2)}) collective-permute-start(bf16[128,1792]{1,0:T(8,128)(2,1)S(1)} %combine.11), channel_id=1, source_target_pairs={{0,2},{1,3},{6,4},{7,5},{8,10},{9,11},{14,12},{15,13},{16,18},{17,... | collective-permute-start | bytes 1376264 | tf_op jit(solution)/shard_map/ppermute | solution.py:327
  129.8 18.3 %collective-permute-start.19 = (bf16[80,3584]{1,0:T(8,128)(2,1)S(1)}, bf16[80,3584]{1,0:T(8,128)(2,1)S(1)}, u32[]{:S(2)}, u32[]{:S(2)}) collective-permute-start(bf16[80,3584]{1,0:T(8,128)(2,1)S(1)} %get-tuple-element.114), channel_id=1, source_target_pairs={{0,1},{1,0},{2,3},{3,2},{4,5},{5,4},{6,7},{7,6},{8,9},{9,8},{10,11... | collective-permute-start | bytes 1720328 | tf_op jit(solution)/shard_map/ppermute | solution.py:327
  131.7 7.8 %collective-permute-start.22 = (bf16[128,1792]{1,0:T(8,128)(2,1)S(1)}, bf16[128,1792]{1,0:T(8,128)(2,1)S(1)}, u32[]{:S(2)}, u32[]{:S(2)}) collective-permute-start(bf16[128,1792]{1,0:T(8,128)(2,1)S(1)} %add_convert_fusion.4), channel_id=1, source_target_pairs={{2,4},{3,5},{4,2},{5,3},{10,12},{11,13},{12,10},{13,11},{18,20},{1... | collective-permute-start | bytes 1376264 | tf_op jit(solution)/shard_map/ppermute | solution.py:327
  138.8 7.1 %collective-permute-start.25 = (bf16[128,1792]{1,0:T(8,128)(2,1)S(1)}, bf16[128,1792]{1,0:T(8,128)(2,1)S(1)}, u32[]{:S(2)}, u32[]{:S(2)}) collective-permute-start(bf16[128,1792]{1,0:T(8,128)(2,1)S(1)} %add_convert_fusion.3), channel_id=1, source_target_pairs={{2,4},{3,5},{4,2},{5,3},{10,12},{11,13},{12,10},{13,11},{18,20},{1... | collective-permute-start | bytes 1376264 | tf_op jit(solution)/shard_map/ppermute | solution.py:327
  139.6 16.5 %collective-permute-start.28 = (bf16[128,1792]{1,0:T(8,128)(2,1)S(1)}, bf16[128,1792]{1,0:T(8,128)(2,1)S(1)}, u32[]{:S(2)}, u32[]{:S(2)}) collective-permute-start(bf16[128,1792]{1,0:T(8,128)(2,1)S(1)} %add_convert_fusion.2), channel_id=1, source_target_pairs={{2,0},{3,1},{4,6},{5,7},{10,8},{11,9},{12,14},{13,15},{18,16},{19,... | collective-permute-start | bytes 1376264 | tf_op jit(solution)/shard_map/ppermute | solution.py:327
  146.1 16.4 %collective-permute-start.26 = (bf16[128,1792]{1,0:T(8,128)(2,1)S(1)}, bf16[128,1792]{1,0:T(8,128)(2,1)S(1)}, u32[]{:S(2)}, u32[]{:S(2)}) collective-permute-start(bf16[128,1792]{1,0:T(8,128)(2,1)S(1)} %add_convert_fusion), channel_id=1, source_target_pairs={{2,0},{3,1},{4,6},{5,7},{10,8},{11,9},{12,14},{13,15},{18,16},{19,... | collective-permute-start | bytes 1376264 | tf_op jit(solution)/shard_map/ppermute | solution.py:327
  147.4 15.1 %collective-permute-start.24 = (bf16[128,1792]{1,0:T(8,128)(2,1)S(1)}, bf16[128,1792]{1,0:T(8,128)(2,1)S(1)}, u32[]{:S(2)}, u32[]{:S(2)}) collective-permute-start(bf16[128,1792]{1,0:T(8,128)(2,1)S(1)} %add_convert_fusion.1), channel_id=1, source_target_pairs={{2,4},{3,5},{4,2},{5,3},{10,12},{11,13},{12,10},{13,11},{18,20},{1... | collective-permute-start | bytes 1376264 | tf_op jit(solution)/shard_map/ppermute | solution.py:327
